TPU v7x, 256 devices: a whole 4x4x8 slice. The times are simulated.
256 devices in a mesh: row: 8 (over z), col: 4 (over y_lo, core), ch: 8 (over x, y_hi).
Axes of the slice: x: 4, y: 4 (y_hi: 2, y_lo: 2; y = y_hi * 2 + y_lo), z: 8, core: 2. Of those that a mesh axis runs over, the one named last changes fastest.
Arguments:
- spectra: float32 [384, 256, 1024], P('ch', 'row', 'col'), may hold values from 0 to 1
- pixel_factor: float32 [64, 256, 1024], P(None, 'row', 'col'), may hold values from 0.1 to 1
- channel_factor: float32 [64, 384], P(None, 'ch'), may hold values from 0.1 to 1
- labels: int32 [256, 1024], P('row', 'col'), may hold values from 0 to 3
Outputs:
- smoothed_factor: float32 [64, 256, 1024], P(None, 'row', 'col')
- new_channel: float32 [64, 384], P(None, 'ch')
All inputs are finite; a program needn't handle non-finite values.
Results may differ from a plain program's by a relative error of at most 0.000068.
Values sent between devices are 32-bit elements; how exact they have to be, the bound alone decides.
No kernel may reach another device: no remote copies, remote signals or barrier semaphores. Data moves between devices by JAX's collectives and lax.ppermute only.
A program may use at most 64 MiB of HBM per device.

v0:
```python
import jax
import jax.numpy as jnp
from jax import lax
from jax.sharding import PartitionSpec as P

SMOOTH = 3


epsilon = 1e-09


def padded_2(block, sides, width):
    for axis, dim in sides:
        count = lax.axis_size(axis)
        forward = [(i, i + 1) for i in range(count - 1)]
        backward = [(target, source) for source, target in forward]
        low = lax.ppermute(
            lax.slice_in_dim(block, block.shape[dim] - width, None, axis=dim), axis, forward
        )
        high = lax.ppermute(lax.slice_in_dim(block, 0, width, axis=dim), axis, backward)
        block = jnp.concatenate([low, block, high], axis=dim)
    return block


def coefficients(marked):
    center = marked[1:-1, 1:-1]
    result = []
    for neighbour in (marked[:-2, 1:-1], marked[2:, 1:-1], marked[1:-1, :-2], marked[1:-1, 2:]):
        result.append(
            jnp.where(neighbour == 0, 0.0, jnp.where(neighbour == center, 1.0, 0.25)).astype(
                jnp.float32
            )
        )
    return result


def smooth_once(padded, field, weights):
    combined = field + weights[0] * padded[:, :-2, 1:-1] + weights[1] * padded[:, 2:, 1:-1]
    combined = combined + weights[2] * padded[:, 1:-1, :-2] + weights[3] * padded[:, 1:-1, 2:]
    return combined / (1.0 + weights[0] + weights[1] + weights[2] + weights[3])


def lift_factor(own_factor, pixel_top, chan_gram):
    factor_rank = own_factor.shape[0]
    flat_own = own_factor.reshape(factor_rank, -1)
    lower = jnp.dot(
        chan_gram, flat_own, precision=lax.Precision.HIGHEST, preferred_element_type=jnp.float32
    )
    return (flat_own * pixel_top.reshape(factor_rank, -1) / (lower + epsilon)).reshape(
        own_factor.shape
    )


def shards(spectra, pixel_factor, channel_factor, labels):
    precise = lax.Precision.HIGHEST
    contraction = (((1,), (1,)), ((), ()))
    factor_rank, row_count, col_count = pixel_factor.shape
    flat_pixel = pixel_factor.reshape(factor_rank, row_count * col_count)
    flat_data = spectra.reshape(spectra.shape[0], row_count * col_count)
    chan_top = lax.dot_general(
        flat_pixel, flat_data, contraction, precision=precise, preferred_element_type=jnp.float32
    )
    pixel_gram = lax.dot_general(
        flat_pixel, flat_pixel, contraction, precision=precise, preferred_element_type=jnp.float32
    )
    chan_top, pixel_gram = lax.psum((chan_top, pixel_gram), ("row", "col"))
    new_channel = (
        channel_factor
        * chan_top
        / (
            jnp.dot(
                pixel_gram, channel_factor, precision=precise, preferred_element_type=jnp.float32
            )
            + epsilon
        )
    )
    part_top = jnp.dot(
        new_channel, flat_data, precision=precise, preferred_element_type=jnp.float32
    ).reshape(factor_rank, row_count, col_count)
    part_gram = lax.dot_general(
        new_channel, new_channel, contraction, precision=precise, preferred_element_type=jnp.float32
    )
    marked = labels + 1
    pixel_top, chan_gram = lax.psum((part_top, part_gram), "ch")
    field = lift_factor(pixel_factor, pixel_top, chan_gram)
    border_marks = padded_2(marked, (("row", 0), ("col", 1)), 1)
    weights = coefficients(border_marks)
    for iteration in range(SMOOTH):
        padded = padded_2(field, (("row", 1), ("col", 2)), 1)
        field = smooth_once(padded, field, weights)
    return (field, new_channel)


def solution(mesh):
    placed = (P("ch", "row", "col"), P(None, "row", "col"), P(None, "ch"), P("row", "col"))
    return jax.shard_map(
        shards,
        mesh=mesh,
        in_specs=placed,
        out_specs=(P(None, "row", "col"), P(None, "ch")),
        check_vma=False,
    )
```

profile of v0, /device:TPU:64, one launch (start us, length us, event | category | flops | bytes accessed | tf_op | source)
XLA Modules:
  0.0 351.7 jit_solution(6095279103476768087)
XLA Ops:
  7.2 6.3 %fusion.35 = f32[64,64]{1,0:T(8,128)S(1)} fusion(f32[64,32,256]{2,1,0:T(8,128)} %param.5), kind=kOutput, calls=%fused_computation.61 | convolution fusion | flops 402653184 | bytes 2113536 | tf_op jit(solution)/shard_map/dot_general | solution.py:63
  13.5 5.7 %fusion.38 = f32[64,48]{0,1:T(8,128)S(1)} fusion(f32[48,32,256]{2,1,0:T(8,128)} %param.4, f32[64,32,256]{2,1,0:T(8,128)} %param.5), kind=kOutput, calls=%fused_computation.62 | convolution fusion | flops 301989888 | bytes 3682304 | tf_op jit(solution)/shard_map/dot_general | solution.py:60
  19.2 96.4 %all-reduce = (f32[64,64]{1,0:T(8,128)S(1)}, f32[64,48]{0,1:T(8,128)S(1)}) all-reduce(f32[64,64]{1,0:T(8,128)S(1)} %fusion.35, f32[64,48]{0,1:T(8,128)S(1)} %fusion.38), channel_id=1, replica_groups=mesh['row'=8,'col'=4,'ch'=8] {'row','col'}, use_global_device_ids=true, to_apply=%region_1.0 | all-reduce | flops 7168 | bytes 57344 | tf_op jit(solution)/shard_map/psum | solution.py:66
  115.8 4.2 %convolution_bitcast_fusion = f32[32,8,8,256]{3,2,1,0:T(8,128)S(1)} fusion(f32[64,48]{0,1:T(8,128)S(1)} %fusion.43, f32[6,8,32,256]{3,2,1,0:T(8,128)} %bitcast.35), kind=kOutput, calls=%fused_computation.57 | convolution fusion | flops 301989888 | bytes 3682304 | tf_op jit(solution)/shard_map/dot_general | solution.py:77
  121.6 9.2 %collective-permute-start.2 = (s32[1,256]{1,0:T(1,128)S(1)}, s32[1,256]{1,0:T(1,128)S(1)}, u32[]{:S(2)}, u32[]{:S(2)}) collective-permute-start(s32[1,256]{1,0:T(1,128)S(1)} %get-tuple-element.31), channel_id=1, source_target_pairs={{32,0},{64,32},{96,64},{128,96},{160,128},{192,160},{224,192},{33,... | collective-permute-start | bytes 3080 | tf_op jit(solution)/shard_map/ppermute | solution.py:20
  132.9 42.2 %psum.31 = f32[64,64]{1,0:T(8,128)S(1)} all-reduce(f32[64,64]{1,0:T(8,128)S(1)} %fusion.54), channel_id=1, replica_groups=mesh['row'=8,'col'=4,'ch'=8] {'ch'}, use_global_device_ids=true, to_apply=%region_3.0 | all-reduce | flops 4096 | bytes 32768 | tf_op jit(solution)/shard_map/psum | solution.py:84
  175.2 2.5 copy.137
  177.7 70.2 %all-reduce.3.cloned.1.call-done = f32[64,8192]{1,0:T(8,128)} async-done(((f32[64,8192]{1,0:T(8,128)}), f32[64,8192]{1,0:T(8,128)}) %all-reduce.3.cloned.1.call-update) | async-done | bytes 2097168 | tf_op jit(solution)/shard_map/psum | solution.py:84
  247.9 5.1 %fusion = f32[64,8192]{1,0:T(8,128)S(1)} fusion(f32[64,64]{1,0:T(8,128)S(1)} %psum.31, f32[64,8192]{1,0:T(8,128)} %bitcast.36, f32[64,8192]{1,0:T(8,128)} %all-reduce.3.cloned.1.call-done), kind=kOutput, calls=%fused_computation.1 | convolution fusion | flops 404226048 | bytes 6307840 | tf_op jit(solution)/shard_map/dot_general | solution.py:46
  253.8 2.4 collective-permute-start.3
  256.2 3.5 collective-permute-start.1
  261.0 3.0 collective-permute-start.4
  264.0 4.5 %copy.109 = f32[64,32,256]{0,1,2:T(8,128)} copy(f32[64,32,256]{2,1,0:T(8,128)S(1)} %bitcast.33) | data formatting | bytes 4194304 | tf_op jit(solution)/shard_map/reshape | solution.py:49
  269.5 2.5 collective-permute-start.5
  275.1 10.6 %fusion.21 = f32[64,32,256]{0,1,2:T(8,128)S(1)} fusion(f32[64,34,1]{0,1,2:T(8,128)S(1)} %collective-permute-done.7, f32[64,1,256]{0,1,2:T(1,128)S(1)} %copy.113, f32[64,32,256]{0,1,2:T(8,128)} %copy.109, f32[64,1,256]{0,1,2:T(1,128)S(1)} %copy.107, f32[64,34,1]{0,1,2:T(8,128)S(1)} %collective-permute-done.5, f32[32,256]{0,1:T(8,128)S(1)} %copy.119, ...), kind=kLoop, calls=%fused_computation.39 | loop fusion | flops 8912896 | bytes 4506624 | tf_op jit(solution)/shard_map/div | solution.py:40
  287.9 2.4 collective-permute-start.9
  290.4 4.2 %collective-permute-start.8 = (f32[64,1,256]{2,0,1:T(8,128)S(1)}, f32[64,1,256]{2,0,1:T(8,128)S(1)}, u32[]{:S(2)}, u32[]{:S(2)}) collective-permute-start(f32[64,1,256]{2,0,1:T(8,128)S(1)} %copy.120), channel_id=1, source_target_pairs={{0,32},{32,64},{64,96},{96,128},{128,160},{160,192},{192,224},{1,3... | collective-permute-start | bytes 196616 | tf_op jit(solution)/shard_map/ppermute | solution.py:17
  297.6 3.6 %collective-permute-start.10 = (f32[64,34,1]{0,1,2:T(8,128)S(1)}, f32[64,34,1]{0,1,2:T(8,128)S(1)}, u32[]{:S(2)}, u32[]{:S(2)}) collective-permute-start(f32[64,34,1]{0,1,2:T(8,128)S(1)} %get-tuple-element.19), channel_id=1, source_target_pairs={{0,8},{8,16},{16,24},{1,9},{9,17},{17,25},{2,10},{10,18},{18,26},{... | collective-permute-start | bytes 26120 | tf_op jit(solution)/shard_map/ppermute | solution.py:17
  304.7 7.4 %fusion.12 = f32[64,32,256]{0,1,2:T(8,128)S(1)} fusion(f32[64,34,1]{0,1,2:T(8,128)S(1)} %collective-permute-done.11, f32[64,1,256]{0,1,2:T(1,128)S(1)} %copy.123, f32[64,32,256]{0,1,2:T(8,128)S(1)} %copy-done.3, f32[64,1,256]{0,1,2:T(1,128)S(1)} %copy.121, f32[64,34,1]{0,1,2:T(8,128)S(1)} %collective-permute-done.10, f32[32,256]{0,1:T(8,128)S(1)} %copy.119, ...), kind=kLoop, calls=%fused_computation.22 | loop fusion | flops 8912896 | bytes 4506624 | tf_op jit(solution)/shard_map/div | solution.py:40
  314.4 2.4 collective-permute-start.13
  316.8 4.6 %collective-permute-start.12 = (f32[64,1,256]{2,0,1:T(8,128)S(1)}, f32[64,1,256]{2,0,1:T(8,128)S(1)}, u32[]{:S(2)}, u32[]{:S(2)}) collective-permute-start(f32[64,1,256]{2,0,1:T(8,128)S(1)} %copy.126), channel_id=1, source_target_pairs={{0,32},{32,64},{64,96},{96,128},{128,160},{160,192},{192,224},{1,3... | collective-permute-start | bytes 196616 | tf_op jit(solution)/shard_map/ppermute | solution.py:17
  324.3 3.7 %collective-permute-start.14 = (f32[64,34,1]{0,1,2:T(8,128)S(1)}, f32[64,34,1]{0,1,2:T(8,128)S(1)}, u32[]{:S(2)}, u32[]{:S(2)}) collective-permute-start(f32[64,34,1]{0,1,2:T(8,128)S(1)} %get-tuple-element.17), channel_id=1, source_target_pairs={{0,8},{8,16},{16,24},{1,9},{9,17},{17,25},{2,10},{10,18},{18,26},{... | collective-permute-start | bytes 26120 | tf_op jit(solution)/shard_map/ppermute | solution.py:17
  331.5 8.2 %fusion.3 = f32[64,32,256]{0,1,2:T(8,128)} fusion(f32[64,34,1]{0,1,2:T(8,128)S(1)} %collective-permute-done.15, f32[64,1,256]{0,1,2:T(1,128)S(1)} %copy.129, f32[64,32,256]{0,1,2:T(8,128)S(1)} %copy-done.1, f32[64,1,256]{0,1,2:T(1,128)S(1)} %copy.127, f32[64,34,1]{0,1,2:T(8,128)S(1)} %collective-permute-done.14, f32[32,256]{0,1:T(8,128)S(1)} %copy.119, ...), kind=kLoop, calls=%fused_computation.5 | loop fusion | flops 8912896 | bytes 4506624 | tf_op jit(solution)/shard_map/div | solution.py:40
  339.7 5.1 %copy.132 = f32[64,32,256]{2,1,0:T(8,128)} copy(f32[64,32,256]{0,1,2:T(8,128)} %fusion.3) | data formatting | bytes 4194304
  (71 shorter events, 27.3 us)
Async XLA Ops:
  7.2 108.4 %copy-start.7 = (f32[64,48]{0,1:T(8,128)S(1)}, f32[64,48]{0,1:T(8,128)}, u32[]{:S(2)}) copy-start(f32[64,48]{0,1:T(8,128)} %param.6) | copy-start | bytes 36868
  7.2 240.7 %all-reduce.3.cloned.1.call-start = ((), (), s32[]{:S(2)}) async-start(), calls=%async_computation | async-start | bytes 4194304 | tf_op jit(solution)/shard_map/psum | solution.py:84
  115.7 16.9 %copy-start.5 = (f32[64,48]{0,1:T(8,128)}, f32[64,48]{0,1:T(8,128)S(1)}, u32[]{:S(2)}) copy-start(f32[64,48]{0,1:T(8,128)S(1)} %fusion.43) | copy-start | bytes 36868
  115.8 5.8 %copy-start.6 = (s32[32,256]{1,0:T(8,128)S(1)}, s32[32,256]{1,0:T(8,128)}, u32[]{:S(2)}) copy-start(s32[32,256]{1,0:T(8,128)} %param.7) | copy-start | bytes 98308
  115.8 59.4 %copy-start.4 = (f32[64,32,256]{2,1,0:T(8,128)S(1)}, f32[64,32,256]{2,1,0:T(8,128)}, u32[]{:S(2)}) copy-start(f32[64,32,256]{2,1,0:T(8,128)} %param.5) | copy-start | bytes 6291460
  121.6 56.1 %collective-permute-start.2 = (s32[1,256]{1,0:T(1,128)S(1)}, s32[1,256]{1,0:T(1,128)S(1)}, u32[]{:S(2)}, u32[]{:S(2)}) collective-permute-start(s32[1,256]{1,0:T(1,128)S(1)} %get-tuple-element.31), channel_id=1, source_target_pairs={{32,0},{64,32},{96,64},{128,96},{160,128},{192,160},{224,192},{33,... | collective-permute-start | bytes 3080 | tf_op jit(solution)/shard_map/ppermute | solution.py:20
  130.8 46.9 %collective-permute-start = (s32[1,256]{1,0:T(1,128)S(1)}, s32[1,256]{1,0:T(1,128)S(1)}, u32[]{:S(2)}, u32[]{:S(2)}) collective-permute-start(s32[1,256]{1,0:T(1,128)S(1)} %get-tuple-element.32), channel_id=1, source_target_pairs={{0,32},{32,64},{64,96},{96,128},{128,160},{160,192},{192,224},{1,3... | collective-permute-start | bytes 3080 | tf_op jit(solution)/shard_map/ppermute | solution.py:17
  253.8 14.8 %collective-permute-start.3 = (f32[64,1,256]{2,0,1:T(8,128)S(1)}, f32[64,1,256]{2,0,1:T(8,128)S(1)}, u32[]{:S(2)}, u32[]{:S(2)}) collective-permute-start(f32[64,1,256]{2,0,1:T(8,128)S(1)} %copy.134), channel_id=1, source_target_pairs={{32,0},{64,32},{96,64},{128,96},{160,128},{192,160},{224,192},{33,... | collective-permute-start | bytes 196616 | tf_op jit(solution)/shard_map/ppermute | solution.py:20
  256.2 12.5 %collective-permute-start.1 = (f32[64,1,256]{2,0,1:T(8,128)S(1)}, f32[64,1,256]{2,0,1:T(8,128)S(1)}, u32[]{:S(2)}, u32[]{:S(2)}) collective-permute-start(f32[64,1,256]{2,0,1:T(8,128)S(1)} %copy.133), channel_id=1, source_target_pairs={{0,32},{32,64},{64,96},{96,128},{128,160},{160,192},{192,224},{1,3... | collective-permute-start | bytes 196616 | tf_op jit(solution)/shard_map/ppermute | solution.py:17
  259.7 13.6 %collective-permute-start.6 = (s32[34,1]{1,0:T(8,128)S(1)}, s32[34,1]{1,0:T(8,128)S(1)}, u32[]{:S(2)}, u32[]{:S(2)}) collective-permute-start(s32[34,1]{1,0:T(8,128)S(1)} %get-tuple-element.29), channel_id=1, source_target_pairs={{8,0},{16,8},{24,16},{9,1},{17,9},{25,17},{10,2},{18,10},{26,18},{... | collective-permute-start | bytes 416 | tf_op jit(solution)/shard_map/ppermute | solution.py:20
  261.0 12.3 %collective-permute-start.4 = (s32[34,1]{1,0:T(8,128)S(1)}, s32[34,1]{1,0:T(8,128)S(1)}, u32[]{:S(2)}, u32[]{:S(2)}) collective-permute-start(s32[34,1]{1,0:T(8,128)S(1)} %get-tuple-element.30), channel_id=1, source_target_pairs={{0,8},{8,16},{16,24},{1,9},{9,17},{17,25},{2,10},{10,18},{18,26},{... | collective-permute-start | bytes 416 | tf_op jit(solution)/shard_map/ppermute | solution.py:17
  269.5 4.4 %collective-permute-start.5 = (f32[64,34,1]{0,1,2:T(8,128)S(1)}, f32[64,34,1]{0,1,2:T(8,128)S(1)}, u32[]{:S(2)}, u32[]{:S(2)}) collective-permute-start(f32[64,34,1]{0,1,2:T(8,128)S(1)} %get-tuple-element.21), channel_id=1, source_target_pairs={{0,8},{8,16},{16,24},{1,9},{9,17},{17,25},{2,10},{10,18},{18,26},{... | collective-permute-start | bytes 26120 | tf_op jit(solution)/shard_map/ppermute | solution.py:17
  272.0 3.1 collective-permute-start.7
  285.7 1.9 copy-start.2
  287.9 6.9 %collective-permute-start.9 = (f32[64,1,256]{2,0,1:T(8,128)S(1)}, f32[64,1,256]{2,0,1:T(8,128)S(1)}, u32[]{:S(2)}, u32[]{:S(2)}) collective-permute-start(f32[64,1,256]{2,0,1:T(8,128)S(1)} %copy.122), channel_id=1, source_target_pairs={{32,0},{64,32},{96,64},{128,96},{160,128},{192,160},{224,192},{33,... | collective-permute-start | bytes 196616 | tf_op jit(solution)/shard_map/ppermute | solution.py:20
  290.4 6.2 %collective-permute-start.8 = (f32[64,1,256]{2,0,1:T(8,128)S(1)}, f32[64,1,256]{2,0,1:T(8,128)S(1)}, u32[]{:S(2)}, u32[]{:S(2)}) collective-permute-start(f32[64,1,256]{2,0,1:T(8,128)S(1)} %copy.120), channel_id=1, source_target_pairs={{0,32},{32,64},{64,96},{96,128},{128,160},{160,192},{192,224},{1,3... | collective-permute-start | bytes 196616 | tf_op jit(solution)/shard_map/ppermute | solution.py:17
  296.7 8.1 %copy-start.3 = (f32[64,32,256]{0,1,2:T(8,128)S(1)}, f32[64,32,256]{0,1,2:T(8,128)}, u32[]{:S(2)}) copy-start(f32[64,32,256]{0,1,2:T(8,128)} %copy-done.2) | copy-start | bytes 6291460
  297.6 5.0 %collective-permute-start.10 = (f32[64,34,1]{0,1,2:T(8,128)S(1)}, f32[64,34,1]{0,1,2:T(8,128)S(1)}, u32[]{:S(2)}, u32[]{:S(2)}) collective-permute-start(f32[64,34,1]{0,1,2:T(8,128)S(1)} %get-tuple-element.19), channel_id=1, source_target_pairs={{0,8},{8,16},{16,24},{1,9},{9,17},{17,25},{2,10},{10,18},{18,26},{... | collective-permute-start | bytes 26120 | tf_op jit(solution)/shard_map/ppermute | solution.py:17
  301.2 3.5 collective-permute-start.11
  314.4 7.3 %collective-permute-start.13 = (f32[64,1,256]{2,0,1:T(8,128)S(1)}, f32[64,1,256]{2,0,1:T(8,128)S(1)}, u32[]{:S(2)}, u32[]{:S(2)}) collective-permute-start(f32[64,1,256]{2,0,1:T(8,128)S(1)} %copy.128), channel_id=1, source_target_pairs={{32,0},{64,32},{96,64},{128,96},{160,128},{192,160},{224,192},{33,... | collective-permute-start | bytes 196616 | tf_op jit(solution)/shard_map/ppermute | solution.py:20
  316.8 6.5 %collective-permute-start.12 = (f32[64,1,256]{2,0,1:T(8,128)S(1)}, f32[64,1,256]{2,0,1:T(8,128)S(1)}, u32[]{:S(2)}, u32[]{:S(2)}) collective-permute-start(f32[64,1,256]{2,0,1:T(8,128)S(1)} %copy.126), channel_id=1, source_target_pairs={{0,32},{32,64},{64,96},{96,128},{128,160},{160,192},{192,224},{1,3... | collective-permute-start | bytes 196616 | tf_op jit(solution)/shard_map/ppermute | solution.py:17
  323.4 8.1 %copy-start.1 = (f32[64,32,256]{0,1,2:T(8,128)S(1)}, f32[64,32,256]{0,1,2:T(8,128)}, u32[]{:S(2)}) copy-start(f32[64,32,256]{0,1,2:T(8,128)} %copy-done) | copy-start | bytes 6291460
  324.3 5.0 %collective-permute-start.14 = (f32[64,34,1]{0,1,2:T(8,128)S(1)}, f32[64,34,1]{0,1,2:T(8,128)S(1)}, u32[]{:S(2)}, u32[]{:S(2)}) collective-permute-start(f32[64,34,1]{0,1,2:T(8,128)S(1)} %get-tuple-element.17), channel_id=1, source_target_pairs={{0,8},{8,16},{16,24},{1,9},{9,17},{17,25},{2,10},{10,18},{18,26},{... | collective-permute-start | bytes 26120 | tf_op jit(solution)/shard_map/ppermute | solution.py:17
  328.1 3.5 collective-permute-start.15
  (1 other events, 1.9 us)
Sparse Core Ops, SparseCore 0:
  121.6 126.2 all-reduce.2
where the time goes:
time: 357 us; the launch traced here: 352 us
  blocking collectives  139 us (39%)
  waiting for transfers between devices  79.4 us (22%)
  starting transfers between devices  48.6 us (14%)
  other arithmetic  28.9 us (8%)
  matrix products  21.7 us (6%)
  local copies, waits for them, and re-layouts  20.1 us (6%)
  between operations  14.5 us (4%)
    psum x1, blocking collectives, shards(): chan_top, pixel_gram = lax.psum((chan_top, pixel_gram), ('row', 'col'))  96.4 us
    psum x1, waiting for transfers between devices, shards(): pixel_top, chan_gram = lax.psum((part_top, part_gram), 'ch')  70.2 us
    psum x1, blocking collectives, shards(): pixel_top, chan_gram = lax.psum((part_top, part_gram), 'ch')  42.2 us
    ppermute x8, starting transfers between devices, padded_2(): lax.ppermute(lax.slice_in_dim(block, block.shape[dim] - width, None, axis...  27.1 us
    div x3, other arithmetic, smooth_once(): return combined / (1.0 + weights[0] + weights[1] + weights[2] + weights[3])  26.2 us
    ppermute x8, starting transfers between devices, padded_2(): lax.ppermute(lax.slice_in_dim(block, 0, width, axis=dim), axis, backward)  21.5 us
    unnamed x21, local copies, waits for them, and re-layouts  12.2 us
  transfers between devices with their start and end apart: 17, of which 8 were waited for; matrix products, arithmetic and copies ran while one was open for 3% of the time, Pallas kernels for 0%

commit v1 on v0

v1 whole, which is shorter than its diff:
```python
import jax
import jax.numpy as jnp
from jax import lax
from jax.sharding import PartitionSpec as P

SMOOTH = 3
epsilon = 1e-09


def with_borders(block, sides, width):
    for axis, dim in sides:
        count = lax.axis_size(axis)
        forward = [(i, i + 1) for i in range(count - 1)]
        backward = [(target, source) for source, target in forward]
        low = lax.ppermute(
            lax.slice_in_dim(block, block.shape[dim] - width, None, axis=dim), axis, forward
        )
        high = lax.ppermute(lax.slice_in_dim(block, 0, width, axis=dim), axis, backward)
        block = jnp.concatenate([low, block, high], axis=dim)
    return block


def coefficients(marked):
    center = marked[1:-1, 1:-1]
    result = []
    for neighbour in (marked[:-2, 1:-1], marked[2:, 1:-1], marked[1:-1, :-2], marked[1:-1, 2:]):
        result.append(
            jnp.where(neighbour == 0, 0.0, jnp.where(neighbour == center, 1.0, 0.25)).astype(
                jnp.float32
            )
        )
    return result


def trimmed(array, width):
    return array if width == 0 else array[..., width:-width, width:-width]


def smooth_share(field, weights):
    for step in range(SMOOTH):
        up, down, left, right = (trimmed(weight, step) for weight in weights)
        combined = field[:, 1:-1, 1:-1] + up * field[:, :-2, 1:-1] + down * field[:, 2:, 1:-1]
        combined = combined + left * field[:, 1:-1, :-2] + right * field[:, 1:-1, 2:]
        field = combined / (1.0 + up + down + left + right)
    return field


def doubled_sum(value, axis):
    count = lax.axis_size(axis)
    distance = 1
    while distance < count:
        value = value + lax.ppermute(value, axis, [(i, i ^ distance) for i in range(count)])
        distance *= 2
    return value


def copies_of_all(value, axis):
    count = lax.axis_size(axis)
    copies = jnp.broadcast_to(value[None], (count,) + value.shape)
    return lax.all_to_all(copies, axis, 0, 0, tiled=True)


def shards(spectra, pixel_factor, channel_factor, labels):
    precise = lax.Precision.HIGHEST
    contraction = (((1,), (1,)), ((), ()))
    factor_rank, row_count, col_count = pixel_factor.shape
    pixels = row_count * col_count
    channels = spectra.shape[0]
    shares = lax.axis_size("ch")
    share = factor_rank // shares
    flat_pixel = pixel_factor.reshape(factor_rank, pixels)
    flat_data = spectra.reshape(channels, pixels)
    marks = with_borders(labels + 1, (("row", 0), ("col", 1)), SMOOTH)
    weights = coefficients(marks)
    chan_top = lax.dot_general(
        flat_pixel, flat_data, contraction, precision=precise, preferred_element_type=jnp.float32
    )
    pixel_gram = lax.dot_general(
        flat_pixel, flat_pixel, contraction, precision=precise, preferred_element_type=jnp.float32
    )
    sums = doubled_sum(jnp.concatenate([pixel_gram, chan_top], axis=1), "col")
    sums = copies_of_all(sums, "row").sum(axis=0)
    pixel_gram, chan_top = sums[:, :factor_rank], sums[:, factor_rank:]
    lower = jnp.dot(
        pixel_gram, channel_factor, precision=precise, preferred_element_type=jnp.float32
    )
    new_channel = channel_factor * chan_top / (lower + epsilon)
    part_top = jnp.dot(
        new_channel, flat_data, precision=precise, preferred_element_type=jnp.float32
    )
    part_gram = lax.dot_general(
        new_channel, new_channel, contraction, precision=precise, preferred_element_type=jnp.float32
    )
    parts = jnp.concatenate([part_top, jnp.pad(part_gram, ((0, 0), (0, -factor_rank % 128)))], 1)
    parts = parts.reshape(shares, share, -1)
    parts = lax.all_to_all(parts, "ch", 0, 0, tiled=True).sum(axis=0)
    top, gram = parts[:, :pixels], parts[:, pixels : pixels + factor_rank]
    own = lax.dynamic_slice_in_dim(flat_pixel, lax.axis_index("ch") * share, share, axis=0)
    lower = jnp.dot(gram, flat_pixel, precision=precise, preferred_element_type=jnp.float32)
    field = (own * top / (lower + epsilon)).reshape(share, row_count, col_count)
    field = with_borders(field, (("row", 1), ("col", 2)), SMOOTH)
    field = smooth_share(field, weights)
    field = copies_of_all(field, "ch").reshape(factor_rank, row_count, col_count)
    return (field, new_channel)


def solution(mesh):
    placed = (P("ch", "row", "col"), P(None, "row", "col"), P(None, "ch"), P("row", "col"))
    return jax.shard_map(
        shards,
        mesh=mesh,
        in_specs=placed,
        out_specs=(P(None, "row", "col"), P(None, "ch")),
        check_vma=False,
    )
```

time: 357 us -> 131 us (0.37)
  the two profiles are of different devices: /device:TPU:64 before, /device:TPU:1 now
where the time goes in v1:
time: 131 us; the launch traced here: 130 us
  starting transfers between devices  40.5 us (31%)
  waiting for transfers between devices  30.2 us (23%)
  blocking collectives  28 us (21%)
  matrix products  16.3 us (12%)
  local copies, waits for them, and re-layouts  8.68 us (7%)
  other arithmetic  5.53 us (4%)
    all_to_all x1, blocking collectives, copies_of_all(): return lax.all_to_all(copies, axis, 0, 0, tiled=True)  28 us
    ppermute x4, starting transfers between devices, with_borders(): lax.ppermute(lax.slice_in_dim(block, block.shape[dim] - width, None, axis...  17.4 us
    ppermute x4, waiting for transfers between devices, with_borders(): lax.ppermute(lax.slice_in_dim(block, 0, width, axis=dim), axis, backward)  13.8 us
    unnamed x14, local copies, waits for them, and re-layouts  7.38 us
    all_to_all x1, starting transfers between devices, shards(): parts = lax.all_to_all(parts, 'ch', 0, 0, tiled=True).sum(axis=0)  6.78 us
    all_to_all x1, waiting for transfers between devices, shards(): parts = lax.all_to_all(parts, 'ch', 0, 0, tiled=True).sum(axis=0)  6.61 us
    all_to_all x1, starting transfers between devices, copies_of_all(): return lax.all_to_all(copies, axis, 0, 0, tiled=True)  6.58 us
    ppermute x4, starting transfers between devices, with_borders(): lax.ppermute(lax.slice_in_dim(block, 0, width, axis=dim), axis, backward)  6.43 us
  transfers between devices with their start and end apart: 12, of which 9 were waited for; matrix products, arithmetic and copies ran while one was open for 5% of the time, Pallas kernels for 0%

profile of v1, /device:TPU:1, one launch (start us, length us, event | category | flops | bytes accessed | tf_op | source)
XLA Modules:
  0.0 130.2 jit_solution(16623230177731219028)
XLA Ops:
  0.6 6.4 %fusion.7 = f32[64,64]{1,0:T(8,128)S(1)} fusion(f32[64,32,256]{2,1,0:T(8,128)} %param.5), kind=kOutput, calls=%fused_computation.10 | convolution fusion | flops 402653184 | bytes 2113536 | tf_op jit(solution)/shard_map/dot_general | solution.py:78
  7.1 5.1 %fusion.10 = f32[64,48]{1,0:T(8,128)S(1)} fusion(f32[48,32,256]{2,1,0:T(8,128)} %param.4, f32[64,32,256]{2,1,0:T(8,128)S(1)} %copy-done), kind=kOutput, calls=%fused_computation.11 | convolution fusion | flops 301989888 | bytes 3682304 | tf_op jit(solution)/shard_map/dot_general | solution.py:75
  12.3 3.3 %collective-permute-start = (f32[64,112]{1,0:T(8,128)S(1)}, f32[64,112]{1,0:T(8,128)S(1)}, u32[]{:S(2)}, u32[]{:S(2)}) collective-permute-start(f32[64,112]{1,0:T(8,128)S(1)} %pad_maximum_fusion.2), channel_id=1, source_target_pairs={{0,8},{8,0},{16,24},{24,16},{1,9},{9,1},{17,25},{25,17},{2,10},{10... | collective-permute-start | bytes 86024 | tf_op jit(solution)/shard_map/ppermute | solution.py:52
  16.5 2.8 %collective-permute-done.1 = f32[64,112]{1,0:T(8,128)S(1)} collective-permute-done((f32[64,112]{1,0:T(8,128)S(1)}, f32[64,112]{1,0:T(8,128)S(1)}, u32[]{:S(2)}, u32[]{:S(2)}) %collective-permute-start.1) | collective-permute-done | bytes 28704 | tf_op jit(solution)/shard_map/ppermute | solution.py:52
  20.0 6.6 %all-to-all-start = ((f32[8,64,112]{2,1,0:T(8,128)}), f32[8,64,112]{2,1,0:T(8,128)S(1)}, u32[]{:S(2)}, u32[]{:S(2)}) async-start(f32[8,64,112]{2,1,0:T(8,128)} %broadcast_in_dim.25), calls=%async_computation | async-start | bytes 524288 | tf_op jit(solution)/shard_map/all_to_all | solution.py:60
  26.6 3.5 %copy.23 = f32[6,8,32,256]{3,1,2,0:T(8,128)} copy(f32[6,8,32,256]{3,2,1,0:T(8,128)} %bitcast.21) | data formatting | bytes 3145728
  30.0 6.1 %all-to-all-done = f32[8,64,112]{2,1,0:T(8,128)S(1)} async-done(((f32[8,64,112]{2,1,0:T(8,128)}), f32[8,64,112]{2,1,0:T(8,128)S(1)}, u32[]{:S(2)}, u32[]{:S(2)}) %all-to-all-start) | async-done | bytes 229408 | tf_op jit(solution)/shard_map/all_to_all | solution.py:60
  36.8 3.2 %fusion.39 = f32[64,8192]{1,0:T(8,128)S(1)} fusion(f32[64,48]{0,1:T(8,128)S(1)} %fusion.15, f32[48,8192]{1,0:T(8,128)} %bitcast.22), kind=kOutput, calls=%fused_computation.63 | convolution fusion | flops 301989888 | bytes 3682304 | tf_op jit(solution)/shard_map/dot_general | solution.py:88
  40.0 1.5 %fusion.1 = f32[8,8,8320]{2,1,0:T(8,128)} fusion(f32[64,64]{1,0:T(8,128)S(1)} %fusion.40, f32[64,8192]{1,0:T(8,128)S(1)} %fusion.39), kind=kLoop, calls=%fused_computation.3 | loop fusion | flops 1597440 | bytes 4243456 | tf_op jit(solution)/shard_map/reshape | solution.py:95
  41.5 6.8 %all-to-all-start.1 = ((f32[8,8,8320]{2,1,0:T(8,128)}), f32[8,8,8320]{2,1,0:T(8,128)}, u32[]{:S(2)}, u32[]{:S(2)}) async-start(f32[8,8,8320]{2,1,0:T(8,128)} %fusion.1), calls=%async_computation.1 | async-start | bytes 4259840 | tf_op jit(solution)/shard_map/all_to_all | solution.py:96
  48.3 1.9 %collective-permute-start.6 = (s32[3,256]{1,0:T(4,128)S(1)}, s32[3,256]{1,0:T(4,128)S(1)}, u32[]{:S(2)}, u32[]{:S(2)}) collective-permute-start(s32[3,256]{1,0:T(4,128)S(1)} %get-tuple-element.23), channel_id=1, source_target_pairs={{0,32},{32,64},{64,96},{96,128},{128,160},{160,192},{192,224},{1,3... | collective-permute-start | bytes 9224 | tf_op jit(solution)/shard_map/ppermute | solution.py:15
  51.5 3.0 %collective-permute-done.7 = s32[3,256]{1,0:T(4,128)S(1)} collective-permute-done((s32[3,256]{1,0:T(4,128)S(1)}, s32[3,256]{1,0:T(4,128)S(1)}, u32[]{:S(2)}, u32[]{:S(2)}) %collective-permute-start.7) | collective-permute-done | bytes 3104 | tf_op jit(solution)/shard_map/ppermute | solution.py:18
  54.6 7.5 %collective-permute-start.8 = (s32[38,3]{1,0:T(8,128)S(1)}, s32[38,3]{1,0:T(8,128)S(1)}, u32[]{:S(2)}, u32[]{:S(2)}) collective-permute-start(s32[38,3]{1,0:T(8,128)S(1)} %get-tuple-element.21), channel_id=1, source_target_pairs={{0,8},{8,16},{16,24},{1,9},{9,17},{17,25},{2,10},{10,18},{18,26},{... | collective-permute-start | bytes 1376 | tf_op jit(solution)/shard_map/ppermute | solution.py:15
  62.1 1.9 %collective-permute-start.9 = (s32[38,3]{1,0:T(8,128)S(1)}, s32[38,3]{1,0:T(8,128)S(1)}, u32[]{:S(2)}, u32[]{:S(2)}) collective-permute-start(s32[38,3]{1,0:T(8,128)S(1)} %get-tuple-element.22), channel_id=1, source_target_pairs={{8,0},{16,8},{24,16},{9,1},{17,9},{25,17},{10,2},{18,10},{26,18},{... | collective-permute-start | bytes 1376 | tf_op jit(solution)/shard_map/ppermute | solution.py:18
  64.0 2.5 %copy.22 = f32[8,8,32,256]{3,1,2,0:T(8,128)} copy(f32[8,8,32,256]{3,2,1,0:T(8,128)S(1)} %bitcast.18) | data formatting | bytes 4194304
  66.6 3.2 %collective-permute-done.9 = s32[38,3]{1,0:T(8,128)S(1)} collective-permute-done((s32[38,3]{1,0:T(8,128)S(1)}, s32[38,3]{1,0:T(8,128)S(1)}, u32[]{:S(2)}, u32[]{:S(2)}) %collective-permute-start.9) | collective-permute-done | bytes 488 | tf_op jit(solution)/shard_map/ppermute | solution.py:18
  70.0 6.6 %all-to-all-done.1 = f32[8,8,8320]{2,1,0:T(8,128)} async-done(((f32[8,8,8320]{2,1,0:T(8,128)}), f32[8,8,8320]{2,1,0:T(8,128)}, u32[]{:S(2)}, u32[]{:S(2)}) %all-to-all-start.1) | async-done | bytes 2129952 | tf_op jit(solution)/shard_map/all_to_all | solution.py:96
  76.6 1.7 %reduce_sum.19 = f32[8,8320]{1,0:T(8,128)S(1)} reduce(f32[8,8,8320]{2,1,0:T(8,128)} %all-to-all-done.1, f32[]{:T(128)} %constant.13.clone.1), dimensions={0}, to_apply=%region_1.2 | reduce | flops 465920 | bytes 2396164 | tf_op jit(solution)/shard_map/reduce_sum | solution.py:96
  79.5 1.6 %collective-permute-start.2 = (f32[8,3,256]{2,0,1:T(8,128)S(1)}, f32[8,3,256]{2,0,1:T(8,128)S(1)}, u32[]{:S(2)}, u32[]{:S(2)}) collective-permute-start(f32[8,3,256]{2,0,1:T(8,128)S(1)} %get-tuple-element.9), channel_id=1, source_target_pairs={{0,32},{32,64},{64,96},{96,128},{128,160},{160,192},{192,224},{1,3... | collective-permute-start | bytes 73736 | tf_op jit(solution)/shard_map/ppermute | solution.py:15
  82.6 3.1 %collective-permute-done.3 = f32[8,3,256]{2,0,1:T(8,128)S(1)} collective-permute-done((f32[8,3,256]{2,0,1:T(8,128)S(1)}, f32[8,3,256]{2,0,1:T(8,128)S(1)}, u32[]{:S(2)}, u32[]{:S(2)}) %collective-permute-start.3) | collective-permute-done | bytes 24608 | tf_op jit(solution)/shard_map/ppermute | solution.py:18
  85.8 6.5 %collective-permute-start.4 = (f32[8,38,3]{2,0,1:T(8,128)S(1)}, f32[8,38,3]{2,0,1:T(8,128)S(1)}, u32[]{:S(2)}, u32[]{:S(2)}) collective-permute-start(f32[8,38,3]{2,0,1:T(8,128)S(1)} %get-tuple-element.7), channel_id=1, source_target_pairs={{0,8},{8,16},{16,24},{1,9},{9,17},{17,25},{2,10},{10,18},{18,26},{... | collective-permute-start | bytes 10952 | tf_op jit(solution)/shard_map/ppermute | solution.py:15
  92.3 1.9 %collective-permute-start.5 = (f32[8,38,3]{2,0,1:T(8,128)S(1)}, f32[8,38,3]{2,0,1:T(8,128)S(1)}, u32[]{:S(2)}, u32[]{:S(2)}) collective-permute-start(f32[8,38,3]{2,0,1:T(8,128)S(1)} %get-tuple-element.8), channel_id=1, source_target_pairs={{8,0},{16,8},{24,16},{9,1},{17,9},{25,17},{10,2},{18,10},{26,18},{... | collective-permute-start | bytes 10952 | tf_op jit(solution)/shard_map/ppermute | solution.py:18
  94.4 4.4 %collective-permute-done.5 = f32[8,38,3]{2,0,1:T(8,128)S(1)} collective-permute-done((f32[8,38,3]{2,0,1:T(8,128)S(1)}, f32[8,38,3]{2,0,1:T(8,128)S(1)}, u32[]{:S(2)}, u32[]{:S(2)}) %collective-permute-start.5) | collective-permute-done | bytes 3680 | tf_op jit(solution)/shard_map/ppermute | solution.py:18
  100.8 28.0 %all_to_all.15 = f32[8,8,32,256]{3,2,1,0:T(8,128)S(1)} all-to-all(f32[8,8,32,256]{3,2,1,0:T(8,128)S(1)} %broadcast_in_dim.52), channel_id=1, replica_groups=mesh['row'=8,'col'=4,'ch'=8] {'ch'}, dimensions={0} | all-to-all | bytes 4194304 | tf_op jit(solution)/shard_map/all_to_all | solution.py:60
  (46 shorter events, 10.2 us)
Async XLA Ops:
  0.6 6.4 %copy-start = (f32[64,32,256]{2,1,0:T(8,128)S(1)}, f32[64,32,256]{2,1,0:T(8,128)}, u32[]{:S(2)}) copy-start(f32[64,32,256]{2,1,0:T(8,128)} %param.5) | copy-start | bytes 6291460
  12.3 4.1 %collective-permute-start = (f32[64,112]{1,0:T(8,128)S(1)}, f32[64,112]{1,0:T(8,128)S(1)}, u32[]{:S(2)}, u32[]{:S(2)}) collective-permute-start(f32[64,112]{1,0:T(8,128)S(1)} %pad_maximum_fusion.2), channel_id=1, source_target_pairs={{0,8},{8,0},{16,24},{24,16},{1,9},{9,1},{17,25},{25,17},{2,10},{10... | collective-permute-start | bytes 86024 | tf_op jit(solution)/shard_map/ppermute | solution.py:52
  16.5 2.8 %collective-permute-start.1 = (f32[64,112]{1,0:T(8,128)S(1)}, f32[64,112]{1,0:T(8,128)S(1)}, u32[]{:S(2)}, u32[]{:S(2)}) collective-permute-start(f32[64,112]{1,0:T(8,128)S(1)} %fusion.47), channel_id=1, source_target_pairs={{0,16},{8,24},{16,0},{24,8},{1,17},{9,25},{17,1},{25,9},{2,18},{10... | collective-permute-start | bytes 86024 | tf_op jit(solution)/shard_map/ppermute | solution.py:52
  20.0 16.3 %copy-start.4 = (f32[64,48]{0,1:T(8,128)S(1)}, f32[64,48]{0,1:T(8,128)}, u32[]{:S(2)}) copy-start(f32[64,48]{0,1:T(8,128)} %param.6) | copy-start | bytes 36868
  20.0 16.1 %all-to-all-start = ((f32[8,64,112]{2,1,0:T(8,128)}), f32[8,64,112]{2,1,0:T(8,128)S(1)}, u32[]{:S(2)}, u32[]{:S(2)}) async-start(f32[8,64,112]{2,1,0:T(8,128)} %broadcast_in_dim.25), calls=%async_computation | async-start | bytes 524288 | tf_op jit(solution)/shard_map/all_to_all | solution.py:60
  36.5 5.0 %copy-start.2 = (f32[64,48]{0,1:T(8,128)}, f32[64,48]{0,1:T(8,128)S(1)}, u32[]{:S(2)}) copy-start(f32[64,48]{0,1:T(8,128)S(1)} %fusion.15) | copy-start | bytes 36868
  41.5 6.8 %copy-start.3 = (s32[32,256]{1,0:T(8,128)S(1)}, s32[32,256]{1,0:T(8,128)}, u32[]{:S(2)}) copy-start(s32[32,256]{1,0:T(8,128)} %param.7) | copy-start | bytes 98308
  41.5 35.1 %all-to-all-start.1 = ((f32[8,8,8320]{2,1,0:T(8,128)}), f32[8,8,8320]{2,1,0:T(8,128)}, u32[]{:S(2)}, u32[]{:S(2)}) async-start(f32[8,8,8320]{2,1,0:T(8,128)} %fusion.1), calls=%async_computation.1 | async-start | bytes 4259840 | tf_op jit(solution)/shard_map/all_to_all | solution.py:96
  48.3 3.2 %collective-permute-start.6 = (s32[3,256]{1,0:T(4,128)S(1)}, s32[3,256]{1,0:T(4,128)S(1)}, u32[]{:S(2)}, u32[]{:S(2)}) collective-permute-start(s32[3,256]{1,0:T(4,128)S(1)} %get-tuple-element.23), channel_id=1, source_target_pairs={{0,32},{32,64},{64,96},{96,128},{128,160},{160,192},{192,224},{1,3... | collective-permute-start | bytes 9224 | tf_op jit(solution)/shard_map/ppermute | solution.py:15
  50.2 4.4 %collective-permute-start.7 = (s32[3,256]{1,0:T(4,128)S(1)}, s32[3,256]{1,0:T(4,128)S(1)}, u32[]{:S(2)}, u32[]{:S(2)}) collective-permute-start(s32[3,256]{1,0:T(4,128)S(1)} %get-tuple-element.24), channel_id=1, source_target_pairs={{32,0},{64,32},{96,64},{128,96},{160,128},{192,160},{224,192},{33,... | collective-permute-start | bytes 9224 | tf_op jit(solution)/shard_map/ppermute | solution.py:18
  54.6 11.9 %collective-permute-start.8 = (s32[38,3]{1,0:T(8,128)S(1)}, s32[38,3]{1,0:T(8,128)S(1)}, u32[]{:S(2)}, u32[]{:S(2)}) collective-permute-start(s32[38,3]{1,0:T(8,128)S(1)} %get-tuple-element.21), channel_id=1, source_target_pairs={{0,8},{8,16},{16,24},{1,9},{9,17},{17,25},{2,10},{10,18},{18,26},{... | collective-permute-start | bytes 1376 | tf_op jit(solution)/shard_map/ppermute | solution.py:15
  62.1 7.7 %collective-permute-start.9 = (s32[38,3]{1,0:T(8,128)S(1)}, s32[38,3]{1,0:T(8,128)S(1)}, u32[]{:S(2)}, u32[]{:S(2)}) collective-permute-start(s32[38,3]{1,0:T(8,128)S(1)} %get-tuple-element.22), channel_id=1, source_target_pairs={{8,0},{16,8},{24,16},{9,1},{17,9},{25,17},{10,2},{18,10},{26,18},{... | collective-permute-start | bytes 1376 | tf_op jit(solution)/shard_map/ppermute | solution.py:18
  66.6 11.8 %copy-start.1 = (f32[8,8,32,256]{3,1,2,0:T(8,128)S(1)}, f32[8,8,32,256]{3,1,2,0:T(8,128)}, u32[]{:S(2)}) copy-start(f32[8,8,32,256]{3,1,2,0:T(8,128)} %copy.22) | copy-start | bytes 6291460
  79.5 3.1 %collective-permute-start.2 = (f32[8,3,256]{2,0,1:T(8,128)S(1)}, f32[8,3,256]{2,0,1:T(8,128)S(1)}, u32[]{:S(2)}, u32[]{:S(2)}) collective-permute-start(f32[8,3,256]{2,0,1:T(8,128)S(1)} %get-tuple-element.9), channel_id=1, source_target_pairs={{0,32},{32,64},{64,96},{96,128},{128,160},{160,192},{192,224},{1,3... | collective-permute-start | bytes 73736 | tf_op jit(solution)/shard_map/ppermute | solution.py:15
  81.1 4.6 %collective-permute-start.3 = (f32[8,3,256]{2,0,1:T(8,128)S(1)}, f32[8,3,256]{2,0,1:T(8,128)S(1)}, u32[]{:S(2)}, u32[]{:S(2)}) collective-permute-start(f32[8,3,256]{2,0,1:T(8,128)S(1)} %get-tuple-element.10), channel_id=1, source_target_pairs={{32,0},{64,32},{96,64},{128,96},{160,128},{192,160},{224,192},{33,... | collective-permute-start | bytes 73736 | tf_op jit(solution)/shard_map/ppermute | solution.py:18
  85.8 8.6 %collective-permute-start.4 = (f32[8,38,3]{2,0,1:T(8,128)S(1)}, f32[8,38,3]{2,0,1:T(8,128)S(1)}, u32[]{:S(2)}, u32[]{:S(2)}) collective-permute-start(f32[8,38,3]{2,0,1:T(8,128)S(1)} %get-tuple-element.7), channel_id=1, source_target_pairs={{0,8},{8,16},{16,24},{1,9},{9,17},{17,25},{2,10},{10,18},{18,26},{... | collective-permute-start | bytes 10952 | tf_op jit(solution)/shard_map/ppermute | solution.py:15
  92.3 6.5 %collective-permute-start.5 = (f32[8,38,3]{2,0,1:T(8,128)S(1)}, f32[8,38,3]{2,0,1:T(8,128)S(1)}, u32[]{:S(2)}, u32[]{:S(2)}) collective-permute-start(f32[8,38,3]{2,0,1:T(8,128)S(1)} %get-tuple-element.8), channel_id=1, source_target_pairs={{8,0},{16,8},{24,16},{9,1},{17,9},{25,17},{10,2},{18,10},{26,18},{... | collective-permute-start | bytes 10952 | tf_op jit(solution)/shard_map/ppermute | solution.py:18

commit v2 on v1

v2 whole, which is shorter than its diff:
```python
import jax
import jax.numpy as jnp
from jax import lax
from jax.experimental import pallas as pl
from jax.experimental.pallas import tpu as pltpu
from jax.sharding import PartitionSpec as P

SMOOTH = 3
LANES = 128
epsilon = 1e-09
VMEM_LIMIT = 56 * 1024 * 1024


def with_borders(block, sides, width):
    for axis, dim in sides:
        count = lax.axis_size(axis)
        forward = [(i, i + 1) for i in range(count - 1)]
        backward = [(target, source) for source, target in forward]
        low = lax.ppermute(
            lax.slice_in_dim(block, block.shape[dim] - width, None, axis=dim), axis, forward
        )
        high = lax.ppermute(lax.slice_in_dim(block, 0, width, axis=dim), axis, backward)
        block = jnp.concatenate([low, block, high], axis=dim)
    return block


def doubled_sum(value, axis):
    count = lax.axis_size(axis)
    distance = 1
    while distance < count:
        value = value + lax.ppermute(value, axis, [(i, i ^ distance) for i in range(count)])
        distance *= 2
    return value


def copies_of_all(value, axis):
    count = lax.axis_size(axis)
    copies = jnp.broadcast_to(value[None], (count,) + value.shape)
    return lax.all_to_all(copies, axis, 0, 0, tiled=True)


def kernel_call(kernel, out_shape, scratch_shapes=(), smem=0, operands=(), flops=0):
    traffic = sum(x.size * 4 for x in operands) + sum(x.size * 4 for x in jax.tree.leaves(out_shape))
    in_specs = [
        pl.BlockSpec(memory_space=pltpu.SMEM if i < smem else pltpu.VMEM)
        for i in range(len(operands))
    ]
    return pl.pallas_call(
        kernel,
        out_shape=out_shape,
        in_specs=in_specs,
        out_specs=jax.tree.map(lambda _: pl.BlockSpec(memory_space=pltpu.VMEM), out_shape),
        scratch_shapes=scratch_shapes,
        compiler_params=pltpu.CompilerParams(vmem_limit_bytes=VMEM_LIMIT),
        cost_estimate=pl.CostEstimate(flops=flops, bytes_accessed=traffic, transcendentals=0),
    )(*operands)


def split(value):
    high = value.astype(jnp.bfloat16)
    low = (value - high.astype(jnp.float32)).astype(jnp.bfloat16)
    return high, low


def gram_kernel(place_ref, data_ref, factor_ref, sums_ref, send_ref, own_ref, rows_ref, wide, tall):
    channels, row_count, col_count = data_ref.shape
    rank = factor_ref.shape[0]
    half = 2 * rank
    for top in (0, half):
        wide[top + rank + channels : top + half, :] = jnp.zeros(
            (rank - channels, row_count * col_count), jnp.bfloat16
        )
    lane = lax.broadcasted_iota(jnp.int32, (rank, LANES), 1)
    data_sides = [jnp.zeros((channels, LANES), jnp.float32)] * 2
    factor_sides = [jnp.zeros((rank, LANES), jnp.float32)] * 2
    for row in range(row_count):
        columns = slice(row * col_count, (row + 1) * col_count)
        data = data_ref[:, row, :]
        factor = factor_ref[:, row, :]
        send_ref[row // 4, row % 4] = data
        rows_ref[row // 4, row % 4] = factor
        if row >= row_count - 3:
            send_ref[row - row_count + 3, 4] = data
            rows_ref[row - row_count + 3, 4] = factor
        if row < 3:
            send_ref[3 + row, 4] = data
            rows_ref[3 + row, 4] = factor
        here = (lane >= 3 * row) & (lane < 3 * row + 3)
        for side, (first, shift) in enumerate(((col_count - LANES, 3 * row + 3), (0, 3 * row))):
            piece = pltpu.roll(data[:, first : first + LANES], shift, 1)
            data_sides[side] = jnp.where(here[:channels], piece, data_sides[side])
            piece = pltpu.roll(factor[:, first : first + LANES], shift, 1)
            factor_sides[side] = jnp.where(here, piece, factor_sides[side])
        high, low = split(factor)
        tall[0:rank, columns] = high
        tall[rank:half, columns] = low
        wide[0:rank, columns] = high
        wide[half : half + rank, columns] = low
        high, low = split(data)
        wide[rank : rank + channels, columns] = high
        wide[half + rank : half + rank + channels, columns] = low
    for side in range(2):
        send_ref[6 + side, 4, :, 0:LANES] = data_sides[side]
        send_ref[6 + side, 4, :, LANES:] = jnp.zeros((channels, col_count - LANES), jnp.float32)
        rows_ref[6 + side, 4, :, 0:LANES] = factor_sides[side]
        rows_ref[6 + side, 4, :, LANES:] = jnp.zeros((rank, col_count - LANES), jnp.float32)
    own_ref[...] = rows_ref[place_ref[0]]
    products = lax.dot_general(
        wide[...], tall[...], (((1,), (1,)), ((), ())), preferred_element_type=jnp.float32
    )
    products = products[0:half] + products[half:]
    products = products + pltpu.roll(products, rank, 1)
    packed = (rank + channels) // 2
    sums_ref[...] = jnp.where(lane[:packed] < rank, products[0:packed], products[packed : 2 * packed])


def channel_kernel(sums_ref, factor_ref, new_ref, copies_ref):
    channels, rank = factor_ref.shape
    total = sums_ref[0]
    for i in range(1, sums_ref.shape[0]):
        total = total + sums_ref[i]
    total = jnp.concatenate([total, pltpu.roll(total, rank, 1)], axis=0)[:, :rank]
    gram, top = total[:rank], total[rank:]
    factor = factor_ref[...]
    lower = lax.dot_general(
        factor,
        gram,
        (((1,), (1,)), ((), ())),
        precision=lax.Precision.HIGHEST,
        preferred_element_type=jnp.float32,
    )
    new = factor * top / (lower + epsilon)
    new_ref[...] = new
    packed = channels // 2
    new = jnp.concatenate([new[:packed], new[packed:]], axis=1)
    for i in range(copies_ref.shape[0]):
        copies_ref[i] = new


def raise_kernel(new_ref, data_ref, factor_ref, raised_ref):
    shares, packed, _ = new_ref.shape
    strip, rank, col_count = factor_ref.shape
    parts = []
    for i in range(shares):
        parts += [new_ref[i], pltpu.roll(new_ref[i], rank, 1)]
    new = jnp.concatenate(parts, axis=0)
    new = jnp.transpose(new)[:rank]
    gram = lax.dot_general(
        new,
        new,
        (((1,), (1,)), ((), ())),
        precision=lax.Precision.HIGHEST,
        preferred_element_type=jnp.float32,
    )
    new = jnp.concatenate(split(new), axis=0)
    gram = jnp.concatenate(split(gram), axis=0)

    def product(left, right):
        high, low = split(right)
        both = jnp.dot(left, high, preferred_element_type=jnp.float32)
        both = both + jnp.dot(left, low, preferred_element_type=jnp.float32)
        return both[:rank] + both[rank:]

    for row in range(strip):
        data = jnp.concatenate([data_ref[i, row] for i in range(shares)], axis=0)
        factor = factor_ref[row]
        raised_ref[row] = factor * product(new, data) / (product(gram, factor) + epsilon)


def smooth_kernel(marks_ref, gathered_ref, out_ref, first, second, weights_ref):
    rank, row_count, col_count = out_ref.shape
    width = marks_ref.shape[1]
    tall = row_count + 2 * SMOOTH
    marks = marks_ref[...]
    total = jnp.ones(marks.shape, jnp.float32)
    found = []
    for shift, axis in ((1, 0), (marks.shape[0] - 1, 0), (1, 1), (width - 1, 1)):
        neighbour = pltpu.roll(marks, shift, axis)
        weight = jnp.where(neighbour == marks, 1.0, 0.25)
        weight = jnp.where(neighbour == 0.0, 0.0, weight)
        found.append(weight)
        total = total + weight
    weights_ref[0] = 1.0 / total
    for i, weight in enumerate(found):
        weights_ref[1 + i] = weight / total
    lane = lax.broadcasted_iota(jnp.int32, (rank, LANES), 1)
    for row in range(tall):
        inner = row - SMOOTH
        if inner < 0:
            main, start, at = gathered_ref[row, 4], LANES, 3 * (row_count + inner)
        elif inner < row_count:
            main, start, at = gathered_ref[inner // 4, inner % 4], 0, 3 * inner
        else:
            main, start, at = gathered_ref[3 + inner - row_count, 4], LANES, 3 * (inner - row_count)
        left = pltpu.roll(gathered_ref[6, 4, :, start : start + LANES], (LANES - 3 - at) % LANES, 1)
        right = pltpu.roll(gathered_ref[7, 4, :, start : start + LANES], (LANES - at) % LANES, 1)
        side = jnp.where(lane >= LANES - 3, left, jnp.where(lane < 3, right, 0.0))
        first[row, :, 0:col_count] = main
        first[row, :, col_count:] = side

    def smoothed(source, row):
        def weight(i):
            return weights_ref[i, pl.ds(row, 1), :]

        field = source[row]
        value = weight(0) * field + weight(1) * source[row - 1] + weight(2) * source[row + 1]
        value = value + weight(3) * pltpu.roll(field, 1, 1)
        return value + weight(4) * pltpu.roll(field, width - 1, 1)

    @pl.loop(1, tall - 1)
    def _(row):
        second[row] = smoothed(first, row)

    @pl.loop(2, tall - 2)
    def _(row):
        first[row] = smoothed(second, row)

    for row in range(row_count):
        out_ref[:, row, :] = smoothed(first, row + SMOOTH)[:, :col_count]


def border_moves(axes, count_ch):
    rows, cols = axes

    def moves(steps):
        pairs = []
        for row in range(rows):
            for col in range(cols):
                for ch, (down, across) in steps.items():
                    if 0 <= row + down < rows and 0 <= col + across < cols:
                        source = (row * cols + col) * count_ch + ch
                        target = ((row + down) * cols + col + across) * count_ch + ch
                        pairs.append((source, target))
        return pairs

    straight = {ch: (1, 0) for ch in range(3)} | {ch: (-1, 0) for ch in range(3, 6)}
    straight |= {6: (0, 1), 7: (0, -1)}
    return moves(straight), moves({6: (1, 1), 7: (1, -1)}), moves({6: (-1, 1), 7: (-1, -1)})


def shards(spectra, pixel_factor, channel_factor, labels):
    rank, row_count, col_count = pixel_factor.shape
    channels = spectra.shape[0]
    shares = lax.axis_size("ch")
    place = lax.axis_index("ch")
    pixels = row_count * col_count
    strip = row_count // shares + 1

    marks = with_borders(labels + 1, (("row", 0), ("col", 1)), SMOOTH).astype(jnp.float32)
    pad = jnp.zeros((marks.shape[0], LANES - 2 * SMOOTH), jnp.float32)
    marks = jnp.concatenate([marks[:, SMOOTH:], pad, marks[:, :SMOOTH]], axis=1)
    marks = jnp.pad(marks, ((0, -marks.shape[0] % 8), (0, 0)))

    f32 = jnp.float32
    operands = (place.reshape(1), spectra, pixel_factor)
    sums, send, own = kernel_call(
        gram_kernel,
        (
            jax.ShapeDtypeStruct(((rank + channels) // 2, 2 * rank), f32),
            jax.ShapeDtypeStruct((shares, strip, channels, col_count), f32),
            jax.ShapeDtypeStruct((strip, rank, col_count), f32),
        ),
        scratch_shapes=[
            pltpu.VMEM((shares, strip, rank, col_count), f32),
            pltpu.VMEM((4 * rank, pixels), jnp.bfloat16),
            pltpu.VMEM((2 * rank, pixels), jnp.bfloat16),
        ],
        smem=1,
        operands=operands,
        flops=16 * rank * rank * pixels,
    )
    data = lax.all_to_all(send, "ch", 0, 0, tiled=True)
    sums = copies_of_all(doubled_sum(sums, "col"), "row")
    new_channel, copies = kernel_call(
        channel_kernel,
        (
            jax.ShapeDtypeStruct((channels, rank), f32),
            jax.ShapeDtypeStruct((shares, channels // 2, 2 * rank), f32),
        ),
        operands=(sums, channel_factor.T),
    )
    copies = lax.all_to_all(copies, "ch", 0, 0, tiled=True)
    raised = kernel_call(
        raise_kernel,
        jax.ShapeDtypeStruct((strip, rank, col_count), f32),
        operands=(copies, data, own),
        flops=8 * rank * (rank + channels * shares) * strip * col_count,
    )
    piece = raised[strip - 1]
    axes = (lax.axis_size("row"), lax.axis_size("col"))
    straight, below, above = border_moves(axes, shares)
    everywhere = ("row", "col", "ch")
    corner = piece[:, :LANES]
    piece = lax.ppermute(piece, everywhere, straight)
    below = lax.ppermute(corner, everywhere, below)
    above = lax.ppermute(corner, everywhere, above)
    lane = lax.broadcasted_iota(jnp.int32, corner.shape, 1)
    corner = jnp.where(lane >= LANES // 2, below, above)
    sides = jnp.concatenate([piece[:, :LANES], corner], axis=1)
    piece = jnp.where(place >= 6, sides, piece)
    gathered = copies_of_all(jnp.concatenate([raised[: strip - 1], piece[None]], axis=0), "ch")
    tall = row_count + 2 * SMOOTH
    width = col_count + LANES
    field = kernel_call(
        smooth_kernel,
        jax.ShapeDtypeStruct((rank, row_count, col_count), f32),
        scratch_shapes=[
            pltpu.VMEM((tall, rank, width), f32),
            pltpu.VMEM((tall, rank, width), f32),
            pltpu.VMEM((5,) + marks.shape, f32),
        ],
        operands=(marks, gathered),
    )
    return (field, new_channel.T)


def solution(mesh):
    placed = (P("ch", "row", "col"), P(None, "row", "col"), P(None, "ch"), P("row", "col"))
    return jax.shard_map(
        shards,
        mesh=mesh,
        in_specs=placed,
        out_specs=(P(None, "row", "col"), P(None, "ch")),
        check_vma=False,
    )
```

time: 131 us -> 161 us (1.23)
  Pallas kernels: 0 us -> 37.5 us
  blocking collectives: 28 us -> 54.8 us
  matrix products: 16.3 us -> 0 us
  starting transfers between devices: 40.5 us -> 29.1 us
  other arithmetic: 5.53 us -> 1 us
  local copies, waits for them, and re-layouts: 8.68 us -> 5.99 us
    all_to_all x0 -> x2, blocking collectives: none -> 39.6 us  [the longest x1 26.2 us: shards(): data = lax.all_to_all(send, 'ch', 0, 0, tiled=True)]
    pallas_call x0 -> x4, Pallas kernels: none -> 37.5 us  [kernel_call(): pl.pallas_call(kernel, out_shape=out_shape, in_specs=in_specs, out_specs=...]
    dot_general x6 -> x0, matrix products: 16.3 us -> none  [the longest x1 6.4 us: shards(): lax.dot_general(flat_pixel, flat_pixel, contraction, precision=precise, p...]
    all_to_all x1, blocking collectives: 28 us -> 15.2 us  [copies_of_all(): return lax.all_to_all(copies, axis, 0, 0, tiled=True)]
    ppermute x4 -> x2, starting transfers between devices: 17.4 us -> 6.39 us  [with_borders(): lax.ppermute(lax.slice_in_dim(block, block.shape[dim] - width, None, axis...]
    ppermute x4 -> x2, waiting for transfers between devices: 13.8 us -> 3.58 us  [with_borders(): lax.ppermute(lax.slice_in_dim(block, 0, width, axis=dim), axis, backward)]
    all_to_all x1, waiting for transfers between devices: 6.09 us -> 15.6 us  [copies_of_all(): return lax.all_to_all(copies, axis, 0, 0, tiled=True)]
    ppermute x4 -> x2, waiting for transfers between devices: 0.13 us -> 7.79 us  [with_borders(): lax.ppermute(lax.slice_in_dim(block, block.shape[dim] - width, None, axis...]
  transfers between devices with their start and end apart: 12 -> 10, of which waited for: 9 -> 7; matrix products, arithmetic and copies ran while one was open for 5% -> 1% of each run, Pallas kernels for 0% -> 0%
where the time goes in v2:
time: 161 us; the launch traced here: 160 us
  blocking collectives  54.8 us (34%)
  Pallas kernels  37.5 us (23%)
  waiting for transfers between devices  31 us (19%)
  starting transfers between devices  29.1 us (18%)
  local copies, waits for them, and re-layouts  5.99 us (4%)
    pallas_call x4, Pallas kernels, kernel_call(): pl.pallas_call(kernel, out_shape=out_shape, in_specs=in_specs, out_specs=...  37.5 us
    all_to_all x1, blocking collectives, shards(): data = lax.all_to_all(send, 'ch', 0, 0, tiled=True)  26.2 us
    all_to_all x1, waiting for transfers between devices, copies_of_all(): return lax.all_to_all(copies, axis, 0, 0, tiled=True)  15.6 us
    all_to_all x1, blocking collectives, copies_of_all(): return lax.all_to_all(copies, axis, 0, 0, tiled=True)  15.2 us
    all_to_all x1, blocking collectives, shards(): copies = lax.all_to_all(copies, 'ch', 0, 0, tiled=True)  13.4 us
    all_to_all x1, starting transfers between devices, copies_of_all(): return lax.all_to_all(copies, axis, 0, 0, tiled=True)  13.2 us
    ppermute x2, waiting for transfers between devices, with_borders(): lax.ppermute(lax.slice_in_dim(block, block.shape[dim] - width, None, axis...  7.79 us
    ppermute x2, starting transfers between devices, with_borders(): lax.ppermute(lax.slice_in_dim(block, block.shape[dim] - width, None, axis...  6.39 us
  transfers between devices with their start and end apart: 10, of which 7 were waited for; matrix products, arithmetic and copies ran while one was open for 1% of the time, Pallas kernels for 0%

profile of v2, /device:TPU:1, one launch (start us, length us, event | category | flops | bytes accessed | tf_op | source)
XLA Modules:
  0.0 160.2 jit_solution(18056371209405314744)
XLA Ops:
  0.6 17.4 %shard_map.59 = (f32[56,128]{1,0:T(8,128)}, f32[8,5,48,256]{3,2,1,0:T(8,128)}, f32[5,64,256]{2,1,0:T(8,128)}) custom-call(s32[1]{0:T(128)} %bitcast.place_ref, f32[48,32,256]{2,1,0:T(8,128)} %data_ref.1, f32[64,32,256]{2,1,0:T(8,128)} %factor_ref.1), custom_call_target="tpu_custom_call" | custom-call | flops 536870912 | bytes 5992452 | tf_op jit(solution)/shard_map/pallas_call | solution.py:48
  18.0 3.2 %collective-permute-start.4 = (f32[56,128]{1,0:T(8,128)}, f32[56,128]{1,0:T(8,128)S(1)}, u32[]{:S(2)}, u32[]{:S(2)}) collective-permute-start(f32[56,128]{1,0:T(8,128)} %get-tuple-element.7), channel_id=1, source_target_pairs={{0,8},{8,0},{16,24},{24,16},{1,9},{9,1},{17,25},{25,17},{2,10},{10... | collective-permute-start | bytes 86024 | tf_op jit(solution)/shard_map/ppermute | solution.py:31
  21.3 1.1 collective-permute-done.4
  22.3 0.8 add.16
  23.1 2.7 %collective-permute-done.5 = f32[56,128]{1,0:T(8,128)S(1)} collective-permute-done((f32[56,128]{1,0:T(8,128)S(1)}, f32[56,128]{1,0:T(8,128)S(1)}, u32[]{:S(2)}, u32[]{:S(2)}) %collective-permute-start.5) | collective-permute-done | bytes 28704 | tf_op jit(solution)/shard_map/ppermute | solution.py:31
  25.8 15.2 %all_to_all.20.sums_ref = f32[8,56,128]{2,1,0:T(8,128)} all-to-all(f32[8,56,128]{2,1,0:T(8,128)S(1)} %broadcast_in_dim.9), channel_id=1, replica_groups=mesh['row'=8,'col'=4,'ch'=8] {'row'}, dimensions={0} | all-to-all | bytes 458752 | tf_op jit(solution)/shard_map/all_to_all | solution.py:39
  41.1 1.9 %shard_map.60 = (f32[48,64]{1,0:T(8,128)}, f32[8,24,128]{2,1,0:T(8,128)}) custom-call(f32[8,56,128]{2,1,0:T(8,128)} %all_to_all.20.sums_ref, f32[48,64]{1,0:T(8,128)} %bitcast.7), custom_call_target="tpu_custom_call" | custom-call | bytes 352256 | tf_op jit(solution)/shard_map/pallas_call | solution.py:48
  43.0 13.4 %all_to_all.21.new_ref = f32[8,24,128]{2,1,0:T(8,128)} all-to-all(f32[8,24,128]{2,1,0:T(8,128)} %get-tuple-element.8), channel_id=1, replica_groups=mesh['row'=8,'col'=4,'ch'=8] {'ch'}, dimensions={0} | all-to-all | bytes 196608 | tf_op jit(solution)/shard_map/all_to_all | solution.py:282
  56.4 26.2 %all_to_all.22.data_ref = f32[8,5,48,256]{3,2,1,0:T(8,128)} all-to-all(f32[8,5,48,256]{3,2,1,0:T(8,128)} %get-tuple-element.9), channel_id=1, replica_groups=mesh['row'=8,'col'=4,'ch'=8] {'ch'}, dimensions={0} | all-to-all | bytes 3932160 | tf_op jit(solution)/shard_map/all_to_all | solution.py:272
  82.5 3.4 %shard_map.61 = f32[5,64,256]{2,1,0:T(8,128)} custom-call(f32[8,24,128]{2,1,0:T(8,128)} %all_to_all.21.new_ref, f32[8,5,48,256]{3,2,1,0:T(8,128)} %all_to_all.22.data_ref, f32[5,64,256]{2,1,0:T(8,128)} %get-tuple-element.10.factor_ref), custom_call_target="tpu_custom_call" | custom-call | flops 293601280 | bytes 2719744 | tf_op jit(solution)/shard_map/pallas_call | solution.py:48
  85.9 0.8 slice_bitcast_fusion
  88.1 1.7 %collective-permute-start.6 = (f32[64,256]{1,0:T(8,128)S(1)}, f32[64,256]{1,0:T(8,128)S(1)}, u32[]{:S(2)}, u32[]{:S(2)}) collective-permute-start(f32[64,256]{1,0:T(8,128)S(1)} %slice_bitcast_fusion), channel_id=1, source_target_pairs={{0,32},{1,33},{2,34},{6,14},{8,40},{9,41},{10,42},{14,22},{15,7},{... | collective-permute-start | bytes 196616 | tf_op jit(solution)/shard_map/ppermute | solution.py:294
  89.8 1.0 slice.45
  91.1 1.8 %broadcast_in_dim.21 = f32[8,5,64,256]{3,2,1,0:T(8,128)} broadcast(f32[5,64,256]{2,1,0:T(8,128)S(1)} %pad_maximum_fusion), dimensions={1,2,3} | broadcast | bytes 2949120 | tf_op jit(solution)/shard_map/broadcast_in_dim | solution.py:38
  92.9 13.2 %all-to-all-start.3 = ((f32[8,5,64,256]{3,2,1,0:T(8,128)}), f32[8,5,64,256]{3,2,1,0:T(8,128)S(1)}, u32[]{:S(2)}, u32[]{:S(2)}) async-start(f32[8,5,64,256]{3,2,1,0:T(8,128)} %broadcast_in_dim.21), calls=%async_computation.3 | async-start | bytes 5242880 | tf_op jit(solution)/shard_map/all_to_all | solution.py:39
  106.2 3.7 %collective-permute-start = (s32[3,256]{1,0:T(4,128)S(1)}, s32[3,256]{1,0:T(4,128)S(1)}, u32[]{:S(2)}, u32[]{:S(2)}) collective-permute-start(s32[3,256]{1,0:T(4,128)S(1)} %get-tuple-element.14), channel_id=1, source_target_pairs={{0,32},{32,64},{64,96},{96,128},{128,160},{160,192},{192,224},{1,3... | collective-permute-start | bytes 9224 | tf_op jit(solution)/shard_map/ppermute | solution.py:19
  109.9 1.3 collective-permute-start.1
  111.3 3.3 %collective-permute-done.1 = s32[3,256]{1,0:T(4,128)S(1)} collective-permute-done((s32[3,256]{1,0:T(4,128)S(1)}, s32[3,256]{1,0:T(4,128)S(1)}, u32[]{:S(2)}, u32[]{:S(2)}) %collective-permute-start.1) | collective-permute-done | bytes 3104 | tf_op jit(solution)/shard_map/ppermute | solution.py:22
  114.7 2.7 %collective-permute-start.2 = (s32[38,3]{1,0:T(8,128)S(1)}, s32[38,3]{1,0:T(8,128)S(1)}, u32[]{:S(2)}, u32[]{:S(2)}) collective-permute-start(s32[38,3]{1,0:T(8,128)S(1)} %get-tuple-element.12), channel_id=1, source_target_pairs={{0,8},{8,16},{16,24},{1,9},{9,17},{17,25},{2,10},{10,18},{18,26},{... | collective-permute-start | bytes 1376 | tf_op jit(solution)/shard_map/ppermute | solution.py:19
  117.4 1.9 %collective-permute-start.3 = (s32[38,3]{1,0:T(8,128)S(1)}, s32[38,3]{1,0:T(8,128)S(1)}, u32[]{:S(2)}, u32[]{:S(2)}) collective-permute-start(s32[38,3]{1,0:T(8,128)S(1)} %get-tuple-element.13), channel_id=1, source_target_pairs={{8,0},{16,8},{24,16},{9,1},{17,9},{25,17},{10,2},{18,10},{26,18},{... | collective-permute-start | bytes 1376 | tf_op jit(solution)/shard_map/ppermute | solution.py:22
  119.4 7.8 %collective-permute-done.2 = s32[38,3]{1,0:T(8,128)S(1)} collective-permute-done((s32[38,3]{1,0:T(8,128)S(1)}, s32[38,3]{1,0:T(8,128)S(1)}, u32[]{:S(2)}, u32[]{:S(2)}) %collective-permute-start.2) | collective-permute-done | bytes 488 | tf_op jit(solution)/shard_map/ppermute | solution.py:19
  128.3 15.6 %all-to-all-done.3.gathered_ref = f32[8,5,64,256]{3,2,1,0:T(8,128)S(1)} async-done(((f32[8,5,64,256]{3,2,1,0:T(8,128)}), f32[8,5,64,256]{3,2,1,0:T(8,128)S(1)}, u32[]{:S(2)}, u32[]{:S(2)}) %all-to-all-start.3) | async-done | bytes 2621472 | tf_op jit(solution)/shard_map/all_to_all | solution.py:39
  143.9 1.5 copy-done
  145.3 14.8 %shard_map.62 = f32[64,32,256]{2,1,0:T(8,128)} custom-call(f32[40,384]{1,0:T(8,128)} %pad.4.marks_ref, f32[8,5,64,256]{3,2,1,0:T(8,128)} %copy-done), custom_call_target="tpu_custom_call" | custom-call | bytes 4780032 | tf_op jit(solution)/shard_map/pallas_call | solution.py:48
  (30 shorter events, 3.0 us)
Async XLA Ops:
  18.0 4.3 %collective-permute-start.4 = (f32[56,128]{1,0:T(8,128)}, f32[56,128]{1,0:T(8,128)S(1)}, u32[]{:S(2)}, u32[]{:S(2)}) collective-permute-start(f32[56,128]{1,0:T(8,128)} %get-tuple-element.7), channel_id=1, source_target_pairs={{0,8},{8,0},{16,24},{24,16},{1,9},{9,1},{17,25},{25,17},{2,10},{10... | collective-permute-start | bytes 86024 | tf_op jit(solution)/shard_map/ppermute | solution.py:31
  23.1 2.7 %collective-permute-start.5 = (f32[56,128]{1,0:T(8,128)S(1)}, f32[56,128]{1,0:T(8,128)S(1)}, u32[]{:S(2)}, u32[]{:S(2)}) collective-permute-start(f32[56,128]{1,0:T(8,128)S(1)} %add.16), channel_id=1, source_target_pairs={{0,16},{8,24},{16,0},{24,8},{1,17},{9,25},{17,1},{25,9},{2,18},{10... | collective-permute-start | bytes 86024 | tf_op jit(solution)/shard_map/ppermute | solution.py:31
  86.8 4.0 %collective-permute-start.7 = (f32[64,128]{1,0:T(8,128)S(1)}, f32[64,128]{1,0:T(8,128)S(1)}, u32[]{:S(2)}, u32[]{:S(2)}) collective-permute-start(f32[64,128]{1,0:T(8,128)S(1)} %slice.48), channel_id=1, source_target_pairs={{6,46},{14,54},{15,39},{22,62},{23,47},{31,55},{38,78},{46,86},{47... | collective-permute-start | bytes 98312 | tf_op jit(solution)/shard_map/ppermute | solution.py:295
  87.4 3.3 %collective-permute-start.8 = (f32[64,128]{1,0:T(8,128)S(1)}, f32[64,128]{1,0:T(8,128)S(1)}, u32[]{:S(2)}, u32[]{:S(2)}) collective-permute-start(f32[64,128]{1,0:T(8,128)S(1)} %slice.48), channel_id=1, source_target_pairs={{38,14},{46,22},{47,7},{54,30},{55,15},{63,23},{70,46},{78,54},{79... | collective-permute-start | bytes 98312 | tf_op jit(solution)/shard_map/ppermute | solution.py:296
  88.1 3.0 %collective-permute-start.6 = (f32[64,256]{1,0:T(8,128)S(1)}, f32[64,256]{1,0:T(8,128)S(1)}, u32[]{:S(2)}, u32[]{:S(2)}) collective-permute-start(f32[64,256]{1,0:T(8,128)S(1)} %slice_bitcast_fusion), channel_id=1, source_target_pairs={{0,32},{1,33},{2,34},{6,14},{8,40},{9,41},{10,42},{14,22},{15,7},{... | collective-permute-start | bytes 196616 | tf_op jit(solution)/shard_map/ppermute | solution.py:294
  92.9 13.2 %copy-start.1 = (s32[32,256]{1,0:T(8,128)S(1)}, s32[32,256]{1,0:T(8,128)}, u32[]{:S(2)}) copy-start(s32[32,256]{1,0:T(8,128)} %param.7) | copy-start | bytes 98308
  92.9 50.9 %all-to-all-start.3 = ((f32[8,5,64,256]{3,2,1,0:T(8,128)}), f32[8,5,64,256]{3,2,1,0:T(8,128)S(1)}, u32[]{:S(2)}, u32[]{:S(2)}) async-start(f32[8,5,64,256]{3,2,1,0:T(8,128)} %broadcast_in_dim.21), calls=%async_computation.3 | async-start | bytes 5242880 | tf_op jit(solution)/shard_map/all_to_all | solution.py:39
  106.2 5.0 %collective-permute-start = (s32[3,256]{1,0:T(4,128)S(1)}, s32[3,256]{1,0:T(4,128)S(1)}, u32[]{:S(2)}, u32[]{:S(2)}) collective-permute-start(s32[3,256]{1,0:T(4,128)S(1)} %get-tuple-element.14), channel_id=1, source_target_pairs={{0,32},{32,64},{64,96},{96,128},{128,160},{160,192},{192,224},{1,3... | collective-permute-start | bytes 9224 | tf_op jit(solution)/shard_map/ppermute | solution.py:19
  109.9 4.6 %collective-permute-start.1 = (s32[3,256]{1,0:T(4,128)S(1)}, s32[3,256]{1,0:T(4,128)S(1)}, u32[]{:S(2)}, u32[]{:S(2)}) collective-permute-start(s32[3,256]{1,0:T(4,128)S(1)} %get-tuple-element.15), channel_id=1, source_target_pairs={{32,0},{64,32},{96,64},{128,96},{160,128},{192,160},{224,192},{33,... | collective-permute-start | bytes 9224 | tf_op jit(solution)/shard_map/ppermute | solution.py:22
  114.7 12.5 %collective-permute-start.2 = (s32[38,3]{1,0:T(8,128)S(1)}, s32[38,3]{1,0:T(8,128)S(1)}, u32[]{:S(2)}, u32[]{:S(2)}) collective-permute-start(s32[38,3]{1,0:T(8,128)S(1)} %get-tuple-element.12), channel_id=1, source_target_pairs={{0,8},{8,16},{16,24},{1,9},{9,17},{17,25},{2,10},{10,18},{18,26},{... | collective-permute-start | bytes 1376 | tf_op jit(solution)/shard_map/ppermute | solution.py:19
  117.4 10.0 %collective-permute-start.3 = (s32[38,3]{1,0:T(8,128)S(1)}, s32[38,3]{1,0:T(8,128)S(1)}, u32[]{:S(2)}, u32[]{:S(2)}) collective-permute-start(s32[38,3]{1,0:T(8,128)S(1)} %get-tuple-element.13), channel_id=1, source_target_pairs={{8,0},{16,8},{24,16},{9,1},{17,9},{25,17},{10,2},{18,10},{26,18},{... | collective-permute-start | bytes 1376 | tf_op jit(solution)/shard_map/ppermute | solution.py:22
  143.9 1.5 copy-start

commit v3 on v2

v3 whole, which is shorter than its diff:
```python
import jax
import jax.numpy as jnp
from jax import lax
from jax.experimental import pallas as pl
from jax.experimental.pallas import tpu as pltpu
from jax.sharding import PartitionSpec as P

SMOOTH = 3
LANES = 128
TILE = 8
epsilon = 1e-09
VMEM_LIMIT = 48 * 1024 * 1024


def doubled_sum(value, axis):
    count = lax.axis_size(axis)
    distance = 1
    while distance < count:
        value = value + lax.ppermute(value, axis, [(i, i ^ distance) for i in range(count)])
        distance *= 2
    return value


def copies_of_all(value, axis):
    count = lax.axis_size(axis)
    copies = jnp.broadcast_to(value[None], (count,) + value.shape)
    return lax.all_to_all(copies, axis, 0, 0, tiled=True)


def kernel_call(kernel, out_shape, scratch_shapes=(), smem=0, waits=0, apart=None, aliases={}, operands=(), flops=0):
    traffic = sum(x.size * 4 for x in operands) + sum(x.size * 4 for x in jax.tree.leaves(out_shape))
    in_specs = [
        pl.BlockSpec(memory_space=pltpu.SMEM if i < smem else pltpu.VMEM)
        for i in range(len(operands) - waits)
    ]
    in_specs += [pl.BlockSpec(memory_space=pl.ANY)] * waits
    return pl.pallas_call(
        kernel,
        out_shape=out_shape,
        in_specs=in_specs,
        out_specs=jax.tree.map(
            lambda x: pl.BlockSpec(memory_space=pl.ANY if x.shape == apart else pltpu.VMEM), out_shape
        ),
        scratch_shapes=scratch_shapes,
        input_output_aliases=aliases,
        compiler_params=pltpu.CompilerParams(vmem_limit_bytes=VMEM_LIMIT),
        cost_estimate=pl.CostEstimate(flops=flops, bytes_accessed=traffic, transcendentals=0),
    )(*operands)


def split(value):
    high = value.astype(jnp.bfloat16)
    low = (value - high.astype(jnp.float32)).astype(jnp.bfloat16)
    return high, low


def gram_kernel(
    place_ref, data_ref, factor_ref, labels_ref, sums_ref, send_ref, own_ref, rows_ref, wide, tall
):
    channels, row_count, col_count = data_ref.shape
    rank = factor_ref.shape[0]
    both = rank + channels
    half = 2 * rank
    lane = lax.broadcasted_iota(jnp.int32, (both + TILE, LANES), 1)
    sides = [jnp.zeros((both + TILE, LANES), jnp.float32)] * 2
    blank = jnp.zeros((half - both, col_count), jnp.bfloat16)
    none = jnp.zeros((both + TILE, col_count - LANES), jnp.float32)

    def keep(strip, at, factor, data, marks):
        send_ref[strip, at] = data
        rows_ref[strip, at, :rank] = factor
        rows_ref[strip, at, rank:] = marks

    for row in range(row_count):
        if row % 8 == 0:
            eight_data = jnp.swapaxes(data_ref[:, row : row + 8, :], 0, 1)
            eight_factor = jnp.swapaxes(factor_ref[:, row : row + 8, :], 0, 1)
        data, factor = eight_data[row % 8], eight_factor[row % 8]
        marks = (labels_ref[row : row + 1, :] + 1).astype(jnp.float32)
        marks = jnp.broadcast_to(marks, (TILE, col_count))
        keep(row // 4, row % 4, factor, data, marks)
        if row >= row_count - SMOOTH:
            keep(row - row_count + SMOOTH, 4, factor, data, marks)
        if row < SMOOTH:
            keep(SMOOTH + row, 4, factor, data, marks)
        value = jnp.concatenate([factor, data, marks], axis=0)
        here = (lane >= 3 * row) & (lane < 3 * row + 3)
        last = pltpu.roll(value[:, col_count - LANES :], 3 * row + 3, 1)
        sides[0] = jnp.where(here, last, sides[0])
        sides[1] = jnp.where(here, pltpu.roll(value[:, :LANES], 3 * row, 1), sides[1])
        high, low = split(value[:both])
        columns = slice(row * col_count, (row + 1) * col_count)
        wide[0:both, columns] = high
        wide[both:half, columns] = blank
        wide[half : half + both, columns] = low
        wide[half + both :, columns] = blank
        tall[0:rank, columns] = high[:rank]
        tall[rank:half, columns] = low[:rank]
    for side in range(2):
        value = jnp.concatenate([sides[side], none], axis=1)
        keep(6 + side, 4, value[:rank], value[rank:both], value[both:])
    own_ref[...] = rows_ref[place_ref[0]]
    products = lax.dot_general(
        wide[...], tall[...], (((1,), (1,)), ((), ())), preferred_element_type=jnp.float32
    )
    products = products[0:half] + products[half:]
    products = products + pltpu.roll(products, rank, 1)
    packed = both // 2
    sums_ref[...] = jnp.where(lane[:packed] < rank, products[0:packed], products[packed:both])


def channel_kernel(sums_ref, factor_ref, data_ref, new_ref, copies_ref):
    channels, rank = factor_ref.shape
    total = sums_ref[...]
    total = jnp.concatenate([total, pltpu.roll(total, rank, 1)], axis=0)[:, :rank]
    gram, top = total[:rank], total[rank:]
    factor = factor_ref[...]
    lower = lax.dot_general(
        factor,
        gram,
        (((1,), (1,)), ((), ())),
        precision=lax.Precision.HIGHEST,
        preferred_element_type=jnp.float32,
    )
    new = factor * top / (lower + epsilon)
    new_ref[...] = new
    packed = channels // 2
    new = jnp.concatenate([new[:packed], new[packed:]], axis=1)
    for i in range(copies_ref.shape[0]):
        copies_ref[i] = new


def factors(new_ref, rank):
    parts = []
    for i in range(new_ref.shape[0]):
        parts += [new_ref[i], pltpu.roll(new_ref[i], rank, 1)]
    new = jnp.transpose(jnp.concatenate(parts, axis=0))[:rank]
    gram = lax.dot_general(
        new,
        new,
        (((1,), (1,)), ((), ())),
        precision=lax.Precision.HIGHEST,
        preferred_element_type=jnp.float32,
    )
    return jnp.concatenate(split(new), axis=0), jnp.concatenate(split(gram), axis=0)


def raised_row(new, gram, data_ref, own_ref, row):
    rank = new.shape[0] // 2

    def product(left, right):
        high, low = split(right)
        both = jnp.dot(left, high, preferred_element_type=jnp.float32)
        both = both + jnp.dot(left, low, preferred_element_type=jnp.float32)
        return both[:rank] + both[rank:]

    data = jnp.concatenate([data_ref[i, row] for i in range(data_ref.shape[0])], axis=0)
    factor = own_ref[row, :rank]
    return factor * product(new, data) / (product(gram, factor) + epsilon)


def border_kernel(new_ref, data_ref, own_ref, piece_ref, corner_ref):
    rank = own_ref.shape[1] - TILE
    new, gram = factors(new_ref, rank)
    last = own_ref.shape[0] - 1
    piece_ref[:rank] = raised_row(new, gram, data_ref, own_ref, last)
    piece_ref[rank:] = own_ref[last, rank:]
    corner_ref[...] = piece_ref[:, :LANES]


def raise_kernel(new_ref, data_ref, own_ref, raised_ref):
    new, gram = factors(new_ref, raised_ref.shape[1])
    for row in range(raised_ref.shape[0]):
        raised_ref[row] = raised_row(new, gram, data_ref, own_ref, row)


def join_kernel(place_ref, straight_ref, below_ref, above_ref, raised_ref, parts_ref):
    shares, _, share, _ = parts_ref.shape
    strip = raised_ref.shape[0]
    lane = lax.broadcasted_iota(jnp.int32, below_ref.shape, 1)
    corner = jnp.where(lane >= LANES // 2, below_ref[...], above_ref[...])
    side = place_ref[0] >= shares - 2
    corner = jnp.where(side, corner, straight_ref[:, LANES:])
    rank = shares * share
    for i in range(shares):
        ranks = slice(i * share, (i + 1) * share)
        for row in range(strip):
            parts_ref[i, row] = raised_ref[row, ranks]
        for at, rows in ((strip, ranks), (strip + 1, slice(rank, rank + TILE))):
            parts_ref[i, at, :, :LANES] = straight_ref[rows, :LANES]
            parts_ref[i, at, :, LANES:] = corner[rows]


def side_of(left, right, at):
    lane = lax.broadcasted_iota(jnp.int32, left.shape, 1)
    left = pltpu.roll(left, (LANES - 3 - at) % LANES, 1)
    right = pltpu.roll(right, (LANES - at) % LANES, 1)
    return jnp.where(lane >= LANES - 3, left, jnp.where(lane < 3, right, 0.0))


def smooth_kernel(labels_ref, parts_ref, copies_ref, first, second, marks_ref, weights_ref, done_ref, written):
    share, row_count, col_count = done_ref.shape
    width = first.shape[2]
    strip = parts_ref.shape[1] - 2
    tall = row_count + 2 * SMOOTH
    marks_ref[...] = jnp.zeros(marks_ref.shape, jnp.float32)
    for row in range(tall):
        inner = row - SMOOTH
        if 0 <= inner < row_count:
            main = parts_ref[inner // strip, inner % strip]
            marks = (labels_ref[inner : inner + 1, :] + 1).astype(jnp.float32)
            start, at = 0, 3 * inner
        else:
            piece = row if inner < 0 else SMOOTH + inner - row_count
            main, marks = parts_ref[piece, strip], parts_ref[piece, strip + 1][:1]
            start, at = LANES, 3 * (inner % row_count)
        first[row, :, :col_count] = main
        marks_ref[row : row + 1, :col_count] = marks
        columns = slice(start, start + LANES)
        left, right = parts_ref[6, strip, :, columns], parts_ref[7, strip, :, columns]
        first[row, :, col_count:] = side_of(left, right, at)
        left, right = parts_ref[6, strip + 1, :, columns], parts_ref[7, strip + 1, :, columns]
        marks_ref[row : row + 1, col_count:] = side_of(left, right, at)[:1]
    marks = marks_ref[...]
    total = jnp.ones(marks.shape, jnp.float32)
    found = []
    for shift, axis in ((1, 0), (marks.shape[0] - 1, 0), (1, 1), (width - 1, 1)):
        neighbour = pltpu.roll(marks, shift, axis)
        weight = jnp.where(neighbour == marks, 1.0, 0.25)
        weight = jnp.where(neighbour == 0.0, 0.0, weight)
        found.append(weight)
        total = total + weight
    inverse = 1.0 / total
    weights_ref[0] = inverse
    for i, weight in enumerate(found):
        weights_ref[1 + i] = weight * inverse

    def smoothed(source, row):
        def weight(i):
            return weights_ref[i, row : row + 1, :]

        field = source[row]
        value = weight(0) * field + weight(1) * source[row - 1] + weight(2) * source[row + 1]
        value = value + weight(3) * pltpu.roll(field, 1, 1)
        return value + weight(4) * pltpu.roll(field, width - 1, 1)

    source, target = first, second
    for step in range(1, SMOOTH):
        for row in range(step, tall - step):
            target[row] = smoothed(source, row)
        source, target = target, source
    for top in range(0, row_count, 8):
        rows = [smoothed(source, top + SMOOTH + i)[None, :, :col_count] for i in range(8)]
        done_ref[:, top : top + 8, :] = jnp.swapaxes(jnp.concatenate(rows, axis=0), 0, 1)
    moves = [
        pltpu.make_async_copy(done_ref, copies_ref.at[i], written.at[i])
        for i in range(copies_ref.shape[0])
    ]
    for move in moves:
        move.start()
    for move in moves:
        move.wait()


def border_moves(axes, count_ch):
    rows, cols = axes

    def moves(steps):
        pairs = []
        for row in range(rows):
            for col in range(cols):
                for ch, (down, across) in steps.items():
                    if 0 <= row + down < rows and 0 <= col + across < cols:
                        source = (row * cols + col) * count_ch + ch
                        target = ((row + down) * cols + col + across) * count_ch + ch
                        pairs.append((source, target))
        return pairs

    straight = {ch: (1, 0) for ch in range(3)} | {ch: (-1, 0) for ch in range(3, 6)}
    straight |= {6: (0, 1), 7: (0, -1)}
    return moves(straight), moves({6: (1, 1), 7: (1, -1)}), moves({6: (-1, 1), 7: (-1, -1)})


def shards(spectra, pixel_factor, channel_factor, labels):
    rank, row_count, col_count = pixel_factor.shape
    channels = spectra.shape[0]
    shares = lax.axis_size("ch")
    place = lax.axis_index("ch")
    pixels = row_count * col_count
    strip = row_count // shares + 1

    f32 = jnp.float32
    place = place.reshape(1)
    operands = (place, spectra, pixel_factor, labels)
    sums, send, own = kernel_call(
        gram_kernel,
        (
            jax.ShapeDtypeStruct(((rank + channels) // 2, 2 * rank), f32),
            jax.ShapeDtypeStruct((shares, strip, channels, col_count), f32),
            jax.ShapeDtypeStruct((strip, rank + TILE, col_count), f32),
        ),
        scratch_shapes=[
            pltpu.VMEM((shares, strip, rank + TILE, col_count), f32),
            pltpu.VMEM((4 * rank, pixels), jnp.bfloat16),
            pltpu.VMEM((2 * rank, pixels), jnp.bfloat16),
        ],
        smem=1,
        operands=operands,
        flops=16 * rank * rank * pixels,
    )
    data = lax.all_to_all(send, "ch", 0, 0, tiled=True)
    sums = doubled_sum(doubled_sum(sums, "row"), "col")
    new_channel, copies = kernel_call(
        channel_kernel,
        (
            jax.ShapeDtypeStruct((channels, rank), f32),
            jax.ShapeDtypeStruct((shares, channels // 2, 2 * rank), f32),
        ),
        waits=1,
        operands=(sums, channel_factor.T, data),
    )
    copies = lax.all_to_all(copies, "ch", 0, 0, tiled=True)
    flops = 8 * rank * (rank + channels * shares) * col_count
    piece, corner = kernel_call(
        border_kernel,
        (
            jax.ShapeDtypeStruct((rank + TILE, col_count), f32),
            jax.ShapeDtypeStruct((rank + TILE, LANES), f32),
        ),
        operands=(copies, data, own),
        flops=flops,
    )
    raised = kernel_call(
        raise_kernel,
        jax.ShapeDtypeStruct((strip - 1, rank, col_count), f32),
        operands=(copies, data, own),
        flops=4 * flops,
    )
    axes = (lax.axis_size("row"), lax.axis_size("col"))
    straight, below, above = border_moves(axes, shares)
    everywhere = ("row", "col", "ch")
    straight = lax.ppermute(piece, everywhere, straight)
    below = lax.ppermute(corner, everywhere, below)
    above = lax.ppermute(corner, everywhere, above)
    share = rank // shares
    parts = kernel_call(
        join_kernel,
        jax.ShapeDtypeStruct((shares, strip + 1, share, col_count), f32),
        smem=1,
        operands=(place, straight, below, above, raised),
    )
    parts = lax.all_to_all(parts, "ch", 0, 0, tiled=True)
    tall = row_count + 2 * SMOOTH
    width = col_count + LANES
    field = (shares, share, row_count, col_count)
    field = kernel_call(
        smooth_kernel,
        jax.ShapeDtypeStruct(field, f32),
        scratch_shapes=[
            pltpu.VMEM((tall, share, width), f32),
            pltpu.VMEM((tall, share, width), f32),
            pltpu.VMEM((tall + -tall % TILE, width), f32),
            pltpu.VMEM((5, tall + -tall % TILE, width), f32),
            pltpu.VMEM(field[1:], f32),
            pltpu.SemaphoreType.DMA((shares,)),
        ],
        apart=field,
        operands=(labels, parts),
    )
    field = lax.all_to_all(field, "ch", 0, 0, tiled=True).reshape(rank, row_count, col_count)
    return (field, new_channel.T)


def solution(mesh):
    placed = (P("ch", "row", "col"), P(None, "row", "col"), P(None, "ch"), P("row", "col"))
    return jax.shard_map(
        shards,
        mesh=mesh,
        in_specs=placed,
        out_specs=(P(None, "row", "col"), P(None, "ch")),
        check_vma=False,
    )
```

time: 161 us -> 114 us (0.71)
  the two profiles are of different devices: /device:TPU:1 before, /device:TPU:64 now
where the time goes in v3:
time: 114 us; the launch traced here: 113 us
  blocking collectives  58.6 us (51%)
  waiting for transfers between devices  21.2 us (19%)
  starting transfers between devices  20.4 us (18%)
  local copies, waits for them, and re-layouts  6.34 us (6%)
  Pallas kernels  5.86 us (5%)
    all_to_all x1, blocking collectives, shards(): lax.all_to_all(field, 'ch', 0, 0, tiled=True)  31.1 us
    all_to_all x1, blocking collectives, shards(): parts = lax.all_to_all(parts, 'ch', 0, 0, tiled=True)  16.9 us
    ppermute x5, waiting for transfers between devices, doubled_sum(): lax.ppermute(value, axis, [(i, i ^ distance) for i in range(count)])  15.9 us
    all_to_all x1, blocking collectives, shards(): copies = lax.all_to_all(copies, 'ch', 0, 0, tiled=True)  10.5 us
    ppermute x5, starting transfers between devices, doubled_sum(): lax.ppermute(value, axis, [(i, i ^ distance) for i in range(count)])  8.13 us
    all_to_all x1, starting transfers between devices, shards(): data = lax.all_to_all(send, 'ch', 0, 0, tiled=True)  7.07 us
    unnamed x13, local copies, waits for them, and re-layouts  6.34 us
    pallas_call x6, Pallas kernels, kernel_call(): pl.pallas_call(kernel, out_shape=out_shape, in_specs=in_specs, out_specs=...  5.86 us
  transfers between devices with their start and end apart: 9, of which 7 were waited for; matrix products, arithmetic and copies ran while one was open for 0% of the time, Pallas kernels for 1%

profile of v3, /device:TPU:64, one launch (start us, length us, event | category | flops | bytes accessed | tf_op | source)
XLA Modules:
  0.0 113.2 jit_solution(14193888844222298515)
XLA Ops:
  0.6 1.6 %copy-done = f32[64,32,256]{2,1,0:T(8,128)S(1)} copy-done((f32[64,32,256]{2,1,0:T(8,128)S(1)}, f32[64,32,256]{2,1,0:T(8,128)}, u32[]{:S(2)}) %copy-start) | copy-done | bytes 2097176
  2.2 1.4 %copy-done.2 = f32[48,32,256]{2,1,0:T(8,128)S(1)} copy-done((f32[48,32,256]{2,1,0:T(8,128)S(1)}, f32[48,32,256]{2,1,0:T(8,128)}, u32[]{:S(2)}) %copy-start.2) | copy-done | bytes 1572888
  3.6 0.8 copy-done.3
  4.4 2.3 %shard_map.59 = (f32[56,128]{1,0:T(8,128)S(1)}, f32[8,5,48,256]{3,2,1,0:T(8,128)S(1)}, f32[5,72,256]{2,1,0:T(8,128)S(1)}) custom-call(s32[1]{0:T(128)} %bitcast.place_ref, f32[48,32,256]{2,1,0:T(8,128)S(1)} %copy-done.2, f32[64,32,256]{2,1,0:T(8,128)S(1)} %copy-done, s32[32,256]{1,0:T(8,128)S(1)} %copy-done.3), custom_call_target="tpu_custom_call" | custom-call | flops 536870912 | bytes 6066180 | tf_op jit(solution)/shard_map/pallas_call | solution.py:37
  6.7 1.3 %copy-done.1 = f32[8,5,48,256]{3,2,1,0:T(8,128)} copy-done((f32[8,5,48,256]{3,2,1,0:T(8,128)}, f32[8,5,48,256]{3,2,1,0:T(8,128)S(1)}, u32[]{:S(2)}) %copy-start.1) | copy-done | bytes 1966104
  7.9 7.1 %all-to-all-start = ((f32[8,5,48,256]{3,2,1,0:T(8,128)}), f32[8,5,48,256]{3,2,1,0:T(8,128)S(1)}, u32[]{:S(2)}, u32[]{:S(2)}) async-start(f32[8,5,48,256]{3,2,1,0:T(8,128)} %copy-done.1), calls=%async_computation | async-start | bytes 3932160 | tf_op jit(solution)/shard_map/all_to_all | solution.py:311
  15.0 1.9 %collective-permute-start = (f32[56,128]{1,0:T(8,128)S(1)}, f32[56,128]{1,0:T(8,128)S(1)}, u32[]{:S(2)}, u32[]{:S(2)}) collective-permute-start(f32[56,128]{1,0:T(8,128)S(1)} %get-tuple-element.9), channel_id=1, source_target_pairs={{0,32},{32,0},{64,96},{96,64},{128,160},{160,128},{192,224},{224,1... | collective-permute-start | bytes 86024 | tf_op jit(solution)/shard_map/ppermute | solution.py:19
  16.9 2.0 %collective-permute-done = f32[56,128]{1,0:T(8,128)S(1)} collective-permute-done((f32[56,128]{1,0:T(8,128)S(1)}, f32[56,128]{1,0:T(8,128)S(1)}, u32[]{:S(2)}, u32[]{:S(2)}) %collective-permute-start) | collective-permute-done | bytes 28704 | tf_op jit(solution)/shard_map/ppermute | solution.py:19
  18.9 4.8 %collective-permute-done.1 = f32[56,128]{1,0:T(8,128)S(1)} collective-permute-done((f32[56,128]{1,0:T(8,128)S(1)}, f32[56,128]{1,0:T(8,128)S(1)}, u32[]{:S(2)}, u32[]{:S(2)}) %collective-permute-start.1) | collective-permute-done | bytes 28704 | tf_op jit(solution)/shard_map/ppermute | solution.py:19
  23.7 5.5 %collective-permute-start.2 = (f32[56,128]{1,0:T(8,128)S(1)}, f32[56,128]{1,0:T(8,128)S(1)}, u32[]{:S(2)}, u32[]{:S(2)}) collective-permute-start(f32[56,128]{1,0:T(8,128)S(1)} %add.16), channel_id=1, source_target_pairs={{0,128},{32,160},{64,192},{96,224},{128,0},{160,32},{192,64},{224,... | collective-permute-start | bytes 86024 | tf_op jit(solution)/shard_map/ppermute | solution.py:19
  29.2 2.2 %collective-permute-done.2 = f32[56,128]{1,0:T(8,128)S(1)} collective-permute-done((f32[56,128]{1,0:T(8,128)S(1)}, f32[56,128]{1,0:T(8,128)S(1)}, u32[]{:S(2)}, u32[]{:S(2)}) %collective-permute-start.2) | collective-permute-done | bytes 28704 | tf_op jit(solution)/shard_map/ppermute | solution.py:19
  31.5 1.2 %collective-permute-done.3 = f32[56,128]{1,0:T(8,128)S(1)} collective-permute-done((f32[56,128]{1,0:T(8,128)S(1)}, f32[56,128]{1,0:T(8,128)S(1)}, u32[]{:S(2)}, u32[]{:S(2)}) %collective-permute-start.3) | collective-permute-done | bytes 28704 | tf_op jit(solution)/shard_map/ppermute | solution.py:19
  32.7 0.7 collective-permute-start.4
  33.3 5.8 %collective-permute-done.4 = f32[56,128]{1,0:T(8,128)S(1)} collective-permute-done((f32[56,128]{1,0:T(8,128)S(1)}, f32[56,128]{1,0:T(8,128)S(1)}, u32[]{:S(2)}, u32[]{:S(2)}) %collective-permute-start.4) | collective-permute-done | bytes 28704 | tf_op jit(solution)/shard_map/ppermute | solution.py:19
  39.1 5.2 %all-to-all-done.data_ref = f32[8,5,48,256]{3,2,1,0:T(8,128)S(1)} async-done(((f32[8,5,48,256]{3,2,1,0:T(8,128)}), f32[8,5,48,256]{3,2,1,0:T(8,128)S(1)}, u32[]{:S(2)}, u32[]{:S(2)}) %all-to-all-start) | async-done | bytes 1966112 | tf_op jit(solution)/shard_map/all_to_all | solution.py:311
  44.3 0.8 shard_map.60
  45.2 10.5 %all_to_all.20.new_ref = f32[8,24,128]{2,1,0:T(8,128)S(1)} all-to-all(f32[8,24,128]{2,1,0:T(8,128)S(1)} %get-tuple-element.11), channel_id=1, replica_groups=mesh['row'=8,'col'=4,'ch'=8] {'ch'}, dimensions={0} | all-to-all | bytes 196608 | tf_op jit(solution)/shard_map/all_to_all | solution.py:322
  56.3 3.9 %collective-permute-start.5 = (f32[72,256]{1,0:T(8,128)S(1)}, f32[72,256]{1,0:T(8,128)S(1)}, u32[]{:S(2)}, u32[]{:S(2)}) collective-permute-start(f32[72,256]{1,0:T(8,128)S(1)} %get-tuple-element.13), channel_id=1, source_target_pairs={{0,32},{1,33},{2,34},{6,14},{8,40},{9,41},{10,42},{14,22},{15,7},{... | collective-permute-start | bytes 221192 | tf_op jit(solution)/shard_map/ppermute | solution.py:342
  60.8 0.7 collective-permute-start.6
  61.5 0.9 shard_map.62.raised_ref
  62.5 16.9 %all_to_all.21.parts_ref = f32[8,6,8,256]{3,2,1,0:T(8,128)S(1)} all-to-all(f32[8,6,8,256]{3,2,1,0:T(8,128)S(1)} %shard_map.63), channel_id=1, replica_groups=mesh['row'=8,'col'=4,'ch'=8] {'ch'}, dimensions={0} | all-to-all | bytes 786432 | tf_op jit(solution)/shard_map/all_to_all | solution.py:352
  79.5 1.2 %shard_map.64 = f32[8,8,32,256]{3,2,1,0:T(8,128)S(1)} custom-call(s32[32,256]{1,0:T(8,128)S(1)} %copy-done.4, f32[8,6,8,256]{3,2,1,0:T(8,128)S(1)} %all_to_all.21.parts_ref), custom_call_target="tpu_custom_call" | custom-call | bytes 2523136 | tf_op jit(solution)/shard_map/pallas_call | solution.py:37
  80.7 31.1 %all_to_all.22 = f32[8,8,32,256]{3,2,1,0:T(8,128)S(1)} all-to-all(f32[8,8,32,256]{3,2,1,0:T(8,128)S(1)} %shard_map.64), channel_id=1, replica_groups=mesh['row'=8,'col'=4,'ch'=8] {'ch'}, dimensions={0} | all-to-all | bytes 4194304 | tf_op jit(solution)/shard_map/all_to_all | solution.py:370
  111.8 1.3 %copy.7 = f32[64,32,256]{2,1,0:T(8,128)} copy(f32[64,32,256]{2,1,0:T(8,128)S(1)} %bitcast.5) | data formatting | bytes 4194304
  (21 shorter events, 1.4 us)
Async XLA Ops:
  0.6 1.6 %copy-start = (f32[64,32,256]{2,1,0:T(8,128)S(1)}, f32[64,32,256]{2,1,0:T(8,128)}, u32[]{:S(2)}) copy-start(f32[64,32,256]{2,1,0:T(8,128)} %factor_ref.1) | copy-start | bytes 6291460
  2.2 1.4 %copy-start.2 = (f32[48,32,256]{2,1,0:T(8,128)S(1)}, f32[48,32,256]{2,1,0:T(8,128)}, u32[]{:S(2)}) copy-start(f32[48,32,256]{2,1,0:T(8,128)} %data_ref.1) | copy-start | bytes 4718596
  3.6 0.8 copy-start.3
  6.7 1.3 %copy-start.1 = (f32[8,5,48,256]{3,2,1,0:T(8,128)}, f32[8,5,48,256]{3,2,1,0:T(8,128)S(1)}, u32[]{:S(2)}) copy-start(f32[8,5,48,256]{3,2,1,0:T(8,128)S(1)} %get-tuple-element.10) | copy-start | bytes 5898244
  7.9 36.4 %copy-start.5 = (f32[64,48]{0,1:T(8,128)S(1)}, f32[64,48]{0,1:T(8,128)}, u32[]{:S(2)}) copy-start(f32[64,48]{0,1:T(8,128)} %param.6) | copy-start | bytes 36868
  7.9 36.4 %all-to-all-start = ((f32[8,5,48,256]{3,2,1,0:T(8,128)}), f32[8,5,48,256]{3,2,1,0:T(8,128)S(1)}, u32[]{:S(2)}, u32[]{:S(2)}) async-start(f32[8,5,48,256]{3,2,1,0:T(8,128)} %copy-done.1), calls=%async_computation | async-start | bytes 3932160 | tf_op jit(solution)/shard_map/all_to_all | solution.py:311
  15.0 3.9 %collective-permute-start = (f32[56,128]{1,0:T(8,128)S(1)}, f32[56,128]{1,0:T(8,128)S(1)}, u32[]{:S(2)}, u32[]{:S(2)}) collective-permute-start(f32[56,128]{1,0:T(8,128)S(1)} %get-tuple-element.9), channel_id=1, source_target_pairs={{0,32},{32,0},{64,96},{96,64},{128,160},{160,128},{192,224},{224,1... | collective-permute-start | bytes 86024 | tf_op jit(solution)/shard_map/ppermute | solution.py:19
  18.9 4.8 %collective-permute-start.1 = (f32[56,128]{1,0:T(8,128)S(1)}, f32[56,128]{1,0:T(8,128)S(1)}, u32[]{:S(2)}, u32[]{:S(2)}) collective-permute-start(f32[56,128]{1,0:T(8,128)S(1)} %add.15), channel_id=1, source_target_pairs={{0,64},{32,96},{64,0},{96,32},{128,192},{160,224},{192,128},{224,1... | collective-permute-start | bytes 86024 | tf_op jit(solution)/shard_map/ppermute | solution.py:19
  23.7 7.8 %collective-permute-start.2 = (f32[56,128]{1,0:T(8,128)S(1)}, f32[56,128]{1,0:T(8,128)S(1)}, u32[]{:S(2)}, u32[]{:S(2)}) collective-permute-start(f32[56,128]{1,0:T(8,128)S(1)} %add.16), channel_id=1, source_target_pairs={{0,128},{32,160},{64,192},{96,224},{128,0},{160,32},{192,64},{224,... | collective-permute-start | bytes 86024 | tf_op jit(solution)/shard_map/ppermute | solution.py:19
  31.4 1.2 %collective-permute-start.3 = (f32[56,128]{1,0:T(8,128)S(1)}, f32[56,128]{1,0:T(8,128)S(1)}, u32[]{:S(2)}, u32[]{:S(2)}) collective-permute-start(f32[56,128]{1,0:T(8,128)S(1)} %add.17), channel_id=1, source_target_pairs={{0,8},{8,0},{16,24},{24,16},{1,9},{9,1},{17,25},{25,17},{2,10},{10... | collective-permute-start | bytes 86024 | tf_op jit(solution)/shard_map/ppermute | solution.py:19
  32.7 6.5 %collective-permute-start.4 = (f32[56,128]{1,0:T(8,128)S(1)}, f32[56,128]{1,0:T(8,128)S(1)}, u32[]{:S(2)}, u32[]{:S(2)}) collective-permute-start(f32[56,128]{1,0:T(8,128)S(1)} %add.18), channel_id=1, source_target_pairs={{0,16},{8,24},{16,0},{24,8},{1,17},{9,25},{17,1},{25,9},{2,18},{10... | collective-permute-start | bytes 86024 | tf_op jit(solution)/shard_map/ppermute | solution.py:19
  56.3 6.2 %collective-permute-start.5 = (f32[72,256]{1,0:T(8,128)S(1)}, f32[72,256]{1,0:T(8,128)S(1)}, u32[]{:S(2)}, u32[]{:S(2)}) collective-permute-start(f32[72,256]{1,0:T(8,128)S(1)} %get-tuple-element.13), channel_id=1, source_target_pairs={{0,32},{1,33},{2,34},{6,14},{8,40},{9,41},{10,42},{14,22},{15,7},{... | collective-permute-start | bytes 221192 | tf_op jit(solution)/shard_map/ppermute | solution.py:342
  60.1 19.3 %copy-start.4 = (s32[32,256]{1,0:T(8,128)S(1)}, s32[32,256]{1,0:T(8,128)}, u32[]{:S(2)}) copy-start(s32[32,256]{1,0:T(8,128)} %labels_ref.3) | copy-start | bytes 98308
  60.1 2.3 %collective-permute-start.7 = (f32[72,128]{1,0:T(8,128)S(1)}, f32[72,128]{1,0:T(8,128)S(1)}, u32[]{:S(2)}, u32[]{:S(2)}) collective-permute-start(f32[72,128]{1,0:T(8,128)S(1)} %get-tuple-element.14), channel_id=1, source_target_pairs={{38,14},{46,22},{47,7},{54,30},{55,15},{63,23},{70,46},{78,54},{79... | collective-permute-start | bytes 110600 | tf_op jit(solution)/shard_map/ppermute | solution.py:344
  60.8 1.6 %collective-permute-start.6 = (f32[72,128]{1,0:T(8,128)S(1)}, f32[72,128]{1,0:T(8,128)S(1)}, u32[]{:S(2)}, u32[]{:S(2)}) collective-permute-start(f32[72,128]{1,0:T(8,128)S(1)} %get-tuple-element.14), channel_id=1, source_target_pairs={{6,46},{14,54},{15,39},{22,62},{23,47},{31,55},{38,78},{46,86},{47... | collective-permute-start | bytes 110600 | tf_op jit(solution)/shard_map/ppermute | solution.py:343

commit v4 on v3

--- a/solution.py
+++ b/solution.py
@@ -10,15 +10,21 @@
 TILE = 8
 epsilon = 1e-09
 VMEM_LIMIT = 48 * 1024 * 1024
-
-
-def doubled_sum(value, axis):
+FIRST_LIMIT = 62 * 1024 * 1024
+
+
+def pair_sum(value, axis, distance):
     count = lax.axis_size(axis)
-    distance = 1
-    while distance < count:
-        value = value + lax.ppermute(value, axis, [(i, i ^ distance) for i in range(count)])
-        distance *= 2
-    return value
+    return value + lax.ppermute(value, axis, [(i, i ^ distance) for i in range(count)])
+
+
+def four_sum(value, axis, near, far):
+    count = lax.axis_size(axis)
+    farthest, middle, close = (
+        lax.ppermute(value, axis, [(i, i ^ distance) for i in range(count)])
+        for distance in (near + far, far, near)
+    )
+    return (value + close) + (middle + farthest)
 
 
 def copies_of_all(value, axis):
@@ -27,7 +33,9 @@
     return lax.all_to_all(copies, axis, 0, 0, tiled=True)
 
 
-def kernel_call(kernel, out_shape, scratch_shapes=(), smem=0, waits=0, apart=None, aliases={}, operands=(), flops=0):
+def kernel_call(
+    kernel, out_shape, scratch_shapes=(), smem=0, waits=0, apart=None, operands=(), flops=0, limit=VMEM_LIMIT
+):
     traffic = sum(x.size * 4 for x in operands) + sum(x.size * 4 for x in jax.tree.leaves(out_shape))
     in_specs = [
         pl.BlockSpec(memory_space=pltpu.SMEM if i < smem else pltpu.VMEM)
@@ -42,8 +50,7 @@
             lambda x: pl.BlockSpec(memory_space=pl.ANY if x.shape == apart else pltpu.VMEM), out_shape
         ),
         scratch_shapes=scratch_shapes,
-        input_output_aliases=aliases,
-        compiler_params=pltpu.CompilerParams(vmem_limit_bytes=VMEM_LIMIT),
+        compiler_params=pltpu.CompilerParams(vmem_limit_bytes=limit),
         cost_estimate=pl.CostEstimate(flops=flops, bytes_accessed=traffic, transcendentals=0),
     )(*operands)
 
@@ -54,51 +61,61 @@
     return high, low
 
 
-def gram_kernel(
-    place_ref, data_ref, factor_ref, labels_ref, sums_ref, send_ref, own_ref, rows_ref, wide, tall
-):
+def side_pieces(value, row, sides):
+    lane = lax.broadcasted_iota(jnp.int32, (value.shape[0], LANES), 1)
+    here = (lane >= 3 * row) & (lane < 3 * row + 3)
+    last = pltpu.roll(value[:, value.shape[1] - LANES :], 3 * row + 3, 1)
+    first = pltpu.roll(value[:, :LANES], 3 * row, 1)
+    return jnp.where(here, last, sides[0]), jnp.where(here, first, sides[1])
+
+
+def strips_kernel(data_ref, send_ref):
     channels, row_count, col_count = data_ref.shape
-    rank = factor_ref.shape[0]
+    sides = (jnp.zeros((channels, LANES), jnp.float32),) * 2
+    for row in range(row_count):
+        if row % 8 == 0:
+            eight = jnp.swapaxes(data_ref[:, row : row + 8, :], 0, 1)
+        data = eight[row % 8]
+        send_ref[row // 4, row % 4] = data
+        if row >= row_count - SMOOTH:
+            send_ref[row - row_count + SMOOTH, 4] = data
+        if row < SMOOTH:
+            send_ref[SMOOTH + row, 4] = data
+        sides = side_pieces(data, row, sides)
+    for i in range(2):
+        send_ref[6 + i, 4, :, :LANES] = sides[i]
+        send_ref[6 + i, 4, :, LANES:] = jnp.zeros((channels, col_count - LANES), jnp.float32)
+
+
+def gram_kernel(place_ref, send_ref, factor_ref, labels_ref, sums_ref, own_ref, rows_ref, wide, tall):
+    channels = send_ref.shape[2]
+    rank, row_count, col_count = factor_ref.shape
     both = rank + channels
     half = 2 * rank
-    lane = lax.broadcasted_iota(jnp.int32, (both + TILE, LANES), 1)
-    sides = [jnp.zeros((both + TILE, LANES), jnp.float32)] * 2
-    blank = jnp.zeros((half - both, col_count), jnp.bfloat16)
-    none = jnp.zeros((both + TILE, col_count - LANES), jnp.float32)
-
-    def keep(strip, at, factor, data, marks):
-        send_ref[strip, at] = data
-        rows_ref[strip, at, :rank] = factor
-        rows_ref[strip, at, rank:] = marks
-
+    for top in (both, half + both):
+        wide[top : top + half - both] = jnp.zeros((half - both, wide.shape[1]), jnp.bfloat16)
+    sides = (jnp.zeros((rank + TILE, LANES), jnp.float32),) * 2
     for row in range(row_count):
         if row % 8 == 0:
-            eight_data = jnp.swapaxes(data_ref[:, row : row + 8, :], 0, 1)
-            eight_factor = jnp.swapaxes(factor_ref[:, row : row + 8, :], 0, 1)
-        data, factor = eight_data[row % 8], eight_factor[row % 8]
+            eight = jnp.swapaxes(factor_ref[:, row : row + 8, :], 0, 1)
+        factor = eight[row % 8]
         marks = (labels_ref[row : row + 1, :] + 1).astype(jnp.float32)
-        marks = jnp.broadcast_to(marks, (TILE, col_count))
-        keep(row // 4, row % 4, factor, data, marks)
+        marked = jnp.concatenate([factor, jnp.broadcast_to(marks, (TILE, col_count))], axis=0)
+        rows_ref[row // 4, row % 4] = marked
         if row >= row_count - SMOOTH:
-            keep(row - row_count + SMOOTH, 4, factor, data, marks)
+            rows_ref[row - row_count + SMOOTH, 4] = marked
         if row < SMOOTH:
-            keep(SMOOTH + row, 4, factor, data, marks)
-        value = jnp.concatenate([factor, data, marks], axis=0)
-        here = (lane >= 3 * row) & (lane < 3 * row + 3)
-        last = pltpu.roll(value[:, col_count - LANES :], 3 * row + 3, 1)
-        sides[0] = jnp.where(here, last, sides[0])
-        sides[1] = jnp.where(here, pltpu.roll(value[:, :LANES], 3 * row, 1), sides[1])
-        high, low = split(value[:both])
+            rows_ref[SMOOTH + row, 4] = marked
+        sides = side_pieces(marked, row, sides)
+        high, low = split(jnp.concatenate([factor, send_ref[row // 4, row % 4]], axis=0))
         columns = slice(row * col_count, (row + 1) * col_count)
         wide[0:both, columns] = high
-        wide[both:half, columns] = blank
         wide[half : half + both, columns] = low
-        wide[half + both :, columns] = blank
         tall[0:rank, columns] = high[:rank]
         tall[rank:half, columns] = low[:rank]
-    for side in range(2):
-        value = jnp.concatenate([sides[side], none], axis=1)
-        keep(6 + side, 4, value[:rank], value[rank:both], value[both:])
+    for i in range(2):
+        rows_ref[6 + i, 4, :, :LANES] = sides[i]
+        rows_ref[6 + i, 4, :, LANES:] = jnp.zeros((rank + TILE, col_count - LANES), jnp.float32)
     own_ref[...] = rows_ref[place_ref[0]]
     products = lax.dot_general(
         wide[...], tall[...], (((1,), (1,)), ((), ())), preferred_element_type=jnp.float32
@@ -106,7 +123,8 @@
     products = products[0:half] + products[half:]
     products = products + pltpu.roll(products, rank, 1)
     packed = both // 2
-    sums_ref[...] = jnp.where(lane[:packed] < rank, products[0:packed], products[packed:both])
+    lane = lax.broadcasted_iota(jnp.int32, (packed, LANES), 1)
+    sums_ref[...] = jnp.where(lane < rank, products[0:packed], products[packed:both])
 
 
 def channel_kernel(sums_ref, factor_ref, data_ref, new_ref, copies_ref):
@@ -253,8 +271,8 @@
         rows = [smoothed(source, top + SMOOTH + i)[None, :, :col_count] for i in range(8)]
         done_ref[:, top : top + 8, :] = jnp.swapaxes(jnp.concatenate(rows, axis=0), 0, 1)
     moves = [
-        pltpu.make_async_copy(done_ref, copies_ref.at[i], written.at[i])
-        for i in range(copies_ref.shape[0])
+        pltpu.make_async_copy(done_ref, copies_ref.at[pl.ds(i * share, share)], written.at[i])
+        for i in range(parts_ref.shape[0])
     ]
     for move in moves:
         move.start()
@@ -291,12 +309,16 @@
 
     f32 = jnp.float32
     place = place.reshape(1)
-    operands = (place, spectra, pixel_factor, labels)
-    sums, send, own = kernel_call(
+    send = kernel_call(
+        strips_kernel,
+        jax.ShapeDtypeStruct((shares, strip, channels, col_count), f32),
+        operands=(spectra,),
+        limit=FIRST_LIMIT,
+    )
+    sums, own = kernel_call(
         gram_kernel,
         (
             jax.ShapeDtypeStruct(((rank + channels) // 2, 2 * rank), f32),
-            jax.ShapeDtypeStruct((shares, strip, channels, col_count), f32),
             jax.ShapeDtypeStruct((strip, rank + TILE, col_count), f32),
         ),
         scratch_shapes=[
@@ -305,11 +327,13 @@
             pltpu.VMEM((2 * rank, pixels), jnp.bfloat16),
         ],
         smem=1,
-        operands=operands,
+        operands=(place, send, pixel_factor, labels),
         flops=16 * rank * rank * pixels,
+        limit=FIRST_LIMIT,
     )
     data = lax.all_to_all(send, "ch", 0, 0, tiled=True)
-    sums = doubled_sum(doubled_sum(sums, "row"), "col")
+    sums = four_sum(pair_sum(sums, "row", 1), "row", 2, 4)
+    sums = pair_sum(pair_sum(sums, "col", 1), "col", 2)
     new_channel, copies = kernel_call(
         channel_kernel,
         (
@@ -352,7 +376,7 @@
     parts = lax.all_to_all(parts, "ch", 0, 0, tiled=True)
     tall = row_count + 2 * SMOOTH
     width = col_count + LANES
-    field = (shares, share, row_count, col_count)
+    field = (rank, row_count, col_count)
     field = kernel_call(
         smooth_kernel,
         jax.ShapeDtypeStruct(field, f32),
@@ -361,13 +385,13 @@
             pltpu.VMEM((tall, share, width), f32),
             pltpu.VMEM((tall + -tall % TILE, width), f32),
             pltpu.VMEM((5, tall + -tall % TILE, width), f32),
-            pltpu.VMEM(field[1:], f32),
+            pltpu.VMEM((share, row_count, col_count), f32),
             pltpu.SemaphoreType.DMA((shares,)),
         ],
         apart=field,
         operands=(labels, parts),
     )
-    field = lax.all_to_all(field, "ch", 0, 0, tiled=True).reshape(rank, row_count, col_count)
+    field = lax.all_to_all(field, "ch", 0, 0, tiled=True)
     return (field, new_channel.T)
 
 

time: 114 us -> 112 us (0.982)
  waiting for transfers between devices: 21.2 us -> 15.1 us
  Pallas kernels: 5.86 us -> 11.5 us
  local copies, waits for them, and re-layouts: 6.34 us -> 1.33 us
  blocking collectives: 58.6 us -> 59.9 us
    pallas_call x6 -> x7, Pallas kernels: 5.86 us -> 11.5 us  [kernel_call(): pl.pallas_call(kernel, out_shape=out_shape, in_specs=in_specs, out_specs=...]
    unnamed x13 -> x7, local copies, waits for them, and re-layouts: 6.34 us -> 1.33 us
    ppermute x5 -> x6, waiting for transfers between devices: 15.9 us -> 12 us  [the longest x3 6.54 us: pair_sum(): lax.ppermute(value, axis, [(i, i ^ distance) for i in range(count)])]
    all_to_all x1, waiting for transfers between devices: 5.19 us -> 2.41 us  [shards(): data = lax.all_to_all(send, 'ch', 0, 0, tiled=True)]
    all_to_all x1, blocking collectives: 10.5 us -> 12.4 us  [shards(): copies = lax.all_to_all(copies, 'ch', 0, 0, tiled=True)]
    ppermute x5 -> x6, starting transfers between devices: 8.13 us -> 9.53 us  [the longest x3 6.84 us: four_sum(): lax.ppermute(value, axis, [(i, i ^ distance) for i in range(count)])]
  transfers between devices with their start and end apart: 9 -> 10, of which waited for: 7 -> 6; matrix products, arithmetic and copies ran while one was open for 0% -> 1% of each run, Pallas kernels for 1% -> 5%
where the time goes in v4:
time: 112 us; the launch traced here: 110 us
  blocking collectives  59.9 us (53%)
  starting transfers between devices  21 us (19%)
  waiting for transfers between devices  15.1 us (13%)
  Pallas kernels  11.5 us (10%)
  local copies, waits for them, and re-layouts  1.33 us (1%)
    all_to_all x1, blocking collectives, shards(): field = lax.all_to_all(field, 'ch', 0, 0, tiled=True)  31.6 us
    all_to_all x1, blocking collectives, shards(): parts = lax.all_to_all(parts, 'ch', 0, 0, tiled=True)  15.9 us
    all_to_all x1, blocking collectives, shards(): copies = lax.all_to_all(copies, 'ch', 0, 0, tiled=True)  12.4 us
    pallas_call x7, Pallas kernels, kernel_call(): pl.pallas_call(kernel, out_shape=out_shape, in_specs=in_specs, out_specs=...  11.5 us
    all_to_all x1, starting transfers between devices, shards(): data = lax.all_to_all(send, 'ch', 0, 0, tiled=True)  6.93 us
    ppermute x3, starting transfers between devices, four_sum(): lax.ppermute(value, axis, [(i, i ^ distance) for i in range(count)])  6.84 us
    ppermute x3, waiting for transfers between devices, pair_sum(): lax.ppermute(value, axis, [(i, i ^ distance) for i in range(count)])  6.54 us
    ppermute x3, waiting for transfers between devices, four_sum(): lax.ppermute(value, axis, [(i, i ^ distance) for i in range(count)])  5.42 us
  transfers between devices with their start and end apart: 10, of which 6 were waited for; matrix products, arithmetic and copies ran while one was open for 1% of the time, Pallas kernels for 5%

profile of v4, /device:TPU:64, one launch (start us, length us, event | category | flops | bytes accessed | tf_op | source)
XLA Modules:
  0.0 110.2 jit_solution(17255976210375709463)
XLA Ops:
  0.6 3.3 %shard_map.59.send_ref = f32[8,5,48,256]{3,2,1,0:T(8,128)} custom-call(f32[48,32,256]{2,1,0:T(8,128)} %data_ref.1), custom_call_target="tpu_custom_call" | custom-call | bytes 3538944 | tf_op jit(solution)/shard_map/pallas_call | solution.py:45
  3.9 6.9 %all-to-all-start = ((f32[8,5,48,256]{3,2,1,0:T(8,128)}), f32[8,5,48,256]{3,2,1,0:T(8,128)S(1)}, u32[]{:S(2)}, u32[]{:S(2)}) async-start(f32[8,5,48,256]{3,2,1,0:T(8,128)} %shard_map.59.send_ref), calls=%async_computation | async-start | bytes 3932160 | tf_op jit(solution)/shard_map/all_to_all | solution.py:334
  10.8 4.6 %shard_map.60 = (f32[56,128]{1,0:T(8,128)}, f32[5,72,256]{2,1,0:T(8,128)}) custom-call(s32[1]{0:T(128)} %bitcast.place_ref, f32[8,5,48,256]{3,2,1,0:T(8,128)} %shard_map.59.send_ref, f32[64,32,256]{2,1,0:T(8,128)} %factor_ref.1, s32[32,256]{1,0:T(8,128)} %labels_ref.3), custom_call_target="tpu_custom_call" | custom-call | flops 536870912 | bytes 4493316 | tf_op jit(solution)/shard_map/pallas_call | solution.py:45
  15.4 1.9 %collective-permute-start = (f32[56,128]{1,0:T(8,128)}, f32[56,128]{1,0:T(8,128)S(1)}, u32[]{:S(2)}, u32[]{:S(2)}) collective-permute-start(f32[56,128]{1,0:T(8,128)} %get-tuple-element.8), channel_id=1, source_target_pairs={{0,32},{32,0},{64,96},{96,64},{128,160},{160,128},{192,224},{224,1... | collective-permute-start | bytes 86024 | tf_op jit(solution)/shard_map/ppermute | solution.py:18
  17.3 2.2 %collective-permute-done = f32[56,128]{1,0:T(8,128)S(1)} collective-permute-done((f32[56,128]{1,0:T(8,128)}, f32[56,128]{1,0:T(8,128)S(1)}, u32[]{:S(2)}, u32[]{:S(2)}) %collective-permute-start) | collective-permute-done | bytes 28704 | tf_op jit(solution)/shard_map/ppermute | solution.py:18
  19.5 0.8 add.18
  20.3 4.5 %collective-permute-start.3 = (f32[56,128]{1,0:T(8,128)S(1)}, f32[56,128]{1,0:T(8,128)S(1)}, u32[]{:S(2)}, u32[]{:S(2)}) collective-permute-start(f32[56,128]{1,0:T(8,128)S(1)} %add.18), channel_id=1, source_target_pairs={{0,192},{32,224},{64,128},{96,160},{128,64},{160,96},{192,0},{224,... | collective-permute-start | bytes 86024 | tf_op jit(solution)/shard_map/ppermute | solution.py:24
  24.7 0.9 collective-permute-start.2
  25.7 1.4 %collective-permute-start.1 = (f32[56,128]{1,0:T(8,128)S(1)}, f32[56,128]{1,0:T(8,128)S(1)}, u32[]{:S(2)}, u32[]{:S(2)}) collective-permute-start(f32[56,128]{1,0:T(8,128)S(1)} %add.18), channel_id=1, source_target_pairs={{0,64},{32,96},{64,0},{96,32},{128,192},{160,224},{192,128},{224,1... | collective-permute-start | bytes 86024 | tf_op jit(solution)/shard_map/ppermute | solution.py:24
  27.1 5.4 %collective-permute-done.2 = f32[56,128]{1,0:T(8,128)S(1)} collective-permute-done((f32[56,128]{1,0:T(8,128)S(1)}, f32[56,128]{1,0:T(8,128)S(1)}, u32[]{:S(2)}, u32[]{:S(2)}) %collective-permute-start.2) | collective-permute-done | bytes 28704 | tf_op jit(solution)/shard_map/ppermute | solution.py:24
  32.6 1.2 %collective-permute-done.4 = f32[56,128]{1,0:T(8,128)S(1)} collective-permute-done((f32[56,128]{1,0:T(8,128)S(1)}, f32[56,128]{1,0:T(8,128)S(1)}, u32[]{:S(2)}, u32[]{:S(2)}) %collective-permute-start.4) | collective-permute-done | bytes 28704 | tf_op jit(solution)/shard_map/ppermute | solution.py:18
  33.8 0.7 collective-permute-start.5
  34.5 3.2 %collective-permute-done.5 = f32[56,128]{1,0:T(8,128)S(1)} collective-permute-done((f32[56,128]{1,0:T(8,128)S(1)}, f32[56,128]{1,0:T(8,128)S(1)}, u32[]{:S(2)}, u32[]{:S(2)}) %collective-permute-start.5) | collective-permute-done | bytes 28704 | tf_op jit(solution)/shard_map/ppermute | solution.py:18
  37.7 2.4 %all-to-all-done.data_ref = f32[8,5,48,256]{3,2,1,0:T(8,128)S(1)} async-done(((f32[8,5,48,256]{3,2,1,0:T(8,128)}), f32[8,5,48,256]{3,2,1,0:T(8,128)S(1)}, u32[]{:S(2)}, u32[]{:S(2)}) %all-to-all-start) | async-done | bytes 1966112 | tf_op jit(solution)/shard_map/all_to_all | solution.py:334
  40.1 0.8 shard_map.61
  41.0 12.4 %all_to_all.20.new_ref = f32[8,24,128]{2,1,0:T(8,128)S(1)} all-to-all(f32[8,24,128]{2,1,0:T(8,128)S(1)} %get-tuple-element.9), channel_id=1, replica_groups=mesh['row'=8,'col'=4,'ch'=8] {'ch'}, dimensions={0} | all-to-all | bytes 196608 | tf_op jit(solution)/shard_map/all_to_all | solution.py:346
  54.0 3.2 %collective-permute-start.6 = (f32[72,256]{1,0:T(8,128)S(1)}, f32[72,256]{1,0:T(8,128)S(1)}, u32[]{:S(2)}, u32[]{:S(2)}) collective-permute-start(f32[72,256]{1,0:T(8,128)S(1)} %get-tuple-element.11), channel_id=1, source_target_pairs={{0,32},{1,33},{2,34},{6,14},{8,40},{9,41},{10,42},{14,22},{15,7},{... | collective-permute-start | bytes 221192 | tf_op jit(solution)/shard_map/ppermute | solution.py:366
  57.2 0.7 collective-permute-start.8
  58.6 0.9 shard_map.63.raised_ref
  59.5 0.7 collective-permute-done.6.straight_ref
  60.2 15.9 %all_to_all.21.parts_ref = f32[8,6,8,256]{3,2,1,0:T(8,128)S(1)} all-to-all(f32[8,6,8,256]{3,2,1,0:T(8,128)S(1)} %shard_map.64), channel_id=1, replica_groups=mesh['row'=8,'col'=4,'ch'=8] {'ch'}, dimensions={0} | all-to-all | bytes 786432 | tf_op jit(solution)/shard_map/all_to_all | solution.py:376
  76.1 1.2 %shard_map.65 = f32[64,32,256]{2,1,0:T(8,128)S(1)} custom-call(s32[32,256]{1,0:T(8,128)S(1)} %copy-done.1, f32[8,6,8,256]{3,2,1,0:T(8,128)S(1)} %all_to_all.21.parts_ref), custom_call_target="tpu_custom_call" | custom-call | bytes 2523136 | tf_op jit(solution)/shard_map/pallas_call | solution.py:45
  77.4 31.6 %all_to_all.22 = f32[64,32,256]{2,1,0:T(8,128)S(1)} all-to-all(f32[64,32,256]{2,1,0:T(8,128)S(1)} %shard_map.65), channel_id=1, replica_groups=mesh['row'=8,'col'=4,'ch'=8] {'ch'}, dimensions={0} | all-to-all | bytes 4194304 | tf_op jit(solution)/shard_map/all_to_all | solution.py:394
  108.9 1.3 %copy.7 = f32[64,32,256]{2,1,0:T(8,128)} copy(f32[64,32,256]{2,1,0:T(8,128)S(1)} %all_to_all.22) | data formatting | bytes 4194304
  (17 shorter events, 1.4 us)
Async XLA Ops:
  3.9 36.2 %all-to-all-start = ((f32[8,5,48,256]{3,2,1,0:T(8,128)}), f32[8,5,48,256]{3,2,1,0:T(8,128)S(1)}, u32[]{:S(2)}, u32[]{:S(2)}) async-start(f32[8,5,48,256]{3,2,1,0:T(8,128)} %shard_map.59.send_ref), calls=%async_computation | async-start | bytes 3932160 | tf_op jit(solution)/shard_map/all_to_all | solution.py:334
  10.8 29.3 %copy-start.2 = (f32[64,48]{0,1:T(8,128)S(1)}, f32[64,48]{0,1:T(8,128)}, u32[]{:S(2)}) copy-start(f32[64,48]{0,1:T(8,128)} %param.6) | copy-start | bytes 36868
  15.4 38.0 %copy-start = (f32[5,72,256]{2,1,0:T(8,128)S(1)}, f32[5,72,256]{2,1,0:T(8,128)}, u32[]{:S(2)}) copy-start(f32[5,72,256]{2,1,0:T(8,128)} %get-tuple-element.10.own_ref) | copy-start | bytes 1105924
  15.4 4.1 %collective-permute-start = (f32[56,128]{1,0:T(8,128)}, f32[56,128]{1,0:T(8,128)S(1)}, u32[]{:S(2)}, u32[]{:S(2)}) collective-permute-start(f32[56,128]{1,0:T(8,128)} %get-tuple-element.8), channel_id=1, source_target_pairs={{0,32},{32,0},{64,96},{96,64},{128,160},{160,128},{192,224},{224,1... | collective-permute-start | bytes 86024 | tf_op jit(solution)/shard_map/ppermute | solution.py:18
  20.3 6.8 %collective-permute-start.3 = (f32[56,128]{1,0:T(8,128)S(1)}, f32[56,128]{1,0:T(8,128)S(1)}, u32[]{:S(2)}, u32[]{:S(2)}) collective-permute-start(f32[56,128]{1,0:T(8,128)S(1)} %add.18), channel_id=1, source_target_pairs={{0,192},{32,224},{64,128},{96,160},{128,64},{160,96},{192,0},{224,... | collective-permute-start | bytes 86024 | tf_op jit(solution)/shard_map/ppermute | solution.py:24
  24.7 7.8 %collective-permute-start.2 = (f32[56,128]{1,0:T(8,128)S(1)}, f32[56,128]{1,0:T(8,128)S(1)}, u32[]{:S(2)}, u32[]{:S(2)}) collective-permute-start(f32[56,128]{1,0:T(8,128)S(1)} %add.18), channel_id=1, source_target_pairs={{0,128},{32,160},{64,192},{96,224},{128,0},{160,32},{192,64},{224,... | collective-permute-start | bytes 86024 | tf_op jit(solution)/shard_map/ppermute | solution.py:24
  25.7 6.9 %collective-permute-start.1 = (f32[56,128]{1,0:T(8,128)S(1)}, f32[56,128]{1,0:T(8,128)S(1)}, u32[]{:S(2)}, u32[]{:S(2)}) collective-permute-start(f32[56,128]{1,0:T(8,128)S(1)} %add.18), channel_id=1, source_target_pairs={{0,64},{32,96},{64,0},{96,32},{128,192},{160,224},{192,128},{224,1... | collective-permute-start | bytes 86024 | tf_op jit(solution)/shard_map/ppermute | solution.py:24
  32.5 1.3 %collective-permute-start.4 = (f32[56,128]{1,0:T(8,128)S(1)}, f32[56,128]{1,0:T(8,128)S(1)}, u32[]{:S(2)}, u32[]{:S(2)}) collective-permute-start(f32[56,128]{1,0:T(8,128)S(1)} %add_add_fusion), channel_id=1, source_target_pairs={{0,8},{8,0},{16,24},{24,16},{1,9},{9,1},{17,25},{25,17},{2,10},{10... | collective-permute-start | bytes 86024 | tf_op jit(solution)/shard_map/ppermute | solution.py:18
  33.8 3.9 %collective-permute-start.5 = (f32[56,128]{1,0:T(8,128)S(1)}, f32[56,128]{1,0:T(8,128)S(1)}, u32[]{:S(2)}, u32[]{:S(2)}) collective-permute-start(f32[56,128]{1,0:T(8,128)S(1)} %add.22), channel_id=1, source_target_pairs={{0,16},{8,24},{16,0},{24,8},{1,17},{9,25},{17,1},{25,9},{2,18},{10... | collective-permute-start | bytes 86024 | tf_op jit(solution)/shard_map/ppermute | solution.py:18
  54.0 6.2 %collective-permute-start.6 = (f32[72,256]{1,0:T(8,128)S(1)}, f32[72,256]{1,0:T(8,128)S(1)}, u32[]{:S(2)}, u32[]{:S(2)}) collective-permute-start(f32[72,256]{1,0:T(8,128)S(1)} %get-tuple-element.11), channel_id=1, source_target_pairs={{0,32},{1,33},{2,34},{6,14},{8,40},{9,41},{10,42},{14,22},{15,7},{... | collective-permute-start | bytes 221192 | tf_op jit(solution)/shard_map/ppermute | solution.py:366
  57.2 18.9 %copy-start.1 = (s32[32,256]{1,0:T(8,128)S(1)}, s32[32,256]{1,0:T(8,128)}, u32[]{:S(2)}) copy-start(s32[32,256]{1,0:T(8,128)} %labels_ref.3) | copy-start | bytes 98308
  57.2 2.3 %collective-permute-start.8 = (f32[72,128]{1,0:T(8,128)S(1)}, f32[72,128]{1,0:T(8,128)S(1)}, u32[]{:S(2)}, u32[]{:S(2)}) collective-permute-start(f32[72,128]{1,0:T(8,128)S(1)} %get-tuple-element.12), channel_id=1, source_target_pairs={{38,14},{46,22},{47,7},{54,30},{55,15},{63,23},{70,46},{78,54},{79... | collective-permute-start | bytes 110600 | tf_op jit(solution)/shard_map/ppermute | solution.py:368
  57.9 1.6 %collective-permute-start.7 = (f32[72,128]{1,0:T(8,128)S(1)}, f32[72,128]{1,0:T(8,128)S(1)}, u32[]{:S(2)}, u32[]{:S(2)}) collective-permute-start(f32[72,128]{1,0:T(8,128)S(1)} %get-tuple-element.12), channel_id=1, source_target_pairs={{6,46},{14,54},{15,39},{22,62},{23,47},{31,55},{38,78},{46,86},{47... | collective-permute-start | bytes 110600 | tf_op jit(solution)/shard_map/ppermute | solution.py:367

commit v5 on v4

--- a/solution.py
+++ b/solution.py
@@ -8,6 +8,9 @@
 SMOOTH = 3
 LANES = 128
 TILE = 8
+UPPER = (0, 1, 2)
+LOWER = (3, 4, 7)
+FIRST, LAST = 5, 6
 epsilon = 1e-09
 VMEM_LIMIT = 48 * 1024 * 1024
 FIRST_LIMIT = 62 * 1024 * 1024
@@ -69,54 +72,65 @@
     return jnp.where(here, last, sides[0]), jnp.where(here, first, sides[1])
 
 
-def strips_kernel(data_ref, send_ref):
+def strips_kernel(data_ref, send_ref, taken, held, arrived, written):
     channels, row_count, col_count = data_ref.shape
+    groups = row_count // 8
+    reads = [
+        pltpu.make_async_copy(data_ref.at[:, pl.ds(8 * i, 8)], taken.at[i], arrived.at[i])
+        for i in range(groups)
+    ]
+    writes = [
+        pltpu.make_async_copy(
+            held.at[pl.ds(2 * i, 2), pl.ds(0, 4)], send_ref.at[pl.ds(2 * i, 2), pl.ds(0, 4)], written.at[i]
+        )
+        for i in range(groups)
+    ]
+    writes.append(
+        pltpu.make_async_copy(
+            held.at[:, pl.ds(4, 1)], send_ref.at[:, pl.ds(4, 1)], written.at[groups]
+        )
+    )
+    for read in reads:
+        read.start()
     sides = (jnp.zeros((channels, LANES), jnp.float32),) * 2
     for row in range(row_count):
         if row % 8 == 0:
-            eight = jnp.swapaxes(data_ref[:, row : row + 8, :], 0, 1)
+            reads[row // 8].wait()
+            eight = jnp.swapaxes(taken[row // 8], 0, 1)
         data = eight[row % 8]
-        send_ref[row // 4, row % 4] = data
+        held[row // 4, row % 4] = data
         if row >= row_count - SMOOTH:
-            send_ref[row - row_count + SMOOTH, 4] = data
+            held[UPPER[row - row_count + SMOOTH], 4] = data
         if row < SMOOTH:
-            send_ref[SMOOTH + row, 4] = data
+            held[LOWER[row], 4] = data
         sides = side_pieces(data, row, sides)
-    for i in range(2):
-        send_ref[6 + i, 4, :, :LANES] = sides[i]
-        send_ref[6 + i, 4, :, LANES:] = jnp.zeros((channels, col_count - LANES), jnp.float32)
-
-
-def gram_kernel(place_ref, send_ref, factor_ref, labels_ref, sums_ref, own_ref, rows_ref, wide, tall):
-    channels = send_ref.shape[2]
+        if row % 8 == 7:
+            writes[row // 8].start()
+    for i, place in enumerate((LAST, FIRST)):
+        held[place, 4, :, :LANES] = sides[i]
+        held[place, 4, :, LANES:] = jnp.zeros((channels, col_count - LANES), jnp.float32)
+    writes[groups].start()
+    for write in writes:
+        write.wait()
+
+
+def gram_kernel(data_ref, factor_ref, sums_ref, wide, tall):
+    channels = data_ref.shape[0]
     rank, row_count, col_count = factor_ref.shape
     both = rank + channels
     half = 2 * rank
     for top in (both, half + both):
         wide[top : top + half - both] = jnp.zeros((half - both, wide.shape[1]), jnp.bfloat16)
-    sides = (jnp.zeros((rank + TILE, LANES), jnp.float32),) * 2
     for row in range(row_count):
         if row % 8 == 0:
-            eight = jnp.swapaxes(factor_ref[:, row : row + 8, :], 0, 1)
-        factor = eight[row % 8]
-        marks = (labels_ref[row : row + 1, :] + 1).astype(jnp.float32)
-        marked = jnp.concatenate([factor, jnp.broadcast_to(marks, (TILE, col_count))], axis=0)
-        rows_ref[row // 4, row % 4] = marked
-        if row >= row_count - SMOOTH:
-            rows_ref[row - row_count + SMOOTH, 4] = marked
-        if row < SMOOTH:
-            rows_ref[SMOOTH + row, 4] = marked
-        sides = side_pieces(marked, row, sides)
-        high, low = split(jnp.concatenate([factor, send_ref[row // 4, row % 4]], axis=0))
+            data = jnp.swapaxes(data_ref[:, row : row + 8, :], 0, 1)
+            factor = jnp.swapaxes(factor_ref[:, row : row + 8, :], 0, 1)
+        high, low = split(jnp.concatenate([factor[row % 8], data[row % 8]], axis=0))
         columns = slice(row * col_count, (row + 1) * col_count)
         wide[0:both, columns] = high
         wide[half : half + both, columns] = low
         tall[0:rank, columns] = high[:rank]
         tall[rank:half, columns] = low[:rank]
-    for i in range(2):
-        rows_ref[6 + i, 4, :, :LANES] = sides[i]
-        rows_ref[6 + i, 4, :, LANES:] = jnp.zeros((rank + TILE, col_count - LANES), jnp.float32)
-    own_ref[...] = rows_ref[place_ref[0]]
     products = lax.dot_general(
         wide[...], tall[...], (((1,), (1,)), ((), ())), preferred_element_type=jnp.float32
     )
@@ -127,7 +141,28 @@
     sums_ref[...] = jnp.where(lane < rank, products[0:packed], products[packed:both])
 
 
-def channel_kernel(sums_ref, factor_ref, data_ref, new_ref, copies_ref):
+def own_kernel(place_ref, factor_ref, labels_ref, own_ref, rows_ref):
+    rank, row_count, col_count = factor_ref.shape
+    sides = (jnp.zeros((rank + TILE, LANES), jnp.float32),) * 2
+    for row in range(row_count):
+        if row % 8 == 0:
+            eight = jnp.swapaxes(factor_ref[:, row : row + 8, :], 0, 1)
+        marks = (labels_ref[row : row + 1, :] + 1).astype(jnp.float32)
+        marks = jnp.broadcast_to(marks, (TILE, col_count))
+        marked = jnp.concatenate([eight[row % 8], marks], axis=0)
+        rows_ref[row // 4, row % 4] = marked
+        if row >= row_count - SMOOTH:
+            rows_ref[UPPER[row - row_count + SMOOTH], 4] = marked
+        if row < SMOOTH:
+            rows_ref[LOWER[row], 4] = marked
+        sides = side_pieces(marked, row, sides)
+    for i, place in enumerate((LAST, FIRST)):
+        rows_ref[place, 4, :, :LANES] = sides[i]
+        rows_ref[place, 4, :, LANES:] = jnp.zeros((rank + TILE, col_count - LANES), jnp.float32)
+    own_ref[...] = rows_ref[place_ref[0]]
+
+
+def channel_kernel(sums_ref, factor_ref, data_ref, own_ref, new_ref, copies_ref):
     channels, rank = factor_ref.shape
     total = sums_ref[...]
     total = jnp.concatenate([total, pltpu.roll(total, rank, 1)], axis=0)[:, :rank]
@@ -163,7 +198,7 @@
     return jnp.concatenate(split(new), axis=0), jnp.concatenate(split(gram), axis=0)
 
 
-def raised_row(new, gram, data_ref, own_ref, row):
+def raised_part(new, gram, data_ref, own_ref, row, columns):
     rank = new.shape[0] // 2
 
     def product(left, right):
@@ -172,41 +207,52 @@
         both = both + jnp.dot(left, low, preferred_element_type=jnp.float32)
         return both[:rank] + both[rank:]
 
-    data = jnp.concatenate([data_ref[i, row] for i in range(data_ref.shape[0])], axis=0)
-    factor = own_ref[row, :rank]
-    return factor * product(new, data) / (product(gram, factor) + epsilon)
-
-
-def border_kernel(new_ref, data_ref, own_ref, piece_ref, corner_ref):
-    rank = own_ref.shape[1] - TILE
+    shares = data_ref.shape[0]
+    data = jnp.concatenate([data_ref[i, row, :, columns] for i in range(shares)], axis=0)
+    own = own_ref[row, :, columns]
+    factor = own[:rank]
+    raised = factor * product(new, data) / (product(gram, factor) + epsilon)
+    return jnp.concatenate([raised, own[rank:]], axis=0)
+
+
+def border_kernel(place_ref, new_ref, data_ref, own_ref, piece_ref, corner_ref):
+    height, col_count = piece_ref.shape
+    row_count = data_ref.shape[0] * (own_ref.shape[0] - 1)
+    new, gram = factors(new_ref, height - TILE)
+    piece_ref[...] = raised_part(new, gram, data_ref, own_ref, own_ref.shape[0] - 1, slice(None))
+    place = place_ref[0]
+    lowest = (place == data_ref.shape[0] - 1).astype(jnp.int32)
+    tile = pl.ds(pl.multiple_of(lowest * (col_count - LANES), LANES), LANES)
+    lane = lax.broadcasted_iota(jnp.int32, corner_ref.shape, 1)
+    corner = jnp.zeros(corner_ref.shape, jnp.float32)
+    for i in range(SMOOTH):
+        value = raised_part(new, gram, data_ref, own_ref, i + lowest, tile)
+        at = 3 * (i + lowest * (row_count - SMOOTH))
+        shift = lax.rem(at + 3 * lowest + 2 * LANES, LANES)
+        corner = jnp.where((lane >= at) & (lane < at + 3), pltpu.roll(value, shift, 1), corner)
+    side = (place == FIRST) | (place == LAST)
+    corner_ref[...] = jnp.where(side, piece_ref[:, :LANES], corner)
+
+
+def raise_kernel(new_ref, data_ref, own_ref, raised_ref):
+    rank = raised_ref.shape[1]
     new, gram = factors(new_ref, rank)
-    last = own_ref.shape[0] - 1
-    piece_ref[:rank] = raised_row(new, gram, data_ref, own_ref, last)
-    piece_ref[rank:] = own_ref[last, rank:]
-    corner_ref[...] = piece_ref[:, :LANES]
-
-
-def raise_kernel(new_ref, data_ref, own_ref, raised_ref):
-    new, gram = factors(new_ref, raised_ref.shape[1])
     for row in range(raised_ref.shape[0]):
-        raised_ref[row] = raised_row(new, gram, data_ref, own_ref, row)
-
-
-def join_kernel(place_ref, straight_ref, below_ref, above_ref, raised_ref, parts_ref):
+        raised_ref[row] = raised_part(new, gram, data_ref, own_ref, row, slice(None))[:rank]
+
+
+def join_kernel(straight_ref, corner_ref, raised_ref, parts_ref):
     shares, _, share, _ = parts_ref.shape
     strip = raised_ref.shape[0]
-    lane = lax.broadcasted_iota(jnp.int32, below_ref.shape, 1)
-    corner = jnp.where(lane >= LANES // 2, below_ref[...], above_ref[...])
-    side = place_ref[0] >= shares - 2
-    corner = jnp.where(side, corner, straight_ref[:, LANES:])
-    rank = shares * share
+    marks = slice(shares * share, shares * share + TILE)
     for i in range(shares):
         ranks = slice(i * share, (i + 1) * share)
         for row in range(strip):
             parts_ref[i, row] = raised_ref[row, ranks]
-        for at, rows in ((strip, ranks), (strip + 1, slice(rank, rank + TILE))):
-            parts_ref[i, at, :, :LANES] = straight_ref[rows, :LANES]
-            parts_ref[i, at, :, LANES:] = corner[rows]
+        parts_ref[i, strip] = straight_ref[ranks]
+        parts_ref[i, strip + 1] = straight_ref[marks]
+        parts_ref[i, strip + 2, :, :LANES] = corner_ref[ranks]
+        parts_ref[i, strip + 2, :, LANES:] = corner_ref[marks]
 
 
 def side_of(left, right, at):
@@ -219,26 +265,31 @@
 def smooth_kernel(labels_ref, parts_ref, copies_ref, first, second, marks_ref, weights_ref, done_ref, written):
     share, row_count, col_count = done_ref.shape
     width = first.shape[2]
-    strip = parts_ref.shape[1] - 2
+    strip = parts_ref.shape[1] - 3
     tall = row_count + 2 * SMOOTH
     marks_ref[...] = jnp.zeros(marks_ref.shape, jnp.float32)
+
+    def tiles(place, row):
+        if row == strip:
+            return parts_ref[place, row, :, :LANES], parts_ref[place, row + 1, :, :LANES]
+        return parts_ref[place, row, :, :LANES], parts_ref[place, row, :, LANES:]
+
     for row in range(tall):
         inner = row - SMOOTH
         if 0 <= inner < row_count:
             main = parts_ref[inner // strip, inner % strip]
             marks = (labels_ref[inner : inner + 1, :] + 1).astype(jnp.float32)
-            start, at = 0, 3 * inner
+            left, right = tiles(LAST, strip), tiles(FIRST, strip)
         else:
-            piece = row if inner < 0 else SMOOTH + inner - row_count
+            piece = UPPER[row] if inner < 0 else LOWER[inner - row_count]
             main, marks = parts_ref[piece, strip], parts_ref[piece, strip + 1][:1]
-            start, at = LANES, 3 * (inner % row_count)
+            places = (parts_ref.shape[0] - 1, FIRST) if inner < 0 else (LAST, 0)
+            left, right = (tiles(place, strip + 2) for place in places)
+        at = 3 * (inner % row_count)
         first[row, :, :col_count] = main
+        first[row, :, col_count:] = side_of(left[0], right[0], at)
         marks_ref[row : row + 1, :col_count] = marks
-        columns = slice(start, start + LANES)
-        left, right = parts_ref[6, strip, :, columns], parts_ref[7, strip, :, columns]
-        first[row, :, col_count:] = side_of(left, right, at)
-        left, right = parts_ref[6, strip + 1, :, columns], parts_ref[7, strip + 1, :, columns]
-        marks_ref[row : row + 1, col_count:] = side_of(left, right, at)[:1]
+        marks_ref[row : row + 1, col_count:] = side_of(left[1], right[1], at)[:1]
     marks = marks_ref[...]
     total = jnp.ones(marks.shape, jnp.float32)
     found = []
@@ -294,9 +345,10 @@
                         pairs.append((source, target))
         return pairs
 
-    straight = {ch: (1, 0) for ch in range(3)} | {ch: (-1, 0) for ch in range(3, 6)}
-    straight |= {6: (0, 1), 7: (0, -1)}
-    return moves(straight), moves({6: (1, 1), 7: (1, -1)}), moves({6: (-1, 1), 7: (-1, -1)})
+    straight = dict.fromkeys(UPPER, (1, 0)) | dict.fromkeys(LOWER, (-1, 0))
+    straight |= {LAST: (0, 1), FIRST: (0, -1)}
+    corners = {count_ch - 1: (1, 1), FIRST: (1, -1), LAST: (-1, 1), 0: (-1, -1)}
+    return moves(straight), moves(corners)
 
 
 def shards(spectra, pixel_factor, channel_factor, labels):
@@ -309,27 +361,37 @@
 
     f32 = jnp.float32
     place = place.reshape(1)
+    send = (shares, strip, channels, col_count)
     send = kernel_call(
         strips_kernel,
-        jax.ShapeDtypeStruct((shares, strip, channels, col_count), f32),
+        jax.ShapeDtypeStruct(send, f32),
+        scratch_shapes=[
+            pltpu.VMEM((row_count // 8, channels, 8, col_count), f32),
+            pltpu.VMEM(send, f32),
+            pltpu.SemaphoreType.DMA((row_count // 8,)),
+            pltpu.SemaphoreType.DMA((row_count // 8 + 1,)),
+        ],
+        waits=1,
+        apart=send,
         operands=(spectra,),
         limit=FIRST_LIMIT,
     )
-    sums, own = kernel_call(
+    sums = kernel_call(
         gram_kernel,
-        (
-            jax.ShapeDtypeStruct(((rank + channels) // 2, 2 * rank), f32),
-            jax.ShapeDtypeStruct((strip, rank + TILE, col_count), f32),
-        ),
+        jax.ShapeDtypeStruct(((rank + channels) // 2, 2 * rank), f32),
         scratch_shapes=[
-            pltpu.VMEM((shares, strip, rank + TILE, col_count), f32),
             pltpu.VMEM((4 * rank, pixels), jnp.bfloat16),
             pltpu.VMEM((2 * rank, pixels), jnp.bfloat16),
         ],
+        operands=(spectra, pixel_factor),
+        flops=16 * rank * rank * pixels,
+    )
+    own = kernel_call(
+        own_kernel,
+        jax.ShapeDtypeStruct((strip, rank + TILE, col_count), f32),
+        scratch_shapes=[pltpu.VMEM((shares, strip, rank + TILE, col_count), f32)],
         smem=1,
-        operands=(place, send, pixel_factor, labels),
-        flops=16 * rank * rank * pixels,
-        limit=FIRST_LIMIT,
+        operands=(place, pixel_factor, labels),
     )
     data = lax.all_to_all(send, "ch", 0, 0, tiled=True)
     sums = four_sum(pair_sum(sums, "row", 1), "row", 2, 4)
@@ -340,8 +402,8 @@
             jax.ShapeDtypeStruct((channels, rank), f32),
             jax.ShapeDtypeStruct((shares, channels // 2, 2 * rank), f32),
         ),
-        waits=1,
-        operands=(sums, channel_factor.T, data),
+        waits=2,
+        operands=(sums, channel_factor.T, data, own),
     )
     copies = lax.all_to_all(copies, "ch", 0, 0, tiled=True)
     flops = 8 * rank * (rank + channels * shares) * col_count
@@ -351,7 +413,8 @@
             jax.ShapeDtypeStruct((rank + TILE, col_count), f32),
             jax.ShapeDtypeStruct((rank + TILE, LANES), f32),
         ),
-        operands=(copies, data, own),
+        smem=1,
+        operands=(place, copies, data, own),
         flops=flops,
     )
     raised = kernel_call(
@@ -361,17 +424,15 @@
         flops=4 * flops,
     )
     axes = (lax.axis_size("row"), lax.axis_size("col"))
-    straight, below, above = border_moves(axes, shares)
+    straight, corners = border_moves(axes, shares)
     everywhere = ("row", "col", "ch")
     straight = lax.ppermute(piece, everywhere, straight)
-    below = lax.ppermute(corner, everywhere, below)
-    above = lax.ppermute(corner, everywhere, above)
+    corner = lax.ppermute(corner, everywhere, corners)
     share = rank // shares
     parts = kernel_call(
         join_kernel,
-        jax.ShapeDtypeStruct((shares, strip + 1, share, col_count), f32),
-        smem=1,
-        operands=(place, straight, below, above, raised),
+        jax.ShapeDtypeStruct((shares, strip + 2, share, col_count), f32),
+        operands=(straight, corner, raised),
     )
     parts = lax.all_to_all(parts, "ch", 0, 0, tiled=True)
     tall = row_count + 2 * SMOOTH

time: 112 us -> 109 us (0.973); the launches traced: 110 us -> 109 us
  blocking collectives: 59.9 us -> 55.8 us
  local copies, waits for them, and re-layouts: 1.33 us -> 5.27 us
  Pallas kernels: 11.5 us -> 9.37 us
    unnamed x7 -> x13, local copies, waits for them, and re-layouts: 1.33 us -> 5.27 us
    ppermute x3, waiting for transfers between devices: 6.54 us -> 3.32 us  [pair_sum(): lax.ppermute(value, axis, [(i, i ^ distance) for i in range(count)])]
    ppermute x2 -> x1, waiting for transfers between devices: 0.01 us -> 3.03 us  [shards(): corner = lax.ppermute(corner, everywhere, corners)]
    all_to_all x1, waiting for transfers between devices: 2.41 us -> 4.98 us  [shards(): data = lax.all_to_all(send, 'ch', 0, 0, tiled=True)]
    all_to_all x1, blocking collectives: 15.9 us -> 13.7 us  [shards(): parts = lax.all_to_all(parts, 'ch', 0, 0, tiled=True)]
    pallas_call x7 -> x8, Pallas kernels: 11.5 us -> 9.37 us  [kernel_call(): pl.pallas_call(kernel, out_shape=out_shape, in_specs=in_specs, out_specs=...]
    all_to_all x1, blocking collectives: 12.4 us -> 10.5 us  [shards(): copies = lax.all_to_all(copies, 'ch', 0, 0, tiled=True)]
  transfers between devices with their start and end apart: 10 -> 9, of which waited for: 6 -> 7; matrix products, arithmetic and copies ran while one was open for 1% -> 0% of each run, Pallas kernels for 5% -> 3%
where the time goes in v5:
time: 109 us
  blocking collectives  55.8 us (51%)
  starting transfers between devices  21.8 us (20%)
  waiting for transfers between devices  15.9 us (15%)
  Pallas kernels  9.37 us (9%)
  local copies, waits for them, and re-layouts  5.27 us (5%)
    all_to_all x1, blocking collectives, shards(): field = lax.all_to_all(field, 'ch', 0, 0, tiled=True)  31.7 us
    all_to_all x1, blocking collectives, shards(): parts = lax.all_to_all(parts, 'ch', 0, 0, tiled=True)  13.7 us
    all_to_all x1, blocking collectives, shards(): copies = lax.all_to_all(copies, 'ch', 0, 0, tiled=True)  10.5 us
    pallas_call x8, Pallas kernels, kernel_call(): pl.pallas_call(kernel, out_shape=out_shape, in_specs=in_specs, out_specs=...  9.37 us
    all_to_all x1, starting transfers between devices, shards(): data = lax.all_to_all(send, 'ch', 0, 0, tiled=True)  7.07 us
    ppermute x3, starting transfers between devices, four_sum(): lax.ppermute(value, axis, [(i, i ^ distance) for i in range(count)])  6.85 us
    unnamed x13, local copies, waits for them, and re-layouts  5.27 us
    all_to_all x1, waiting for transfers between devices, shards(): data = lax.all_to_all(send, 'ch', 0, 0, tiled=True)  4.98 us
  transfers between devices with their start and end apart: 9, of which 7 were waited for; matrix products, arithmetic and copies ran while one was open for 0% of the time, Pallas kernels for 3%

profile of v5, /device:TPU:64, one launch (start us, length us, event | category | flops | bytes accessed | tf_op | source)
XLA Modules:
  0.0 108.9 jit_solution(11684178644953721672)
XLA Ops:
  0.6 2.6 %shard_map.60 = f32[8,5,48,256]{3,2,1,0:T(8,128)} custom-call(f32[48,32,256]{2,1,0:T(8,128)} %data_ref.3), custom_call_target="tpu_custom_call" | custom-call | bytes 3538944 | tf_op jit(solution)/shard_map/pallas_call | solution.py:48
  3.3 7.1 %all-to-all-start = ((f32[8,5,48,256]{3,2,1,0:T(8,128)}), f32[8,5,48,256]{3,2,1,0:T(8,128)S(1)}, u32[]{:S(2)}, u32[]{:S(2)}) async-start(f32[8,5,48,256]{3,2,1,0:T(8,128)} %shard_map.60), calls=%async_computation | async-start | bytes 3932160 | tf_op jit(solution)/shard_map/all_to_all | solution.py:396
  10.4 1.6 %copy-done = f32[64,32,256]{2,1,0:T(8,128)S(1)} copy-done((f32[64,32,256]{2,1,0:T(8,128)S(1)}, f32[64,32,256]{2,1,0:T(8,128)}, u32[]{:S(2)}) %copy-start) | copy-done | bytes 2097176
  11.9 1.9 %shard_map.59 = f32[56,128]{1,0:T(8,128)S(1)} custom-call(f32[48,32,256]{2,1,0:T(8,128)S(1)} %copy-done.2, f32[64,32,256]{2,1,0:T(8,128)S(1)} %copy-done), custom_call_target="tpu_custom_call" | custom-call | flops 536870912 | bytes 3698688 | tf_op jit(solution)/shard_map/pallas_call | solution.py:48
  13.8 2.0 %collective-permute-start = (f32[56,128]{1,0:T(8,128)S(1)}, f32[56,128]{1,0:T(8,128)S(1)}, u32[]{:S(2)}, u32[]{:S(2)}) collective-permute-start(f32[56,128]{1,0:T(8,128)S(1)} %shard_map.59), channel_id=1, source_target_pairs={{0,32},{32,0},{64,96},{96,64},{128,160},{160,128},{192,224},{224,1... | collective-permute-start | bytes 86024 | tf_op jit(solution)/shard_map/ppermute | solution.py:21
  15.8 2.0 %collective-permute-done = f32[56,128]{1,0:T(8,128)S(1)} collective-permute-done((f32[56,128]{1,0:T(8,128)S(1)}, f32[56,128]{1,0:T(8,128)S(1)}, u32[]{:S(2)}, u32[]{:S(2)}) %collective-permute-start) | collective-permute-done | bytes 28704 | tf_op jit(solution)/shard_map/ppermute | solution.py:21
  17.8 5.4 %collective-permute-start.2 = (f32[56,128]{1,0:T(8,128)S(1)}, f32[56,128]{1,0:T(8,128)S(1)}, u32[]{:S(2)}, u32[]{:S(2)}) collective-permute-start(f32[56,128]{1,0:T(8,128)S(1)} %add.18), channel_id=1, source_target_pairs={{0,128},{32,160},{64,192},{96,224},{128,0},{160,32},{192,64},{224,... | collective-permute-start | bytes 86024 | tf_op jit(solution)/shard_map/ppermute | solution.py:27
  23.2 1.5 %collective-permute-start.1 = (f32[56,128]{1,0:T(8,128)S(1)}, f32[56,128]{1,0:T(8,128)S(1)}, u32[]{:S(2)}, u32[]{:S(2)}) collective-permute-start(f32[56,128]{1,0:T(8,128)S(1)} %add.18), channel_id=1, source_target_pairs={{0,64},{32,96},{64,0},{96,32},{128,192},{160,224},{192,128},{224,1... | collective-permute-start | bytes 86024 | tf_op jit(solution)/shard_map/ppermute | solution.py:27
  24.6 1.0 collective-permute-done.2
  25.7 3.5 %collective-permute-done.3 = f32[56,128]{1,0:T(8,128)S(1)} collective-permute-done((f32[56,128]{1,0:T(8,128)S(1)}, f32[56,128]{1,0:T(8,128)S(1)}, u32[]{:S(2)}, u32[]{:S(2)}) %collective-permute-start.3) | collective-permute-done | bytes 28704 | tf_op jit(solution)/shard_map/ppermute | solution.py:27
  29.3 1.2 %collective-permute-done.4 = f32[56,128]{1,0:T(8,128)S(1)} collective-permute-done((f32[56,128]{1,0:T(8,128)S(1)}, f32[56,128]{1,0:T(8,128)S(1)}, u32[]{:S(2)}, u32[]{:S(2)}) %collective-permute-start.4) | collective-permute-done | bytes 28704 | tf_op jit(solution)/shard_map/ppermute | solution.py:21
  31.1 1.6 %copy-done.1 = f32[64,32,256]{2,1,0:T(8,128)S(1)} copy-done((f32[64,32,256]{2,1,0:T(8,128)S(1)}, f32[64,32,256]{2,1,0:T(8,128)}, u32[]{:S(2)}) %copy-start.1) | copy-done | bytes 2097176
  33.5 1.0 shard_map.61.own_ref
  34.6 5.0 %all-to-all-done.data_ref = f32[8,5,48,256]{3,2,1,0:T(8,128)S(1)} async-done(((f32[8,5,48,256]{3,2,1,0:T(8,128)}), f32[8,5,48,256]{3,2,1,0:T(8,128)S(1)}, u32[]{:S(2)}, u32[]{:S(2)}) %all-to-all-start) | async-done | bytes 1966112 | tf_op jit(solution)/shard_map/all_to_all | solution.py:396
  40.5 10.5 %all_to_all.20.new_ref = f32[8,24,128]{2,1,0:T(8,128)S(1)} all-to-all(f32[8,24,128]{2,1,0:T(8,128)S(1)} %get-tuple-element.6), channel_id=1, replica_groups=mesh['row'=8,'col'=4,'ch'=8] {'ch'}, dimensions={0} | all-to-all | bytes 196608 | tf_op jit(solution)/shard_map/all_to_all | solution.py:408
  51.0 0.9 shard_map.63
  51.9 3.8 %collective-permute-start.6 = (f32[72,256]{1,0:T(8,128)S(1)}, f32[72,256]{1,0:T(8,128)S(1)}, u32[]{:S(2)}, u32[]{:S(2)}) collective-permute-start(f32[72,256]{1,0:T(8,128)S(1)} %get-tuple-element.7), channel_id=1, source_target_pairs={{0,32},{1,33},{2,34},{6,14},{8,40},{9,41},{10,42},{14,22},{13,5},{... | collective-permute-start | bytes 221192 | tf_op jit(solution)/shard_map/ppermute | solution.py:429
  55.7 1.3 %collective-permute-start.7 = (f32[72,128]{1,0:T(8,128)S(1)}, f32[72,128]{1,0:T(8,128)S(1)}, u32[]{:S(2)}, u32[]{:S(2)}) collective-permute-start(f32[72,128]{1,0:T(8,128)S(1)} %get-tuple-element.8), channel_id=1, source_target_pairs={{7,47},{15,55},{13,37},{23,63},{21,45},{29,53},{39,79},{38,14},{47... | collective-permute-start | bytes 110600 | tf_op jit(solution)/shard_map/ppermute | solution.py:430
  57.0 0.9 shard_map.64.raised_ref
  58.0 3.0 %collective-permute-done.7.corner_ref = f32[72,128]{1,0:T(8,128)S(1)} collective-permute-done((f32[72,128]{1,0:T(8,128)S(1)}, f32[72,128]{1,0:T(8,128)S(1)}, u32[]{:S(2)}, u32[]{:S(2)}) %collective-permute-start.7) | collective-permute-done | bytes 36896 | tf_op jit(solution)/shard_map/ppermute | solution.py:430
  61.1 13.7 %all_to_all.21.parts_ref = f32[8,7,8,256]{3,2,1,0:T(8,128)S(1)} all-to-all(f32[8,7,8,256]{3,2,1,0:T(8,128)S(1)} %shard_map.65), channel_id=1, replica_groups=mesh['row'=8,'col'=4,'ch'=8] {'ch'}, dimensions={0} | all-to-all | bytes 917504 | tf_op jit(solution)/shard_map/all_to_all | solution.py:437
  74.7 1.2 %shard_map.66 = f32[64,32,256]{2,1,0:T(8,128)S(1)} custom-call(s32[32,256]{1,0:T(8,128)S(1)} %copy-done.4, f32[8,7,8,256]{3,2,1,0:T(8,128)S(1)} %all_to_all.21.parts_ref), custom_call_target="tpu_custom_call" | custom-call | bytes 2588672 | tf_op jit(solution)/shard_map/pallas_call | solution.py:48
  75.9 31.7 %all_to_all.22 = f32[64,32,256]{2,1,0:T(8,128)S(1)} all-to-all(f32[64,32,256]{2,1,0:T(8,128)S(1)} %shard_map.66), channel_id=1, replica_groups=mesh['row'=8,'col'=4,'ch'=8] {'ch'}, dimensions={0} | all-to-all | bytes 4194304 | tf_op jit(solution)/shard_map/all_to_all | solution.py:455
  107.6 1.3 %copy.7 = f32[64,32,256]{2,1,0:T(8,128)} copy(f32[64,32,256]{2,1,0:T(8,128)S(1)} %all_to_all.22) | data formatting | bytes 4194304
  (22 shorter events, 2.6 us)
Async XLA Ops:
  3.2 7.1 %copy-start.2 = (f32[48,32,256]{2,1,0:T(8,128)S(1)}, f32[48,32,256]{2,1,0:T(8,128)}, u32[]{:S(2)}) copy-start(f32[48,32,256]{2,1,0:T(8,128)} %data_ref.3) | copy-start | bytes 4718596
  3.3 36.4 %all-to-all-start = ((f32[8,5,48,256]{3,2,1,0:T(8,128)}), f32[8,5,48,256]{3,2,1,0:T(8,128)S(1)}, u32[]{:S(2)}, u32[]{:S(2)}) async-start(f32[8,5,48,256]{3,2,1,0:T(8,128)} %shard_map.60), calls=%async_computation | async-start | bytes 3932160 | tf_op jit(solution)/shard_map/all_to_all | solution.py:396
  10.3 1.6 %copy-start = (f32[64,32,256]{2,1,0:T(8,128)S(1)}, f32[64,32,256]{2,1,0:T(8,128)}, u32[]{:S(2)}) copy-start(f32[64,32,256]{2,1,0:T(8,128)} %factor_ref.3) | copy-start | bytes 6291460
  13.8 25.8 %copy-start.5 = (f32[64,48]{0,1:T(8,128)S(1)}, f32[64,48]{0,1:T(8,128)}, u32[]{:S(2)}) copy-start(f32[64,48]{0,1:T(8,128)} %param.6) | copy-start | bytes 36868
  13.8 4.0 %collective-permute-start = (f32[56,128]{1,0:T(8,128)S(1)}, f32[56,128]{1,0:T(8,128)S(1)}, u32[]{:S(2)}, u32[]{:S(2)}) collective-permute-start(f32[56,128]{1,0:T(8,128)S(1)} %shard_map.59), channel_id=1, source_target_pairs={{0,32},{32,0},{64,96},{96,64},{128,160},{160,128},{192,224},{224,1... | collective-permute-start | bytes 86024 | tf_op jit(solution)/shard_map/ppermute | solution.py:21
  17.8 7.9 %collective-permute-start.2 = (f32[56,128]{1,0:T(8,128)S(1)}, f32[56,128]{1,0:T(8,128)S(1)}, u32[]{:S(2)}, u32[]{:S(2)}) collective-permute-start(f32[56,128]{1,0:T(8,128)S(1)} %add.18), channel_id=1, source_target_pairs={{0,128},{32,160},{64,192},{96,224},{128,0},{160,32},{192,64},{224,... | collective-permute-start | bytes 86024 | tf_op jit(solution)/shard_map/ppermute | solution.py:27
  23.2 6.0 %collective-permute-start.3 = (f32[56,128]{1,0:T(8,128)S(1)}, f32[56,128]{1,0:T(8,128)S(1)}, u32[]{:S(2)}, u32[]{:S(2)}) collective-permute-start(f32[56,128]{1,0:T(8,128)S(1)} %add.18), channel_id=1, source_target_pairs={{0,192},{32,224},{64,128},{96,160},{128,64},{160,96},{192,0},{224,... | collective-permute-start | bytes 86024 | tf_op jit(solution)/shard_map/ppermute | solution.py:27
  23.2 6.0 %collective-permute-start.1 = (f32[56,128]{1,0:T(8,128)S(1)}, f32[56,128]{1,0:T(8,128)S(1)}, u32[]{:S(2)}, u32[]{:S(2)}) collective-permute-start(f32[56,128]{1,0:T(8,128)S(1)} %add.18), channel_id=1, source_target_pairs={{0,64},{32,96},{64,0},{96,32},{128,192},{160,224},{192,128},{224,1... | collective-permute-start | bytes 86024 | tf_op jit(solution)/shard_map/ppermute | solution.py:27
  29.2 1.3 %collective-permute-start.4 = (f32[56,128]{1,0:T(8,128)S(1)}, f32[56,128]{1,0:T(8,128)S(1)}, u32[]{:S(2)}, u32[]{:S(2)}) collective-permute-start(f32[56,128]{1,0:T(8,128)S(1)} %add_add_fusion), channel_id=1, source_target_pairs={{0,8},{8,0},{16,24},{24,16},{1,9},{9,1},{17,25},{25,17},{2,10},{10... | collective-permute-start | bytes 86024 | tf_op jit(solution)/shard_map/ppermute | solution.py:21
  30.5 4.2 %collective-permute-start.5 = (f32[56,128]{1,0:T(8,128)S(1)}, f32[56,128]{1,0:T(8,128)S(1)}, u32[]{:S(2)}, u32[]{:S(2)}) collective-permute-start(f32[56,128]{1,0:T(8,128)S(1)} %add.22), channel_id=1, source_target_pairs={{0,16},{8,24},{16,0},{24,8},{1,17},{9,25},{17,1},{25,9},{2,18},{10... | collective-permute-start | bytes 86024 | tf_op jit(solution)/shard_map/ppermute | solution.py:21
  31.1 1.6 %copy-start.1 = (f32[64,32,256]{2,1,0:T(8,128)S(1)}, f32[64,32,256]{2,1,0:T(8,128)}, u32[]{:S(2)}) copy-start(f32[64,32,256]{2,1,0:T(8,128)} %factor_ref.3) | copy-start | bytes 6291460
  32.7 0.8 copy-start.3
  51.9 9.1 %collective-permute-start.6 = (f32[72,256]{1,0:T(8,128)S(1)}, f32[72,256]{1,0:T(8,128)S(1)}, u32[]{:S(2)}, u32[]{:S(2)}) collective-permute-start(f32[72,256]{1,0:T(8,128)S(1)} %get-tuple-element.7), channel_id=1, source_target_pairs={{0,32},{1,33},{2,34},{6,14},{8,40},{9,41},{10,42},{14,22},{13,5},{... | collective-permute-start | bytes 221192 | tf_op jit(solution)/shard_map/ppermute | solution.py:429
  55.7 19.0 %copy-start.4 = (s32[32,256]{1,0:T(8,128)S(1)}, s32[32,256]{1,0:T(8,128)}, u32[]{:S(2)}) copy-start(s32[32,256]{1,0:T(8,128)} %labels_ref.3) | copy-start | bytes 98308
  55.7 5.3 %collective-permute-start.7 = (f32[72,128]{1,0:T(8,128)S(1)}, f32[72,128]{1,0:T(8,128)S(1)}, u32[]{:S(2)}, u32[]{:S(2)}) collective-permute-start(f32[72,128]{1,0:T(8,128)S(1)} %get-tuple-element.8), channel_id=1, source_target_pairs={{7,47},{15,55},{13,37},{23,63},{21,45},{29,53},{39,79},{38,14},{47... | collective-permute-start | bytes 110600 | tf_op jit(solution)/shard_map/ppermute | solution.py:430

commit v6 on v5

--- a/solution.py
+++ b/solution.py
@@ -215,10 +215,14 @@
     return jnp.concatenate([raised, own[rank:]], axis=0)
 
 
-def border_kernel(place_ref, new_ref, data_ref, own_ref, piece_ref, corner_ref):
+def border_kernel(
+    place_ref, new_ref, data_ref, own_ref, piece_ref, corner_ref, all_new_ref, gram_ref
+):
     height, col_count = piece_ref.shape
     row_count = data_ref.shape[0] * (own_ref.shape[0] - 1)
     new, gram = factors(new_ref, height - TILE)
+    all_new_ref[...] = new
+    gram_ref[...] = gram
     piece_ref[...] = raised_part(new, gram, data_ref, own_ref, own_ref.shape[0] - 1, slice(None))
     place = place_ref[0]
     lowest = (place == data_ref.shape[0] - 1).astype(jnp.int32)
@@ -234,9 +238,9 @@
     corner_ref[...] = jnp.where(side, piece_ref[:, :LANES], corner)
 
 
-def raise_kernel(new_ref, data_ref, own_ref, raised_ref):
+def raise_kernel(new_ref, gram_ref, data_ref, own_ref, raised_ref):
     rank = raised_ref.shape[1]
-    new, gram = factors(new_ref, rank)
+    new, gram = new_ref[...], gram_ref[...]
     for row in range(raised_ref.shape[0]):
         raised_ref[row] = raised_part(new, gram, data_ref, own_ref, row, slice(None))[:rank]
 
@@ -407,11 +411,13 @@
     )
     copies = lax.all_to_all(copies, "ch", 0, 0, tiled=True)
     flops = 8 * rank * (rank + channels * shares) * col_count
-    piece, corner = kernel_call(
+    piece, corner, all_new, gram = kernel_call(
         border_kernel,
         (
             jax.ShapeDtypeStruct((rank + TILE, col_count), f32),
             jax.ShapeDtypeStruct((rank + TILE, LANES), f32),
+            jax.ShapeDtypeStruct((2 * rank, shares * channels), jnp.bfloat16),
+            jax.ShapeDtypeStruct((2 * rank, rank), jnp.bfloat16),
         ),
         smem=1,
         operands=(place, copies, data, own),
@@ -420,7 +426,7 @@
     raised = kernel_call(
         raise_kernel,
         jax.ShapeDtypeStruct((strip - 1, rank, col_count), f32),
-        operands=(copies, data, own),
+        operands=(all_new, gram, data, own),
         flops=4 * flops,
     )
     axes = (lax.axis_size("row"), lax.axis_size("col"))

time: 109 us -> 109 us (level)
  no operation moved by 1% of the time
where the time goes in v6:
time: 109 us
  blocking collectives  55.8 us (51%)
  starting transfers between devices  21.8 us (20%)
  waiting for transfers between devices  16.2 us (15%)
  Pallas kernels  9.05 us (8%)
  local copies, waits for them, and re-layouts  5.27 us (5%)
    all_to_all x1, blocking collectives, shards(): field = lax.all_to_all(field, 'ch', 0, 0, tiled=True)  31.7 us
    all_to_all x1, blocking collectives, shards(): parts = lax.all_to_all(parts, 'ch', 0, 0, tiled=True)  13.7 us
    all_to_all x1, blocking collectives, shards(): copies = lax.all_to_all(copies, 'ch', 0, 0, tiled=True)  10.5 us
    pallas_call x8, Pallas kernels, kernel_call(): pl.pallas_call(kernel, out_shape=out_shape, in_specs=in_specs, out_specs=...  9.05 us
    all_to_all x1, starting transfers between devices, shards(): data = lax.all_to_all(send, 'ch', 0, 0, tiled=True)  7.07 us
    ppermute x3, starting transfers between devices, four_sum(): lax.ppermute(value, axis, [(i, i ^ distance) for i in range(count)])  6.85 us
    unnamed x13, local copies, waits for them, and re-layouts  5.27 us
    all_to_all x1, waiting for transfers between devices, shards(): data = lax.all_to_all(send, 'ch', 0, 0, tiled=True)  4.98 us
  transfers between devices with their start and end apart: 9, of which 7 were waited for; matrix products, arithmetic and copies ran while one was open for 0% of the time, Pallas kernels for 3%

profile of v6, /device:TPU:64, one launch (start us, length us, event | category | flops | bytes accessed | tf_op | source)
XLA Modules:
  0.0 108.9 jit_solution(10842552673067515518)
XLA Ops:
  0.6 2.6 %shard_map.60 = f32[8,5,48,256]{3,2,1,0:T(8,128)} custom-call(f32[48,32,256]{2,1,0:T(8,128)} %data_ref.3), custom_call_target="tpu_custom_call" | custom-call | bytes 3538944 | tf_op jit(solution)/shard_map/pallas_call | solution.py:48
  3.3 7.1 %all-to-all-start = ((f32[8,5,48,256]{3,2,1,0:T(8,128)}), f32[8,5,48,256]{3,2,1,0:T(8,128)S(1)}, u32[]{:S(2)}, u32[]{:S(2)}) async-start(f32[8,5,48,256]{3,2,1,0:T(8,128)} %shard_map.60), calls=%async_computation | async-start | bytes 3932160 | tf_op jit(solution)/shard_map/all_to_all | solution.py:400
  10.4 1.6 %copy-done = f32[64,32,256]{2,1,0:T(8,128)S(1)} copy-done((f32[64,32,256]{2,1,0:T(8,128)S(1)}, f32[64,32,256]{2,1,0:T(8,128)}, u32[]{:S(2)}) %copy-start) | copy-done | bytes 2097176
  11.9 1.9 %shard_map.59 = f32[56,128]{1,0:T(8,128)S(1)} custom-call(f32[48,32,256]{2,1,0:T(8,128)S(1)} %copy-done.2, f32[64,32,256]{2,1,0:T(8,128)S(1)} %copy-done), custom_call_target="tpu_custom_call" | custom-call | flops 536870912 | bytes 3698688 | tf_op jit(solution)/shard_map/pallas_call | solution.py:48
  13.8 2.0 %collective-permute-start = (f32[56,128]{1,0:T(8,128)S(1)}, f32[56,128]{1,0:T(8,128)S(1)}, u32[]{:S(2)}, u32[]{:S(2)}) collective-permute-start(f32[56,128]{1,0:T(8,128)S(1)} %shard_map.59), channel_id=1, source_target_pairs={{0,32},{32,0},{64,96},{96,64},{128,160},{160,128},{192,224},{224,1... | collective-permute-start | bytes 86024 | tf_op jit(solution)/shard_map/ppermute | solution.py:21
  15.8 2.0 %collective-permute-done = f32[56,128]{1,0:T(8,128)S(1)} collective-permute-done((f32[56,128]{1,0:T(8,128)S(1)}, f32[56,128]{1,0:T(8,128)S(1)}, u32[]{:S(2)}, u32[]{:S(2)}) %collective-permute-start) | collective-permute-done | bytes 28704 | tf_op jit(solution)/shard_map/ppermute | solution.py:21
  17.8 5.4 %collective-permute-start.2 = (f32[56,128]{1,0:T(8,128)S(1)}, f32[56,128]{1,0:T(8,128)S(1)}, u32[]{:S(2)}, u32[]{:S(2)}) collective-permute-start(f32[56,128]{1,0:T(8,128)S(1)} %add.18), channel_id=1, source_target_pairs={{0,128},{32,160},{64,192},{96,224},{128,0},{160,32},{192,64},{224,... | collective-permute-start | bytes 86024 | tf_op jit(solution)/shard_map/ppermute | solution.py:27
  23.2 1.5 %collective-permute-start.1 = (f32[56,128]{1,0:T(8,128)S(1)}, f32[56,128]{1,0:T(8,128)S(1)}, u32[]{:S(2)}, u32[]{:S(2)}) collective-permute-start(f32[56,128]{1,0:T(8,128)S(1)} %add.18), channel_id=1, source_target_pairs={{0,64},{32,96},{64,0},{96,32},{128,192},{160,224},{192,128},{224,1... | collective-permute-start | bytes 86024 | tf_op jit(solution)/shard_map/ppermute | solution.py:27
  24.6 1.0 collective-permute-done.2
  25.7 3.5 %collective-permute-done.3 = f32[56,128]{1,0:T(8,128)S(1)} collective-permute-done((f32[56,128]{1,0:T(8,128)S(1)}, f32[56,128]{1,0:T(8,128)S(1)}, u32[]{:S(2)}, u32[]{:S(2)}) %collective-permute-start.3) | collective-permute-done | bytes 28704 | tf_op jit(solution)/shard_map/ppermute | solution.py:27
  29.3 1.2 %collective-permute-done.4 = f32[56,128]{1,0:T(8,128)S(1)} collective-permute-done((f32[56,128]{1,0:T(8,128)S(1)}, f32[56,128]{1,0:T(8,128)S(1)}, u32[]{:S(2)}, u32[]{:S(2)}) %collective-permute-start.4) | collective-permute-done | bytes 28704 | tf_op jit(solution)/shard_map/ppermute | solution.py:21
  31.1 1.6 %copy-done.1 = f32[64,32,256]{2,1,0:T(8,128)S(1)} copy-done((f32[64,32,256]{2,1,0:T(8,128)S(1)}, f32[64,32,256]{2,1,0:T(8,128)}, u32[]{:S(2)}) %copy-start.1) | copy-done | bytes 2097176
  33.5 1.0 shard_map.61.own_ref
  34.6 5.0 %all-to-all-done.data_ref = f32[8,5,48,256]{3,2,1,0:T(8,128)S(1)} async-done(((f32[8,5,48,256]{3,2,1,0:T(8,128)}), f32[8,5,48,256]{3,2,1,0:T(8,128)S(1)}, u32[]{:S(2)}, u32[]{:S(2)}) %all-to-all-start) | async-done | bytes 1966112 | tf_op jit(solution)/shard_map/all_to_all | solution.py:400
  39.6 0.8 shard_map.62
  40.5 10.5 %all_to_all.20.new_ref = f32[8,24,128]{2,1,0:T(8,128)S(1)} all-to-all(f32[8,24,128]{2,1,0:T(8,128)S(1)} %get-tuple-element.8), channel_id=1, replica_groups=mesh['row'=8,'col'=4,'ch'=8] {'ch'}, dimensions={0} | all-to-all | bytes 196608 | tf_op jit(solution)/shard_map/all_to_all | solution.py:412
  51.0 0.9 shard_map.63
  51.9 3.8 %collective-permute-start.6 = (f32[72,256]{1,0:T(8,128)S(1)}, f32[72,256]{1,0:T(8,128)S(1)}, u32[]{:S(2)}, u32[]{:S(2)}) collective-permute-start(f32[72,256]{1,0:T(8,128)S(1)} %get-tuple-element.9), channel_id=1, source_target_pairs={{0,32},{1,33},{2,34},{6,14},{8,40},{9,41},{10,42},{14,22},{13,5},{... | collective-permute-start | bytes 221192 | tf_op jit(solution)/shard_map/ppermute | solution.py:435
  55.7 1.3 %collective-permute-start.7 = (f32[72,128]{1,0:T(8,128)S(1)}, f32[72,128]{1,0:T(8,128)S(1)}, u32[]{:S(2)}, u32[]{:S(2)}) collective-permute-start(f32[72,128]{1,0:T(8,128)S(1)} %get-tuple-element.10), channel_id=1, source_target_pairs={{7,47},{15,55},{13,37},{23,63},{21,45},{29,53},{39,79},{38,14},{47... | collective-permute-start | bytes 110600 | tf_op jit(solution)/shard_map/ppermute | solution.py:436
  57.7 3.4 %collective-permute-done.7.corner_ref = f32[72,128]{1,0:T(8,128)S(1)} collective-permute-done((f32[72,128]{1,0:T(8,128)S(1)}, f32[72,128]{1,0:T(8,128)S(1)}, u32[]{:S(2)}, u32[]{:S(2)}) %collective-permute-start.7) | collective-permute-done | bytes 36896 | tf_op jit(solution)/shard_map/ppermute | solution.py:436
  61.1 13.7 %all_to_all.21.parts_ref = f32[8,7,8,256]{3,2,1,0:T(8,128)S(1)} all-to-all(f32[8,7,8,256]{3,2,1,0:T(8,128)S(1)} %shard_map.65), channel_id=1, replica_groups=mesh['row'=8,'col'=4,'ch'=8] {'ch'}, dimensions={0} | all-to-all | bytes 917504 | tf_op jit(solution)/shard_map/all_to_all | solution.py:443
  74.7 1.2 %shard_map.66 = f32[64,32,256]{2,1,0:T(8,128)S(1)} custom-call(s32[32,256]{1,0:T(8,128)S(1)} %copy-done.4, f32[8,7,8,256]{3,2,1,0:T(8,128)S(1)} %all_to_all.21.parts_ref), custom_call_target="tpu_custom_call" | custom-call | bytes 2588672 | tf_op jit(solution)/shard_map/pallas_call | solution.py:48
  76.0 31.7 %all_to_all.22 = f32[64,32,256]{2,1,0:T(8,128)S(1)} all-to-all(f32[64,32,256]{2,1,0:T(8,128)S(1)} %shard_map.66), channel_id=1, replica_groups=mesh['row'=8,'col'=4,'ch'=8] {'ch'}, dimensions={0} | all-to-all | bytes 4194304 | tf_op jit(solution)/shard_map/all_to_all | solution.py:461
  107.6 1.3 %copy.7 = f32[64,32,256]{2,1,0:T(8,128)} copy(f32[64,32,256]{2,1,0:T(8,128)S(1)} %all_to_all.22) | data formatting | bytes 4194304
  (22 shorter events, 2.4 us)
Async XLA Ops:
  3.2 7.1 %copy-start.2 = (f32[48,32,256]{2,1,0:T(8,128)S(1)}, f32[48,32,256]{2,1,0:T(8,128)}, u32[]{:S(2)}) copy-start(f32[48,32,256]{2,1,0:T(8,128)} %data_ref.3) | copy-start | bytes 4718596
  3.3 36.4 %all-to-all-start = ((f32[8,5,48,256]{3,2,1,0:T(8,128)}), f32[8,5,48,256]{3,2,1,0:T(8,128)S(1)}, u32[]{:S(2)}, u32[]{:S(2)}) async-start(f32[8,5,48,256]{3,2,1,0:T(8,128)} %shard_map.60), calls=%async_computation | async-start | bytes 3932160 | tf_op jit(solution)/shard_map/all_to_all | solution.py:400
  10.3 1.6 %copy-start = (f32[64,32,256]{2,1,0:T(8,128)S(1)}, f32[64,32,256]{2,1,0:T(8,128)}, u32[]{:S(2)}) copy-start(f32[64,32,256]{2,1,0:T(8,128)} %factor_ref.3) | copy-start | bytes 6291460
  13.8 25.8 %copy-start.5 = (f32[64,48]{0,1:T(8,128)S(1)}, f32[64,48]{0,1:T(8,128)}, u32[]{:S(2)}) copy-start(f32[64,48]{0,1:T(8,128)} %param.6) | copy-start | bytes 36868
  13.8 4.0 %collective-permute-start = (f32[56,128]{1,0:T(8,128)S(1)}, f32[56,128]{1,0:T(8,128)S(1)}, u32[]{:S(2)}, u32[]{:S(2)}) collective-permute-start(f32[56,128]{1,0:T(8,128)S(1)} %shard_map.59), channel_id=1, source_target_pairs={{0,32},{32,0},{64,96},{96,64},{128,160},{160,128},{192,224},{224,1... | collective-permute-start | bytes 86024 | tf_op jit(solution)/shard_map/ppermute | solution.py:21
  17.8 7.9 %collective-permute-start.2 = (f32[56,128]{1,0:T(8,128)S(1)}, f32[56,128]{1,0:T(8,128)S(1)}, u32[]{:S(2)}, u32[]{:S(2)}) collective-permute-start(f32[56,128]{1,0:T(8,128)S(1)} %add.18), channel_id=1, source_target_pairs={{0,128},{32,160},{64,192},{96,224},{128,0},{160,32},{192,64},{224,... | collective-permute-start | bytes 86024 | tf_op jit(solution)/shard_map/ppermute | solution.py:27
  23.2 6.0 %collective-permute-start.3 = (f32[56,128]{1,0:T(8,128)S(1)}, f32[56,128]{1,0:T(8,128)S(1)}, u32[]{:S(2)}, u32[]{:S(2)}) collective-permute-start(f32[56,128]{1,0:T(8,128)S(1)} %add.18), channel_id=1, source_target_pairs={{0,192},{32,224},{64,128},{96,160},{128,64},{160,96},{192,0},{224,... | collective-permute-start | bytes 86024 | tf_op jit(solution)/shard_map/ppermute | solution.py:27
  23.2 6.0 %collective-permute-start.1 = (f32[56,128]{1,0:T(8,128)S(1)}, f32[56,128]{1,0:T(8,128)S(1)}, u32[]{:S(2)}, u32[]{:S(2)}) collective-permute-start(f32[56,128]{1,0:T(8,128)S(1)} %add.18), channel_id=1, source_target_pairs={{0,64},{32,96},{64,0},{96,32},{128,192},{160,224},{192,128},{224,1... | collective-permute-start | bytes 86024 | tf_op jit(solution)/shard_map/ppermute | solution.py:27
  29.2 1.3 %collective-permute-start.4 = (f32[56,128]{1,0:T(8,128)S(1)}, f32[56,128]{1,0:T(8,128)S(1)}, u32[]{:S(2)}, u32[]{:S(2)}) collective-permute-start(f32[56,128]{1,0:T(8,128)S(1)} %add_add_fusion), channel_id=1, source_target_pairs={{0,8},{8,0},{16,24},{24,16},{1,9},{9,1},{17,25},{25,17},{2,10},{10... | collective-permute-start | bytes 86024 | tf_op jit(solution)/shard_map/ppermute | solution.py:21
  30.5 4.2 %collective-permute-start.5 = (f32[56,128]{1,0:T(8,128)S(1)}, f32[56,128]{1,0:T(8,128)S(1)}, u32[]{:S(2)}, u32[]{:S(2)}) collective-permute-start(f32[56,128]{1,0:T(8,128)S(1)} %add.22), channel_id=1, source_target_pairs={{0,16},{8,24},{16,0},{24,8},{1,17},{9,25},{17,1},{25,9},{2,18},{10... | collective-permute-start | bytes 86024 | tf_op jit(solution)/shard_map/ppermute | solution.py:21
  31.1 1.6 %copy-start.1 = (f32[64,32,256]{2,1,0:T(8,128)S(1)}, f32[64,32,256]{2,1,0:T(8,128)}, u32[]{:S(2)}) copy-start(f32[64,32,256]{2,1,0:T(8,128)} %factor_ref.3) | copy-start | bytes 6291460
  32.7 0.8 copy-start.3
  51.9 9.1 %collective-permute-start.6 = (f32[72,256]{1,0:T(8,128)S(1)}, f32[72,256]{1,0:T(8,128)S(1)}, u32[]{:S(2)}, u32[]{:S(2)}) collective-permute-start(f32[72,256]{1,0:T(8,128)S(1)} %get-tuple-element.9), channel_id=1, source_target_pairs={{0,32},{1,33},{2,34},{6,14},{8,40},{9,41},{10,42},{14,22},{13,5},{... | collective-permute-start | bytes 221192 | tf_op jit(solution)/shard_map/ppermute | solution.py:435
  55.7 5.3 %collective-permute-start.7 = (f32[72,128]{1,0:T(8,128)S(1)}, f32[72,128]{1,0:T(8,128)S(1)}, u32[]{:S(2)}, u32[]{:S(2)}) collective-permute-start(f32[72,128]{1,0:T(8,128)S(1)} %get-tuple-element.10), channel_id=1, source_target_pairs={{7,47},{15,55},{13,37},{23,63},{21,45},{29,53},{39,79},{38,14},{47... | collective-permute-start | bytes 110600 | tf_op jit(solution)/shard_map/ppermute | solution.py:436
  57.0 17.7 %copy-start.4 = (s32[32,256]{1,0:T(8,128)S(1)}, s32[32,256]{1,0:T(8,128)}, u32[]{:S(2)}) copy-start(s32[32,256]{1,0:T(8,128)} %labels_ref.3) | copy-start | bytes 98308

commit v7 on v6

--- a/solution.py
+++ b/solution.py
@@ -322,15 +322,16 @@
         for row in range(step, tall - step):
             target[row] = smoothed(source, row)
         source, target = target, source
+    moves = []
     for top in range(0, row_count, 8):
         rows = [smoothed(source, top + SMOOTH + i)[None, :, :col_count] for i in range(8)]
         done_ref[:, top : top + 8, :] = jnp.swapaxes(jnp.concatenate(rows, axis=0), 0, 1)
-    moves = [
-        pltpu.make_async_copy(done_ref, copies_ref.at[pl.ds(i * share, share)], written.at[i])
-        for i in range(parts_ref.shape[0])
-    ]
-    for move in moves:
-        move.start()
+        for i in range(copies_ref.shape[0] // share):
+            target = copies_ref.at[pl.ds(i * share, share), pl.ds(top, 8)]
+            moves.append(
+                pltpu.make_async_copy(done_ref.at[:, pl.ds(top, 8)], target, written.at[len(moves)])
+            )
+            moves[-1].start()
     for move in moves:
         move.wait()
 
@@ -453,7 +454,7 @@
             pltpu.VMEM((tall + -tall % TILE, width), f32),
             pltpu.VMEM((5, tall + -tall % TILE, width), f32),
             pltpu.VMEM((share, row_count, col_count), f32),
-            pltpu.SemaphoreType.DMA((shares,)),
+            pltpu.SemaphoreType.DMA((shares * row_count // 8,)),
         ],
         apart=field,
         operands=(labels, parts),

time: 109 us -> 110 us (level)
  no operation moved by 1% of the time
where the time goes in v7:
time: 110 us
  blocking collectives  55.8 us (51%)
  starting transfers between devices  21.8 us (20%)
  waiting for transfers between devices  16.2 us (15%)
  Pallas kernels  9.77 us (9%)
  local copies, waits for them, and re-layouts  5.27 us (5%)
    all_to_all x1, blocking collectives, shards(): field = lax.all_to_all(field, 'ch', 0, 0, tiled=True)  31.7 us
    all_to_all x1, blocking collectives, shards(): parts = lax.all_to_all(parts, 'ch', 0, 0, tiled=True)  13.7 us
    all_to_all x1, blocking collectives, shards(): copies = lax.all_to_all(copies, 'ch', 0, 0, tiled=True)  10.5 us
    pallas_call x8, Pallas kernels, kernel_call(): pl.pallas_call(kernel, out_shape=out_shape, in_specs=in_specs, out_specs=...  9.77 us
    all_to_all x1, starting transfers between devices, shards(): data = lax.all_to_all(send, 'ch', 0, 0, tiled=True)  7.07 us
    ppermute x3, starting transfers between devices, four_sum(): lax.ppermute(value, axis, [(i, i ^ distance) for i in range(count)])  6.85 us
    unnamed x13, local copies, waits for them, and re-layouts  5.27 us
    all_to_all x1, waiting for transfers between devices, shards(): data = lax.all_to_all(send, 'ch', 0, 0, tiled=True)  4.98 us
  transfers between devices with their start and end apart: 9, of which 7 were waited for; matrix products, arithmetic and copies ran while one was open for 0% of the time, Pallas kernels for 3%

profile of v7, /device:TPU:64, one launch (start us, length us, event | category | flops | bytes accessed | tf_op | source)
XLA Modules:
  0.0 109.7 jit_solution(5300378997296520357)
XLA Ops:
  0.6 2.6 %shard_map.60 = f32[8,5,48,256]{3,2,1,0:T(8,128)} custom-call(f32[48,32,256]{2,1,0:T(8,128)} %data_ref.3), custom_call_target="tpu_custom_call" | custom-call | bytes 3538944 | tf_op jit(solution)/shard_map/pallas_call | solution.py:48
  3.3 7.1 %all-to-all-start = ((f32[8,5,48,256]{3,2,1,0:T(8,128)}), f32[8,5,48,256]{3,2,1,0:T(8,128)S(1)}, u32[]{:S(2)}, u32[]{:S(2)}) async-start(f32[8,5,48,256]{3,2,1,0:T(8,128)} %shard_map.60), calls=%async_computation | async-start | bytes 3932160 | tf_op jit(solution)/shard_map/all_to_all | solution.py:401
  10.4 1.6 %copy-done = f32[64,32,256]{2,1,0:T(8,128)S(1)} copy-done((f32[64,32,256]{2,1,0:T(8,128)S(1)}, f32[64,32,256]{2,1,0:T(8,128)}, u32[]{:S(2)}) %copy-start) | copy-done | bytes 2097176
  11.9 1.9 %shard_map.59 = f32[56,128]{1,0:T(8,128)S(1)} custom-call(f32[48,32,256]{2,1,0:T(8,128)S(1)} %copy-done.2, f32[64,32,256]{2,1,0:T(8,128)S(1)} %copy-done), custom_call_target="tpu_custom_call" | custom-call | flops 536870912 | bytes 3698688 | tf_op jit(solution)/shard_map/pallas_call | solution.py:48
  13.8 2.0 %collective-permute-start = (f32[56,128]{1,0:T(8,128)S(1)}, f32[56,128]{1,0:T(8,128)S(1)}, u32[]{:S(2)}, u32[]{:S(2)}) collective-permute-start(f32[56,128]{1,0:T(8,128)S(1)} %shard_map.59), channel_id=1, source_target_pairs={{0,32},{32,0},{64,96},{96,64},{128,160},{160,128},{192,224},{224,1... | collective-permute-start | bytes 86024 | tf_op jit(solution)/shard_map/ppermute | solution.py:21
  15.8 2.0 %collective-permute-done = f32[56,128]{1,0:T(8,128)S(1)} collective-permute-done((f32[56,128]{1,0:T(8,128)S(1)}, f32[56,128]{1,0:T(8,128)S(1)}, u32[]{:S(2)}, u32[]{:S(2)}) %collective-permute-start) | collective-permute-done | bytes 28704 | tf_op jit(solution)/shard_map/ppermute | solution.py:21
  17.8 5.4 %collective-permute-start.2 = (f32[56,128]{1,0:T(8,128)S(1)}, f32[56,128]{1,0:T(8,128)S(1)}, u32[]{:S(2)}, u32[]{:S(2)}) collective-permute-start(f32[56,128]{1,0:T(8,128)S(1)} %add.18), channel_id=1, source_target_pairs={{0,128},{32,160},{64,192},{96,224},{128,0},{160,32},{192,64},{224,... | collective-permute-start | bytes 86024 | tf_op jit(solution)/shard_map/ppermute | solution.py:27
  23.2 1.5 %collective-permute-start.1 = (f32[56,128]{1,0:T(8,128)S(1)}, f32[56,128]{1,0:T(8,128)S(1)}, u32[]{:S(2)}, u32[]{:S(2)}) collective-permute-start(f32[56,128]{1,0:T(8,128)S(1)} %add.18), channel_id=1, source_target_pairs={{0,64},{32,96},{64,0},{96,32},{128,192},{160,224},{192,128},{224,1... | collective-permute-start | bytes 86024 | tf_op jit(solution)/shard_map/ppermute | solution.py:27
  24.6 1.0 collective-permute-done.2
  25.7 3.5 %collective-permute-done.3 = f32[56,128]{1,0:T(8,128)S(1)} collective-permute-done((f32[56,128]{1,0:T(8,128)S(1)}, f32[56,128]{1,0:T(8,128)S(1)}, u32[]{:S(2)}, u32[]{:S(2)}) %collective-permute-start.3) | collective-permute-done | bytes 28704 | tf_op jit(solution)/shard_map/ppermute | solution.py:27
  29.3 1.2 %collective-permute-done.4 = f32[56,128]{1,0:T(8,128)S(1)} collective-permute-done((f32[56,128]{1,0:T(8,128)S(1)}, f32[56,128]{1,0:T(8,128)S(1)}, u32[]{:S(2)}, u32[]{:S(2)}) %collective-permute-start.4) | collective-permute-done | bytes 28704 | tf_op jit(solution)/shard_map/ppermute | solution.py:21
  31.1 1.6 %copy-done.1 = f32[64,32,256]{2,1,0:T(8,128)S(1)} copy-done((f32[64,32,256]{2,1,0:T(8,128)S(1)}, f32[64,32,256]{2,1,0:T(8,128)}, u32[]{:S(2)}) %copy-start.1) | copy-done | bytes 2097176
  33.5 1.0 shard_map.61.own_ref
  34.6 5.0 %all-to-all-done.data_ref = f32[8,5,48,256]{3,2,1,0:T(8,128)S(1)} async-done(((f32[8,5,48,256]{3,2,1,0:T(8,128)}), f32[8,5,48,256]{3,2,1,0:T(8,128)S(1)}, u32[]{:S(2)}, u32[]{:S(2)}) %all-to-all-start) | async-done | bytes 1966112 | tf_op jit(solution)/shard_map/all_to_all | solution.py:401
  39.6 0.8 shard_map.62
  40.5 10.5 %all_to_all.20.new_ref = f32[8,24,128]{2,1,0:T(8,128)S(1)} all-to-all(f32[8,24,128]{2,1,0:T(8,128)S(1)} %get-tuple-element.8), channel_id=1, replica_groups=mesh['row'=8,'col'=4,'ch'=8] {'ch'}, dimensions={0} | all-to-all | bytes 196608 | tf_op jit(solution)/shard_map/all_to_all | solution.py:413
  51.0 0.9 shard_map.63
  51.9 3.8 %collective-permute-start.6 = (f32[72,256]{1,0:T(8,128)S(1)}, f32[72,256]{1,0:T(8,128)S(1)}, u32[]{:S(2)}, u32[]{:S(2)}) collective-permute-start(f32[72,256]{1,0:T(8,128)S(1)} %get-tuple-element.9), channel_id=1, source_target_pairs={{0,32},{1,33},{2,34},{6,14},{8,40},{9,41},{10,42},{14,22},{13,5},{... | collective-permute-start | bytes 221192 | tf_op jit(solution)/shard_map/ppermute | solution.py:436
  55.7 1.3 %collective-permute-start.7 = (f32[72,128]{1,0:T(8,128)S(1)}, f32[72,128]{1,0:T(8,128)S(1)}, u32[]{:S(2)}, u32[]{:S(2)}) collective-permute-start(f32[72,128]{1,0:T(8,128)S(1)} %get-tuple-element.10), channel_id=1, source_target_pairs={{7,47},{15,55},{13,37},{23,63},{21,45},{29,53},{39,79},{38,14},{47... | collective-permute-start | bytes 110600 | tf_op jit(solution)/shard_map/ppermute | solution.py:437
  57.7 3.4 %collective-permute-done.7.corner_ref = f32[72,128]{1,0:T(8,128)S(1)} collective-permute-done((f32[72,128]{1,0:T(8,128)S(1)}, f32[72,128]{1,0:T(8,128)S(1)}, u32[]{:S(2)}, u32[]{:S(2)}) %collective-permute-start.7) | collective-permute-done | bytes 36896 | tf_op jit(solution)/shard_map/ppermute | solution.py:437
  61.1 13.7 %all_to_all.21.parts_ref = f32[8,7,8,256]{3,2,1,0:T(8,128)S(1)} all-to-all(f32[8,7,8,256]{3,2,1,0:T(8,128)S(1)} %shard_map.65), channel_id=1, replica_groups=mesh['row'=8,'col'=4,'ch'=8] {'ch'}, dimensions={0} | all-to-all | bytes 917504 | tf_op jit(solution)/shard_map/all_to_all | solution.py:444
  74.7 2.0 %shard_map.66 = f32[64,32,256]{2,1,0:T(8,128)S(1)} custom-call(s32[32,256]{1,0:T(8,128)S(1)} %copy-done.4, f32[8,7,8,256]{3,2,1,0:T(8,128)S(1)} %all_to_all.21.parts_ref), custom_call_target="tpu_custom_call" | custom-call | bytes 2588672 | tf_op jit(solution)/shard_map/pallas_call | solution.py:48
  76.7 31.7 %all_to_all.22 = f32[64,32,256]{2,1,0:T(8,128)S(1)} all-to-all(f32[64,32,256]{2,1,0:T(8,128)S(1)} %shard_map.66), channel_id=1, replica_groups=mesh['row'=8,'col'=4,'ch'=8] {'ch'}, dimensions={0} | all-to-all | bytes 4194304 | tf_op jit(solution)/shard_map/all_to_all | solution.py:462
  108.3 1.3 %copy.7 = f32[64,32,256]{2,1,0:T(8,128)} copy(f32[64,32,256]{2,1,0:T(8,128)S(1)} %all_to_all.22) | data formatting | bytes 4194304
  (22 shorter events, 2.4 us)
Async XLA Ops:
  3.2 7.1 %copy-start.2 = (f32[48,32,256]{2,1,0:T(8,128)S(1)}, f32[48,32,256]{2,1,0:T(8,128)}, u32[]{:S(2)}) copy-start(f32[48,32,256]{2,1,0:T(8,128)} %data_ref.3) | copy-start | bytes 4718596
  3.3 36.4 %all-to-all-start = ((f32[8,5,48,256]{3,2,1,0:T(8,128)}), f32[8,5,48,256]{3,2,1,0:T(8,128)S(1)}, u32[]{:S(2)}, u32[]{:S(2)}) async-start(f32[8,5,48,256]{3,2,1,0:T(8,128)} %shard_map.60), calls=%async_computation | async-start | bytes 3932160 | tf_op jit(solution)/shard_map/all_to_all | solution.py:401
  10.3 1.6 %copy-start = (f32[64,32,256]{2,1,0:T(8,128)S(1)}, f32[64,32,256]{2,1,0:T(8,128)}, u32[]{:S(2)}) copy-start(f32[64,32,256]{2,1,0:T(8,128)} %factor_ref.3) | copy-start | bytes 6291460
  13.8 25.8 %copy-start.5 = (f32[64,48]{0,1:T(8,128)S(1)}, f32[64,48]{0,1:T(8,128)}, u32[]{:S(2)}) copy-start(f32[64,48]{0,1:T(8,128)} %param.6) | copy-start | bytes 36868
  13.8 4.0 %collective-permute-start = (f32[56,128]{1,0:T(8,128)S(1)}, f32[56,128]{1,0:T(8,128)S(1)}, u32[]{:S(2)}, u32[]{:S(2)}) collective-permute-start(f32[56,128]{1,0:T(8,128)S(1)} %shard_map.59), channel_id=1, source_target_pairs={{0,32},{32,0},{64,96},{96,64},{128,160},{160,128},{192,224},{224,1... | collective-permute-start | bytes 86024 | tf_op jit(solution)/shard_map/ppermute | solution.py:21
  17.8 7.9 %collective-permute-start.2 = (f32[56,128]{1,0:T(8,128)S(1)}, f32[56,128]{1,0:T(8,128)S(1)}, u32[]{:S(2)}, u32[]{:S(2)}) collective-permute-start(f32[56,128]{1,0:T(8,128)S(1)} %add.18), channel_id=1, source_target_pairs={{0,128},{32,160},{64,192},{96,224},{128,0},{160,32},{192,64},{224,... | collective-permute-start | bytes 86024 | tf_op jit(solution)/shard_map/ppermute | solution.py:27
  23.2 6.0 %collective-permute-start.3 = (f32[56,128]{1,0:T(8,128)S(1)}, f32[56,128]{1,0:T(8,128)S(1)}, u32[]{:S(2)}, u32[]{:S(2)}) collective-permute-start(f32[56,128]{1,0:T(8,128)S(1)} %add.18), channel_id=1, source_target_pairs={{0,192},{32,224},{64,128},{96,160},{128,64},{160,96},{192,0},{224,... | collective-permute-start | bytes 86024 | tf_op jit(solution)/shard_map/ppermute | solution.py:27
  23.2 6.0 %collective-permute-start.1 = (f32[56,128]{1,0:T(8,128)S(1)}, f32[56,128]{1,0:T(8,128)S(1)}, u32[]{:S(2)}, u32[]{:S(2)}) collective-permute-start(f32[56,128]{1,0:T(8,128)S(1)} %add.18), channel_id=1, source_target_pairs={{0,64},{32,96},{64,0},{96,32},{128,192},{160,224},{192,128},{224,1... | collective-permute-start | bytes 86024 | tf_op jit(solution)/shard_map/ppermute | solution.py:27
  29.2 1.3 %collective-permute-start.4 = (f32[56,128]{1,0:T(8,128)S(1)}, f32[56,128]{1,0:T(8,128)S(1)}, u32[]{:S(2)}, u32[]{:S(2)}) collective-permute-start(f32[56,128]{1,0:T(8,128)S(1)} %add_add_fusion), channel_id=1, source_target_pairs={{0,8},{8,0},{16,24},{24,16},{1,9},{9,1},{17,25},{25,17},{2,10},{10... | collective-permute-start | bytes 86024 | tf_op jit(solution)/shard_map/ppermute | solution.py:21
  30.5 4.2 %collective-permute-start.5 = (f32[56,128]{1,0:T(8,128)S(1)}, f32[56,128]{1,0:T(8,128)S(1)}, u32[]{:S(2)}, u32[]{:S(2)}) collective-permute-start(f32[56,128]{1,0:T(8,128)S(1)} %add.22), channel_id=1, source_target_pairs={{0,16},{8,24},{16,0},{24,8},{1,17},{9,25},{17,1},{25,9},{2,18},{10... | collective-permute-start | bytes 86024 | tf_op jit(solution)/shard_map/ppermute | solution.py:21
  31.1 1.6 %copy-start.1 = (f32[64,32,256]{2,1,0:T(8,128)S(1)}, f32[64,32,256]{2,1,0:T(8,128)}, u32[]{:S(2)}) copy-start(f32[64,32,256]{2,1,0:T(8,128)} %factor_ref.3) | copy-start | bytes 6291460
  32.7 0.8 copy-start.3
  51.9 9.1 %collective-permute-start.6 = (f32[72,256]{1,0:T(8,128)S(1)}, f32[72,256]{1,0:T(8,128)S(1)}, u32[]{:S(2)}, u32[]{:S(2)}) collective-permute-start(f32[72,256]{1,0:T(8,128)S(1)} %get-tuple-element.9), channel_id=1, source_target_pairs={{0,32},{1,33},{2,34},{6,14},{8,40},{9,41},{10,42},{14,22},{13,5},{... | collective-permute-start | bytes 221192 | tf_op jit(solution)/shard_map/ppermute | solution.py:436
  55.7 5.3 %collective-permute-start.7 = (f32[72,128]{1,0:T(8,128)S(1)}, f32[72,128]{1,0:T(8,128)S(1)}, u32[]{:S(2)}, u32[]{:S(2)}) collective-permute-start(f32[72,128]{1,0:T(8,128)S(1)} %get-tuple-element.10), channel_id=1, source_target_pairs={{7,47},{15,55},{13,37},{23,63},{21,45},{29,53},{39,79},{38,14},{47... | collective-permute-start | bytes 110600 | tf_op jit(solution)/shard_map/ppermute | solution.py:437
  57.0 17.7 %copy-start.4 = (s32[32,256]{1,0:T(8,128)S(1)}, s32[32,256]{1,0:T(8,128)}, u32[]{:S(2)}) copy-start(s32[32,256]{1,0:T(8,128)} %labels_ref.3) | copy-start | bytes 98308
